TPU v7x, 128 devices: a whole 4x4x4 slice. The times are simulated.
128 devices in a mesh: row: 8 (over x, core), col: 16 (over z, y).
Axes of the slice: x: 4, y: 4, z: 4, core: 2. Of those that a mesh axis runs over, the one named last changes fastest.
Arguments:
- object_field: float32 [2, 6144, 12288], P(None, 'row', 'col'), may hold values from -1.5 to 1.5, as said below
- probe_modes: float32 [2, 2, 256, 256], replicated, may hold values from -3 to 3
- counts: int32 [8, 16], replicated, may hold values from 1 to 12, 64 in all within a row
- centers: int32 [8, 16, 2, 12], P('row', 'col'), may hold values from 0 to 767
- patterns: bfloat16 [8, 16, 12, 256, 256], P('row', 'col'), may hold values from 1 to 32
Outputs:
- new_object: float32 [2, 6144, 12288], P(None, 'row', 'col')
- new_probe: float32 [2, 2, 256, 256], replicated
Inputs may be any that keep to these rules, and one draw needn't show every extreme that they name: Each row of counts sums to 64 and its largest entry is 12. `centers`: slot s of tile (r, c) is used only if s < counts[r, c]. `object_field`: each pixel is a complex value of magnitude between 0.5 and 1.5.
All inputs are finite; a program needn't handle non-finite values.
Results may differ from a plain program's by a relative error of at most 0.0038.
The roundings to bfloat16 on the way count: a program that leaves them out, or rounds other values in their place, can miss the bound.
Values may be sent and summed in bfloat16 or wider, within the bound.
A program may use at most 128 MiB of HBM per device.

v0:
```python
import math

import jax
import jax.numpy as jnp
from jax import lax
from jax.sharding import PartitionSpec as P


def with_halo(array, sides, width):
    for axis, dim in sides:
        devices, length = (lax.axis_size(axis), array.shape[dim])
        up = [(i, (i + 1) % devices) for i in range(devices - 1)]
        down = [(j, i) for i, j in up]
        last = lax.slice_in_dim(array, length - width, length, axis=dim)
        initial = lax.slice_in_dim(array, 0, width, axis=dim)
        before = lax.ppermute(last, axis, up)
        after = lax.ppermute(initial, axis, down)
        array = jnp.concatenate([before, array, after], axis=dim)
    return array


def dft_tables(length):
    indices = jnp.arange(length, dtype=jnp.int32)
    product = indices[:, None] * indices[None, :] % length
    angles = product.astype(jnp.float32) * (2.0 * jnp.pi / length)
    factor = 1.0 / jnp.sqrt(jnp.float32(length))
    cosine_table = (jnp.cos(angles) * factor).astype(jnp.bfloat16)
    sine_table = (jnp.sin(angles) * factor).astype(jnp.bfloat16)
    positive_table = jnp.concatenate(
        [
            jnp.concatenate([cosine_table, -sine_table], 1),
            jnp.concatenate([sine_table, cosine_table], 1),
        ],
        0,
    )
    negative_table = jnp.concatenate(
        [
            jnp.concatenate([cosine_table, sine_table], 1),
            jnp.concatenate([-sine_table, cosine_table], 1),
        ],
        0,
    )
    return (positive_table, negative_table)


def right_apply(real_part, imag_part, table):
    joined = jnp.concatenate([real_part, imag_part], -1)
    return jnp.einsum("nmjk,kl->nmjl", joined, table, preferred_element_type=jnp.float32)


def left_apply(real_part, imag_part, table):
    joined = jnp.concatenate([real_part, imag_part], -2)
    return jnp.einsum("jk,nmkl->nmjl", table, joined, preferred_element_type=jnp.float32)


def process_block(
    patch_block, amp_block, live_block, probe_lower_edge, positive_table, negative_table
):
    patch_size = patch_block.shape[-1]
    obj_real = patch_block[:, 0].astype(jnp.float32)[:, None]
    obj_imag = patch_block[:, 1].astype(jnp.float32)[:, None]
    probe_real = probe_lower_edge[:, 0].astype(jnp.float32)[None]
    probe_imag = probe_lower_edge[:, 1].astype(jnp.float32)[None]
    wave_real = (probe_real * obj_real - probe_imag * obj_imag).astype(jnp.bfloat16)
    wave_imag = (probe_real * obj_imag + probe_imag * obj_real).astype(jnp.bfloat16)
    first_pass = right_apply(wave_real, wave_imag, positive_table).astype(jnp.bfloat16)
    spectrum = left_apply(
        first_pass[..., :patch_size], first_pass[..., patch_size:], negative_table
    )
    spec_real = spectrum[:, :, :patch_size]
    spec_imag = spectrum[:, :, patch_size:]
    total_power = jnp.sum(spec_real * spec_real + spec_imag * spec_imag, axis=1, keepdims=True)
    factor = amp_block.astype(jnp.float32)[:, None] / jnp.sqrt(jnp.maximum(total_power, 0.5)) - 1.0
    shift_real = (factor * spec_real).astype(jnp.bfloat16)
    shift_imag = (factor * spec_imag).astype(jnp.bfloat16)
    back_pass = right_apply(shift_real, shift_imag, negative_table).astype(jnp.bfloat16)
    change = left_apply(back_pass[..., :patch_size], back_pass[..., patch_size:], positive_table)
    change_real = change[:, :, :patch_size]
    change_imag = change[:, :, patch_size:]
    grad_real = jnp.sum(probe_real * change_real + probe_imag * change_imag, axis=1)
    grad_imag = jnp.sum(probe_real * change_imag - probe_imag * change_real, axis=1)
    live_low = live_block.astype(jnp.bfloat16)[:, None, None, None]
    object_terms = jnp.stack([grad_real, grad_imag], 1).astype(jnp.bfloat16) * live_low
    weights = live_block[:, None, None, None]
    probe_real_part = jnp.sum(weights * (obj_real * change_real + obj_imag * change_imag), 0)
    probe_imag_part = jnp.sum(weights * (obj_real * change_imag - obj_imag * change_real), 0)
    cover_part = jnp.sum(
        live_block[:, None, None]
        * (obj_real[:, 0] * obj_real[:, 0] + obj_imag[:, 0] * obj_imag[:, 0]),
        0,
    )
    return (object_terms, jnp.stack([probe_real_part, probe_imag_part], 1), cover_part)


def handle_every_block(
    object_patches,
    measured_amplitudes,
    activity_flags,
    probe_lower_edge,
    positive_table,
    negative_table,
):
    count_total = object_patches.shape[0]
    patch_size = object_patches.shape[-1]
    block_extent = math.gcd(count_total, 4)
    count_of_blocks = count_total // block_extent
    patch_blocks = object_patches.reshape(
        (count_of_blocks, block_extent) + object_patches.shape[1:]
    )
    amp_blocks = measured_amplitudes.reshape(
        (count_of_blocks, block_extent) + measured_amplitudes.shape[1:]
    )
    active_blocks = activity_flags.reshape(count_of_blocks, block_extent)

    def step_block(running, inputs):
        object_terms, probe_part, cover_part = process_block(
            inputs[0], inputs[1], inputs[2], probe_lower_edge, positive_table, negative_table
        )
        return ((running[0] + probe_part, running[1] + cover_part), object_terms)

    starting_guess = (
        jnp.zeros(probe_lower_edge.shape, jnp.float32),
        jnp.zeros((patch_size, patch_size), jnp.float32),
    )
    sums, object_terms = lax.scan(
        step_block, starting_guess, (patch_blocks, amp_blocks, active_blocks)
    )
    return (object_terms.reshape((count_total,) + object_patches.shape[1:]), sums[0], sums[1])


def cut_patches(padded, spots, patch_size):

    def cut_single(row_start, col_start):
        return lax.dynamic_slice(
            padded, (jnp.int32(0), row_start, col_start), (2, patch_size, patch_size)
        )

    return jax.vmap(cut_single)(spots[0], spots[1])


def place_terms(object_terms, spots, padded_size):
    canvas = jnp.zeros((2, padded_size, padded_size), jnp.float32)

    def add_single(slot_index, current_canvas):
        piece = lax.dynamic_index_in_dim(object_terms, slot_index, 0, keepdims=False).astype(
            jnp.float32
        )
        row_start = spots[0, slot_index]
        col_start = spots[1, slot_index]
        anchor = (jnp.int32(0), row_start, col_start)
        current = lax.dynamic_slice(current_canvas, anchor, piece.shape)
        return lax.dynamic_update_slice(current_canvas, current + piece, anchor)

    return lax.fori_loop(0, object_terms.shape[0], add_single, canvas)


def fold_rims(extended, tile_size, half_width, patch_size):
    inner_end = patch_size + tile_size
    low_edge = tile_size - half_width
    interior = extended[:, patch_size:inner_end, patch_size:inner_end]
    interior = interior.at[:, :half_width, :].add(extended[:, :half_width, patch_size:inner_end])
    interior = interior.at[:, low_edge:, :].add(extended[:, -half_width:, patch_size:inner_end])
    interior = interior.at[:, :, :half_width].add(extended[:, patch_size:inner_end, :half_width])
    interior = interior.at[:, :, low_edge:].add(extended[:, patch_size:inner_end, -half_width:])
    interior = interior.at[:, :half_width, :half_width].add(extended[:, :half_width, :half_width])
    interior = interior.at[:, :half_width, low_edge:].add(extended[:, :half_width, -half_width:])
    interior = interior.at[:, low_edge:, :half_width].add(extended[:, -half_width:, :half_width])
    interior = interior.at[:, low_edge:, low_edge:].add(extended[:, -half_width:, -half_width:])
    return interior


def on_device(object_field, probe_modes, counts, centers, patterns):
    patch_size = probe_modes.shape[-1]
    half_width = patch_size // 2
    tile_size = object_field.shape[1]
    slot_count = patterns.shape[2]
    positive_table, negative_table = dft_tables(patch_size)
    object_low = object_field.astype(jnp.bfloat16)
    probe_lower_edge = probe_modes.astype(jnp.bfloat16)
    padded = with_halo(object_low, (("row", 1), ("col", 2)), half_width)
    spots = centers[0, 0]
    measured_amplitudes = patterns[0, 0]
    object_patches = cut_patches(padded, spots, patch_size)
    row_position = lax.axis_index("row")
    col_position = lax.axis_index("col")
    counts_row = lax.dynamic_index_in_dim(counts, row_position, 0, keepdims=False)
    col_width = lax.axis_size("col")
    peer_ids = jnp.arange(col_width, dtype=jnp.int32)
    local_count = jnp.sum(jnp.where(peer_ids == col_position, counts_row, 0))
    slot_numbers = jnp.arange(slot_count, dtype=jnp.int32)
    activity_flags = (slot_numbers < local_count).astype(jnp.float32)
    object_terms, probe_total, cover_total = handle_every_block(
        object_patches,
        measured_amplitudes,
        activity_flags,
        probe_lower_edge,
        positive_table,
        negative_table,
    )
    canvas = place_terms(object_terms, spots, tile_size + patch_size)
    extended = with_halo(canvas.astype(jnp.bfloat16), (("row", 1), ("col", 2)), half_width).astype(
        canvas.dtype
    )
    gradient = fold_rims(extended, tile_size, half_width, patch_size)
    intensity = jnp.sum(probe_modes * probe_modes, axis=(0, 1))
    peak = jnp.max(intensity) + 1e-06
    new_object = object_field + gradient / peak
    probe_total, cover_total = lax.psum((probe_total, cover_total), ("row", "col"))
    new_probe = probe_modes + probe_total / jnp.sqrt(cover_total)
    return (new_object, new_probe)


def solution(mesh):
    placed = (
        P(None, "row", "col"),
        P(),
        P(),
        P("row", "col", None, None),
        P("row", "col", None, None, None),
    )
    return jax.shard_map(
        on_device,
        mesh=mesh,
        in_specs=placed,
        out_specs=(P(None, "row", "col"), P()),
        check_vma=False,
    )
```

profile of v0, /device:TPU:1, one launch (start us, length us, event | category | flops | bytes accessed | tf_op | source)
XLA Modules:
  0.0 497.0 jit_solution(4542660549130709600)
XLA Ops:
  7.2 2.6 convert_element_type.180
  10.7 4.5 collective-permute-start
  15.2 1.9 collective-permute-start.1
  18.5 1.8 collective-permute-done
  20.2 4.3 collective-permute-done.1
  25.7 4.0 collective-permute-start.2
  31.6 2.6 copy.24
  34.2 2.1 copy.36
  40.8 3.5 pad_maximum_fusion
  44.3 44.2 %while.40 = (s32[]{:T(128)}, bf16[2,1024,1024]{2,1,0:T(8,128)(2,1)}, s32[12,3]{0,1:T(4,128)S(1)}, bf16[12,2,256,256]{3,2,1,0:T(8,128)(2,1)}, s32[]{:T(128)}) while((s32[]{:T(128)}, bf16[2,1024,1024]{2,1,0:T(8,128)(2,1)}, s32[12,3]{0,1:T(4,128)S(1)}, bf16[12,2,256,256]{3,2,1,0:T(8,128)(2,1)}, s32[]{:T(128)}) %tuple.144), condition=%wide.while_cond.8, body=%wide.while_body.8.sunk | while | flops 2 | bytes 525929 | solution.py:134
  44.9 3.1 bitcast_dynamic-update-slice_fusion.2
  48.6 3.1 bitcast_dynamic-update-slice_fusion.2
  52.2 3.1 bitcast_dynamic-update-slice_fusion.2
  55.9 3.1 bitcast_dynamic-update-slice_fusion.2
  59.6 3.1 bitcast_dynamic-update-slice_fusion.2
  63.3 3.1 bitcast_dynamic-update-slice_fusion.2
  67.0 3.1 bitcast_dynamic-update-slice_fusion.2
  70.7 3.1 bitcast_dynamic-update-slice_fusion.2
  74.4 3.1 bitcast_dynamic-update-slice_fusion.2
  78.1 3.1 bitcast_dynamic-update-slice_fusion.2
  81.8 3.1 bitcast_dynamic-update-slice_fusion.2
  85.5 3.1 bitcast_dynamic-update-slice_fusion.2
  88.6 43.4 %while.41 = (s32[]{:T(128)}, f32[2,2,256,256]{3,2,1,0:T(8,128)S(1)}, f32[256,256]{1,0:T(8,128)}, bf16[3,4,2,256,256]{4,3,2,1,0:T(8,128)(2,1)}, f32[3,4]{1,0:T(4,...) while((s32[]{:T(128)}, ...), condition=%wide.region_8.9_spmd.clone, body=%wide.region_1.8_spmd.clone.sunk | while | flops 4338286592 | bytes 83887464 | solution.py:125
  100.2 1.5 fusion.95
  114.7 1.5 fusion.95
  129.1 1.5 fusion.95
  132.0 4.3 broadcast_in_dim.13
  136.2 147.4 %while.39 = (s32[]{:T(128)}, f32[2,1024,1024]{2,1,0:T(8,128)}, s32[2,12]{1,0:T(2,128)S(1)}, bf16[12,2,256,256]{3,2,1,0:T(8,128)(2,1)}, s32[]{:T(128)}, /*index=5*/s32[]{:T(128)}, s32[]{:T(128)}) while((s32[]{:T(128)}, f32[2,1024,1024]{2,1,0:T(8,128)}, s32[2,12]{1,0:T(2,128)S(1)}, bf16[12,2,256,256]{3,2,1,0:T(8,128)(2,1)}, s32[]{:T(128)}, ...), condition=%wide.region_10.11_spmd, body=%wide.region_9.10_spmd.sunk | while | flops 262152 | bytes 2359477 | solution.py:154
  140.6 1.4 convert_add_fusion.9
  142.1 6.7 %dynamic_update_slice.18 = f32[2,1024,1024]{2,1,0:T(8,128)} dynamic-update-slice(f32[2,1024,1024]{2,1,0:T(8,128)} %get-tuple-element.663, f32[2,256,256]{2,1,0:T(8,128)S(1)} %convert_add_fusion.9, s32[]{:T(128)} %constant.321.clone.1..sunk, s32[]{:T(128)S(6)} %select_n.96, s32[]{:T(128)S(6)} %select_n.97) | dynamic-update-slice | bytes 1048580 | tf_op jit(solution)/shard_map/while/body/eval_jaxpr/dynamic_update_slice | solution.py:152
  153.2 1.4 convert_add_fusion.9
  154.6 6.8 %dynamic_update_slice.18 = f32[2,1024,1024]{2,1,0:T(8,128)} dynamic-update-slice(f32[2,1024,1024]{2,1,0:T(8,128)} %get-tuple-element.663, f32[2,256,256]{2,1,0:T(8,128)S(1)} %convert_add_fusion.9, s32[]{:T(128)} %constant.321.clone.1..sunk, s32[]{:T(128)S(6)} %select_n.96, s32[]{:T(128)S(6)} %select_n.97) | dynamic-update-slice | bytes 1048580 | tf_op jit(solution)/shard_map/while/body/eval_jaxpr/dynamic_update_slice | solution.py:152
  165.8 1.4 convert_add_fusion.9
  167.2 6.6 %dynamic_update_slice.18 = f32[2,1024,1024]{2,1,0:T(8,128)} dynamic-update-slice(f32[2,1024,1024]{2,1,0:T(8,128)} %get-tuple-element.663, f32[2,256,256]{2,1,0:T(8,128)S(1)} %convert_add_fusion.9, s32[]{:T(128)} %constant.321.clone.1..sunk, s32[]{:T(128)S(6)} %select_n.96, s32[]{:T(128)S(6)} %select_n.97) | dynamic-update-slice | bytes 1048580 | tf_op jit(solution)/shard_map/while/body/eval_jaxpr/dynamic_update_slice | solution.py:152
  178.2 1.4 convert_add_fusion.9
  179.7 6.3 %dynamic_update_slice.18 = f32[2,1024,1024]{2,1,0:T(8,128)} dynamic-update-slice(f32[2,1024,1024]{2,1,0:T(8,128)} %get-tuple-element.663, f32[2,256,256]{2,1,0:T(8,128)S(1)} %convert_add_fusion.9, s32[]{:T(128)} %constant.321.clone.1..sunk, s32[]{:T(128)S(6)} %select_n.96, s32[]{:T(128)S(6)} %select_n.97) | dynamic-update-slice | bytes 1048580 | tf_op jit(solution)/shard_map/while/body/eval_jaxpr/dynamic_update_slice | solution.py:152
  191.8 6.5 %dynamic_update_slice.18 = f32[2,1024,1024]{2,1,0:T(8,128)} dynamic-update-slice(f32[2,1024,1024]{2,1,0:T(8,128)} %get-tuple-element.663, f32[2,256,256]{2,1,0:T(8,128)S(1)} %convert_add_fusion.9, s32[]{:T(128)} %constant.321.clone.1..sunk, s32[]{:T(128)S(6)} %select_n.96, s32[]{:T(128)S(6)} %select_n.97) | dynamic-update-slice | bytes 1048580 | tf_op jit(solution)/shard_map/while/body/eval_jaxpr/dynamic_update_slice | solution.py:152
  202.6 1.4 convert_add_fusion.9
  204.0 5.9 %dynamic_update_slice.18 = f32[2,1024,1024]{2,1,0:T(8,128)} dynamic-update-slice(f32[2,1024,1024]{2,1,0:T(8,128)} %get-tuple-element.663, f32[2,256,256]{2,1,0:T(8,128)S(1)} %convert_add_fusion.9, s32[]{:T(128)} %constant.321.clone.1..sunk, s32[]{:T(128)S(6)} %select_n.96, s32[]{:T(128)S(6)} %select_n.97) | dynamic-update-slice | bytes 1048580 | tf_op jit(solution)/shard_map/while/body/eval_jaxpr/dynamic_update_slice | solution.py:152
  215.8 6.8 %dynamic_update_slice.18 = f32[2,1024,1024]{2,1,0:T(8,128)} dynamic-update-slice(f32[2,1024,1024]{2,1,0:T(8,128)} %get-tuple-element.663, f32[2,256,256]{2,1,0:T(8,128)S(1)} %convert_add_fusion.9, s32[]{:T(128)} %constant.321.clone.1..sunk, s32[]{:T(128)S(6)} %select_n.96, s32[]{:T(128)S(6)} %select_n.97) | dynamic-update-slice | bytes 1048580 | tf_op jit(solution)/shard_map/while/body/eval_jaxpr/dynamic_update_slice | solution.py:152
  228.4 6.1 %dynamic_update_slice.18 = f32[2,1024,1024]{2,1,0:T(8,128)} dynamic-update-slice(f32[2,1024,1024]{2,1,0:T(8,128)} %get-tuple-element.663, f32[2,256,256]{2,1,0:T(8,128)S(1)} %convert_add_fusion.9, s32[]{:T(128)} %constant.321.clone.1..sunk, s32[]{:T(128)S(6)} %select_n.96, s32[]{:T(128)S(6)} %select_n.97) | dynamic-update-slice | bytes 1048580 | tf_op jit(solution)/shard_map/while/body/eval_jaxpr/dynamic_update_slice | solution.py:152
  240.3 5.8 %dynamic_update_slice.18 = f32[2,1024,1024]{2,1,0:T(8,128)} dynamic-update-slice(f32[2,1024,1024]{2,1,0:T(8,128)} %get-tuple-element.663, f32[2,256,256]{2,1,0:T(8,128)S(1)} %convert_add_fusion.9, s32[]{:T(128)} %constant.321.clone.1..sunk, s32[]{:T(128)S(6)} %select_n.96, s32[]{:T(128)S(6)} %select_n.97) | dynamic-update-slice | bytes 1048580 | tf_op jit(solution)/shard_map/while/body/eval_jaxpr/dynamic_update_slice | solution.py:152
  251.9 6.8 %dynamic_update_slice.18 = f32[2,1024,1024]{2,1,0:T(8,128)} dynamic-update-slice(f32[2,1024,1024]{2,1,0:T(8,128)} %get-tuple-element.663, f32[2,256,256]{2,1,0:T(8,128)S(1)} %convert_add_fusion.9, s32[]{:T(128)} %constant.321.clone.1..sunk, s32[]{:T(128)S(6)} %select_n.96, s32[]{:T(128)S(6)} %select_n.97) | dynamic-update-slice | bytes 1048580 | tf_op jit(solution)/shard_map/while/body/eval_jaxpr/dynamic_update_slice | solution.py:152
  264.5 6.6 %dynamic_update_slice.18 = f32[2,1024,1024]{2,1,0:T(8,128)} dynamic-update-slice(f32[2,1024,1024]{2,1,0:T(8,128)} %get-tuple-element.663, f32[2,256,256]{2,1,0:T(8,128)S(1)} %convert_add_fusion.9, s32[]{:T(128)} %constant.321.clone.1..sunk, s32[]{:T(128)S(6)} %select_n.96, s32[]{:T(128)S(6)} %select_n.97) | dynamic-update-slice | bytes 1048580 | tf_op jit(solution)/shard_map/while/body/eval_jaxpr/dynamic_update_slice | solution.py:152
  276.8 6.8 %dynamic_update_slice.18 = f32[2,1024,1024]{2,1,0:T(8,128)} dynamic-update-slice(f32[2,1024,1024]{2,1,0:T(8,128)} %get-tuple-element.663, f32[2,256,256]{2,1,0:T(8,128)S(1)} %convert_add_fusion.9, s32[]{:T(128)} %constant.321.clone.1..sunk, s32[]{:T(128)S(6)} %select_n.96, s32[]{:T(128)S(6)} %select_n.97) | dynamic-update-slice | bytes 1048580 | tf_op jit(solution)/shard_map/while/body/eval_jaxpr/dynamic_update_slice | solution.py:152
  283.6 4.0 convert_element_type.185
  287.7 2.0 copy-done
  289.7 9.3 %collective-permute-start.4 = (bf16[2,128,1024]{2,1,0:T(8,128)(2,1)S(1)}, bf16[2,128,1024]{2,1,0:T(8,128)(2,1)S(1)}, u32[]{:S(2)}, u32[]{:S(2)}) collective-permute-start(bf16[2,128,1024]{2,1,0:T(8,128)(2,1)S(1)} %get-tuple-element.433), channel_id=1, source_target_pairs={{0,16},{16,32},{32,48},{48,64},{64,80},{80,96},{96,112},{1,17},{17... | collective-permute-start | bytes 1572872 | tf_op jit(solution)/shard_map/ppermute | solution.py:16
  299.1 1.9 collective-permute-start.5
  301.0 4.1 collective-permute-done.4
  305.2 4.4 collective-permute-done.5
  309.6 2.5 pad_maximum_fusion.7
  312.0 2.9 collective-permute-start.6
  317.6 138.3 %all-reduce.3.cloned.1.call-done = (f32[2,2,256,256]{3,2,1,0:T(8,128)}, f32[256,256]{1,0:T(8,128)}) async-done(((f32[2,2,256,256]{3,2,1,0:T(8,128)}, f32[256,256]{1,0:T(8,128)}), (f32[2,2,256,256]{3,2,1,0:T(8,128)}, f32[256,256]{1,0:T(8,128)})) %all-reduce.3.cloned.1.call-update) | async-done | bytes 1310736 | tf_op jit(solution)/shard_map/psum | solution.py:208
  456.9 3.1 divide_add_fusion.1
  460.0 1.7 reduce_max.9
  462.3 6.4 %maximum_convert_fusion = f32[2,1280,1280]{2,1,0:T(8,128)S(1)} fusion(bf16[2,1280,128]{2,1,0:T(8,128)(2,1)S(1)} %collective-permute-done.7, bf16[2,128,1024]{2,1,0:T(8,128)(2,1)S(1)} %collective-permute-done.5, bf16[2,1024,1024]{2,1,0:T(8,128)(2,1)} %copy-done, bf16[2,128,1024]{2,1,0:T(8,128)(2,1)S(1)} %collective-permute-done.4, ...), kind=kLoop, calls=%fused_computation.62 | loop fusion | flops 32768000 | bytes 19660800 | tf_op jit(solution)/shard_map/convert_element_type | solution.py:201
  469.1 1.9 copy-done.1
  471.6 2.2 copy-done.4
  473.8 2.0 add_select_fusion.1
  475.8 3.9 scatter-add.35
  479.7 1.7 fusion.48
  482.0 1.6 fusion.47
  483.6 6.6 %divide_add_fusion = f32[2,768,768]{2,1,0:T(8,128)} fusion(f32[2,768,768]{2,1,0:T(8,128)} %param.25, f32[2,768,768]{2,1,0:T(8,128)} %fusion.47, f32[]{:T(128)S(6)} %add.233), kind=kLoop, calls=%fused_computation.63 | loop fusion | flops 2359296 | bytes 14155780 | tf_op jit(solution)/shard_map/add | solution.py:207
  (177 shorter events, 78.0 us)
Async XLA Ops:
  7.2 11.3 %copy-start.13 = (s32[1,1,2,12]{3,2,1,0:T(2,128)S(1)}, s32[1,1,2,12]{3,2,1,0:T(2,128)}, u32[]{:S(2)}) copy-start(s32[1,1,2,12]{3,2,1,0:T(2,128)} %param.28) | copy-start | bytes 292
  7.2 448.7 %all-reduce.3.cloned.1.call-start = ((), (), s32[]{:S(2)}) async-start(), calls=%async_computation | async-start | bytes 2621440 | tf_op jit(solution)/shard_map/psum | solution.py:208
  10.7 9.5 %collective-permute-start = (bf16[2,128,768]{2,1,0:T(8,128)(2,1)}, bf16[2,128,768]{2,1,0:T(8,128)(2,1)S(1)}, u32[]{:S(2)}, u32[]{:S(2)}) collective-permute-start(bf16[2,128,768]{2,1,0:T(8,128)(2,1)} %get-tuple-element.437), channel_id=1, source_target_pairs={{0,16},{16,32},{32,48},{48,64},{64,80},{80,96},{96,112},{1,17},{17... | collective-permute-start | bytes 1179656 | tf_op jit(solution)/shard_map/ppermute | solution.py:16
  15.2 9.3 %collective-permute-start.1 = (bf16[2,128,768]{2,1,0:T(8,128)(2,1)}, bf16[2,128,768]{2,1,0:T(8,128)(2,1)S(1)}, u32[]{:S(2)}, u32[]{:S(2)}) collective-permute-start(bf16[2,128,768]{2,1,0:T(8,128)(2,1)} %get-tuple-element.438), channel_id=1, source_target_pairs={{16,0},{32,16},{48,32},{64,48},{80,64},{96,80},{112,96},{17,1},{33... | collective-permute-start | bytes 1179656 | tf_op jit(solution)/shard_map/ppermute | solution.py:17
  20.2 11.3 %copy-start.11 = (bf16[2,128,768]{2,1,0:T(8,128)(2,1)}, bf16[2,128,768]{2,1,0:T(8,128)(2,1)S(1)}, u32[]{:S(2)}) copy-start(bf16[2,128,768]{2,1,0:T(8,128)(2,1)S(1)} %collective-permute-done) | copy-start | bytes 1179652
  24.5 7.0 %copy-start.12 = (bf16[2,128,768]{2,1,0:T(8,128)(2,1)}, bf16[2,128,768]{2,1,0:T(8,128)(2,1)S(1)}, u32[]{:S(2)}) copy-start(bf16[2,128,768]{2,1,0:T(8,128)(2,1)S(1)} %collective-permute-done.1) | copy-start | bytes 1179652
  25.7 13.8 %collective-permute-start.2 = (bf16[2,1024,128]{2,1,0:T(8,128)(2,1)}, bf16[2,1024,128]{2,1,0:T(8,128)(2,1)}, u32[]{:S(2)}, u32[]{:S(2)}) collective-permute-start(bf16[2,1024,128]{2,1,0:T(8,128)(2,1)} %get-tuple-element.435), channel_id=1, source_target_pairs={{0,1},{1,2},{2,3},{3,4},{4,5},{5,6},{6,7},{7,8},{8,9},{9,10},{10,1... | collective-permute-start | bytes 1572872 | tf_op jit(solution)/shard_map/ppermute | solution.py:16
  29.7 11.1 %collective-permute-start.3 = (bf16[2,1024,128]{2,1,0:T(8,128)(2,1)}, bf16[2,1024,128]{2,1,0:T(8,128)(2,1)}, u32[]{:S(2)}, u32[]{:S(2)}) collective-permute-start(bf16[2,1024,128]{2,1,0:T(8,128)(2,1)} %get-tuple-element.436), channel_id=1, source_target_pairs={{1,0},{2,1},{3,2},{4,3},{5,4},{6,5},{7,6},{8,7},{9,8},{10,9},{11,1... | collective-permute-start | bytes 1572872 | tf_op jit(solution)/shard_map/ppermute | solution.py:17
  88.6 1.6 copy-start.5
  90.1 1.0 copy-start.7
  91.2 1.5 copy-start.6
  100.2 2.1 copy-start.8
  102.4 0.7 copy-start.9
  103.1 1.6 copy-start.5
  104.6 1.0 copy-start.7
  105.7 1.5 copy-start.6
  114.7 2.0 copy-start.8
  116.8 0.7 copy-start.9
  117.5 1.6 copy-start.5
  119.1 1.0 copy-start.7
  120.1 1.5 copy-start.6
  129.1 2.0 copy-start.8
  131.3 0.7 copy-start.9
  131.9 4.3 copy-start.3
  287.7 2.0 copy-start
  289.7 27.2 %copy-start.14 = (s32[3]{0:T(128)S(1)}, s32[3]{0:T(128)}, u32[]{:S(2)}) copy-start(s32[3]{0:T(128)} %constant.336.clone.1) | copy-start | bytes 40
  289.7 15.4 %collective-permute-start.4 = (bf16[2,128,1024]{2,1,0:T(8,128)(2,1)S(1)}, bf16[2,128,1024]{2,1,0:T(8,128)(2,1)S(1)}, u32[]{:S(2)}, u32[]{:S(2)}) collective-permute-start(bf16[2,128,1024]{2,1,0:T(8,128)(2,1)S(1)} %get-tuple-element.433), channel_id=1, source_target_pairs={{0,16},{16,32},{32,48},{48,64},{64,80},{80,96},{96,112},{1,17},{17... | collective-permute-start | bytes 1572872 | tf_op jit(solution)/shard_map/ppermute | solution.py:16
  299.1 10.5 %collective-permute-start.5 = (bf16[2,128,1024]{2,1,0:T(8,128)(2,1)S(1)}, bf16[2,128,1024]{2,1,0:T(8,128)(2,1)S(1)}, u32[]{:S(2)}, u32[]{:S(2)}) collective-permute-start(bf16[2,128,1024]{2,1,0:T(8,128)(2,1)S(1)} %get-tuple-element.434), channel_id=1, source_target_pairs={{16,0},{32,16},{48,32},{64,48},{80,64},{96,80},{112,96},{17,1},{33... | collective-permute-start | bytes 1572872 | tf_op jit(solution)/shard_map/ppermute | solution.py:17
  301.0 155.9 %copy-start.10 = (f32[2,2,256,256]{3,2,1,0:T(8,128)S(1)}, f32[2,2,256,256]{3,2,1,0:T(8,128)}, u32[]{:S(2)}) copy-start(f32[2,2,256,256]{3,2,1,0:T(8,128)} %param.26) | copy-start | bytes 3145732
  312.0 150.3 %collective-permute-start.6 = (bf16[2,1280,128]{2,1,0:T(8,128)(2,1)}, bf16[2,1280,128]{2,1,0:T(8,128)(2,1)S(1)}, u32[]{:S(2)}, u32[]{:S(2)}) collective-permute-start(bf16[2,1280,128]{2,1,0:T(8,128)(2,1)} %get-tuple-element.431), channel_id=1, source_target_pairs={{0,1},{1,2},{2,3},{3,4},{4,5},{5,6},{6,7},{7,8},{8,9},{9,10},{10,1... | collective-permute-start | bytes 1966088 | tf_op jit(solution)/shard_map/ppermute | solution.py:16
  315.0 147.4 %collective-permute-start.7 = (bf16[2,1280,128]{2,1,0:T(8,128)(2,1)}, bf16[2,1280,128]{2,1,0:T(8,128)(2,1)S(1)}, u32[]{:S(2)}, u32[]{:S(2)}) collective-permute-start(bf16[2,1280,128]{2,1,0:T(8,128)(2,1)} %get-tuple-element.432), channel_id=1, source_target_pairs={{1,0},{2,1},{3,2},{4,3},{5,4},{6,5},{7,6},{8,7},{9,8},{10,9},{11,1... | collective-permute-start | bytes 1966088 | tf_op jit(solution)/shard_map/ppermute | solution.py:17
  468.8 2.2 copy-start.1
  471.6 2.2 copy-start.4
  479.7 2.3 copy-start.2
Sparse Core Ops, SparseCore 0:
  301.2 154.7 all-reduce.2
where the time goes:
time: 502 us; the launch traced here: 497 us
  local copies, waits for them, and re-layouts  160 us (32%)
  waiting for transfers between devices  154 us (31%)
  other arithmetic  79.7 us (16%)
  loops' own time  45.7 us (9%)
  starting transfers between devices  27.2 us (5%)
  matrix products  15.3 us (3%)
  between operations  15 us (3%)
    psum x1, waiting for transfers between devices, on_device(): lax.psum((probe_total, cover_total), ('row', 'col'))  138 us
    dynamic_update_slice x12, local copies, waits for them, and re-layouts, add_single(): return lax.dynamic_update_slice(current_canvas, current + piece, anchor)  77.7 us
    another operation x1, loops' own time, place_terms(): return lax.fori_loop(0, object_terms.shape[0], add_single, canvas)  45.3 us
    gather x36, local copies, waits for them, and re-layouts  44.2 us
    ppermute x4, starting transfers between devices, with_halo(): before = lax.ppermute(last, axis, up)  20.7 us
    add x12, other arithmetic, add_single(): return lax.dynamic_update_slice(current_canvas, current + piece, anchor)  17 us
    unnamed x22, local copies, waits for them, and re-layouts  11.3 us
  transfers between devices with their start and end apart: 9, of which 6 were waited for; matrix products, arithmetic and copies ran while one was open for 4% of the time, Pallas kernels for 0%

commit v1 on v0

v1 whole, which is shorter than its diff:
```python
import functools
import math

import jax
import jax.numpy as jnp
import ml_dtypes
import numpy as np
from jax import lax
from jax.experimental import pallas as pl
from jax.experimental.pallas import tpu as pltpu
from jax.sharding import PartitionSpec as P

MESH = pl.DeviceIdType.MESH
F32, BF16 = jnp.float32, jnp.bfloat16
SIZE, TILE, HALF, LANES = 256, 768, 128, 128
EXT = TILE + 2 * HALF
PANELS = TILE // LANES
MODES = 2
PLANES = 2 * MODES
N_ROW, N_COL = 8, 16
UNITS = 128
VMEM = pl.BlockSpec(memory_space=pltpu.VMEM)
SMEM = pl.BlockSpec(memory_space=pltpu.SMEM)
ANY = pl.BlockSpec(memory_space=pl.ANY)
LIMIT = 40 * 2**20


def dft_tables():
    indices = np.arange(SIZE)
    product = indices[:, None] * indices[None, :] % SIZE
    angles = product.astype(np.float32) * np.float32(2.0 * np.pi / SIZE)
    scale = np.float32(1.0 / math.sqrt(SIZE))
    cosine = (np.cos(angles) * scale).astype(ml_dtypes.bfloat16)
    sine = (np.sin(angles) * scale).astype(ml_dtypes.bfloat16)
    positive = np.block([[cosine, -sine], [sine, cosine]])
    negative = np.block([[cosine, sine], [-sine, cosine]])
    return positive, negative


def around(row, col):
    up, down = lax.rem(row + N_ROW - 1, N_ROW), lax.rem(row + 1, N_ROW)
    left, right = lax.rem(col + N_COL - 1, N_COL), lax.rem(col + 1, N_COL)
    return [(up, col), (down, col), (row, left), (row, right), (up, left), (up, right), (down, left), (down, right)]


def greet(targets):
    barrier = pltpu.get_barrier_semaphore()
    for target in targets:
        pl.semaphore_signal(barrier, inc=1, device_id=target, device_id_type=MESH)
    return barrier


def remote(src, dst, send, recv, target):
    return pltpu.make_async_remote_copy(
        src_ref=src, dst_ref=dst, send_sem=send, recv_sem=recv, device_id=target, device_id_type=MESH
    )


def inside(row, col):
    up, down, left, right = row > 0, row < N_ROW - 1, col > 0, col < N_COL - 1
    return [up, down, left, right, up & left, up & right, down & left, down & right]


def rim_copies(out, got, send, recv, row, col):
    opposite = (1, 0, 3, 2, 7, 6, 5, 4)
    return [
        remote(out[i], got[opposite[i]], send.at[i], recv.at[opposite[i]], target)
        for i, target in enumerate(around(row, col))
    ]


def exchange_object(obj, wide, held, low_v, low_h, got_v, got_h, got_c, load, send, recv):
    row, col = lax.axis_index("row"), lax.axis_index("col")
    order = (0, PANELS - 1) + tuple(range(1, PANELS - 1))
    loads = [
        pltpu.make_async_copy(obj.at[:, :, k * LANES : (k + 1) * LANES], held.at[:, k], load.at[k])
        for k in range(PANELS)
    ]
    for k in order:
        loads[k].start()
    barrier = greet(around(row, col))
    rims = rim_copies(
        [low_v.at[0], low_v.at[1], low_h.at[0], low_h.at[1]]
        + [low_h.at[0, :, 0:HALF], low_h.at[1, :, 0:HALF], low_h.at[0, :, TILE - HALF :], low_h.at[1, :, TILE - HALF :]],
        [got_v.at[0], got_v.at[1], got_h.at[0], got_h.at[1]] + [got_c.at[i] for i in range(4)],
        send,
        recv,
        row,
        col,
    )
    for step, k in enumerate(order):
        loads[k].wait()

        @pl.loop(0, TILE // HALF)
        def _(i, k=k):
            rows = pl.ds(pl.multiple_of(i * HALF, HALF), HALF)
            for p in range(2):
                low = held[p, k, rows, :].astype(BF16)
                wide[p, k + 1, pl.ds(pl.multiple_of(i * HALF + HALF, HALF), HALF), :] = low.astype(F32)
                if k == 0:
                    low_h[0, p, rows, :] = low
                if k == PANELS - 1:
                    low_h[1, p, rows, :] = low

        for p in range(2):
            low_v[0, p, k] = held[p, k, 0:HALF, :].astype(BF16)
            low_v[1, p, k] = held[p, k, TILE - HALF :, :].astype(BF16)
        if step == 1:
            pl.semaphore_wait(barrier, 8)
            for i in (2, 3, 4, 5, 6, 7):
                rims[i].start()
    for i in (0, 1):
        rims[i].start()
    have = inside(row, col)

    def keep(i, value):
        return jnp.where(have[i], value.astype(F32), 0.0)

    for i in (0, 1, 4, 5, 6, 7, 2, 3):
        rims[i].wait()
    for p in range(2):
        for k in range(PANELS):
            wide[p, k + 1, 0:HALF, :] = keep(0, got_v[0, p, k])
            wide[p, k + 1, EXT - HALF :, :] = keep(1, got_v[1, p, k])
        for corner in range(4):
            rows = slice(0, HALF) if corner < 2 else slice(EXT - HALF, EXT)
            wide[p, (corner % 2) * (PANELS + 1), rows, :] = keep(4 + corner, got_c[corner, p])

    @pl.loop(0, TILE // HALF)
    def _(i):
        rows = pl.ds(pl.multiple_of(i * HALF, HALF), HALF)
        to = pl.ds(pl.multiple_of(i * HALF + HALF, HALF), HALF)
        for p in range(2):
            wide[p, 0, to, :] = keep(2, got_h[0, p, rows, :])
            wide[p, PANELS + 1, to, :] = keep(3, got_h[1, p, rows, :])


def process_slots(counts, centers, wide, probe, patterns, positive, negative, units, canvas, low, sums, patch, wave, half, shift, back):
    row_id, col_id = lax.axis_index("row"), lax.axis_index("col")

    @pl.loop(0, EXT // 32)
    def _(i):
        rows = pl.ds(pl.multiple_of(i * 32, 32), 32)
        for p in range(2):
            for k in range(PANELS + 2):
                canvas[p, k, rows, :] = jnp.zeros((32, LANES), F32)

    low[...] = probe[...].astype(BF16).astype(F32)
    sums[...] = jnp.zeros_like(sums)
    lane = lax.broadcasted_iota(jnp.int32, (SIZE, LANES), 1)
    real, imag = slice(0, SIZE), slice(SIZE, 2 * SIZE)

    @pl.loop(0, counts[row_id, col_id])
    def _(s):
        row, col = centers[0, s], centers[1, s]
        panel = col // LANES
        turn = col - panel * LANES
        rows = pl.ds(row, SIZE)
        field = []
        for p in range(2):
            parts = [pltpu.roll(wide[p, panel + k, rows, :], lax.rem(LANES - turn, LANES), 1) for k in range(3)]
            whole = jnp.concatenate(
                [jnp.where(lane < LANES - turn, parts[k], parts[k + 1]) for k in range(2)], 1
            )
            patch[p] = whole
            field.append(whole)
        sums[PLANES] += field[0] * field[0] + field[1] * field[1]
        for m in range(MODES):
            wave[m, :, real] = (low[m, 0] * field[0] - low[m, 1] * field[1]).astype(BF16)
            wave[m, :, imag] = (low[m, 0] * field[1] + low[m, 1] * field[0]).astype(BF16)
        for m in range(MODES):
            product = jnp.dot(wave[m], positive[...], preferred_element_type=F32)
            half[m, real, :] = product[:, real].astype(BF16)
            half[m, imag, :] = product[:, imag].astype(BF16)
        spectra = []
        for m in range(MODES):
            spectra.append(
                (
                    jnp.dot(negative[real, :], half[m], preferred_element_type=F32),
                    jnp.dot(negative[imag, :], half[m], preferred_element_type=F32),
                )
            )
        power = (
            spectra[0][0] * spectra[0][0]
            + spectra[0][1] * spectra[0][1]
            + spectra[1][0] * spectra[1][0]
            + spectra[1][1] * spectra[1][1]
        )
        factor = patterns[s].astype(F32) * lax.rsqrt(jnp.maximum(power, 0.5)) - 1.0
        for m in range(MODES):
            shift[m, :, real] = (factor * spectra[m][0]).astype(BF16)
            shift[m, :, imag] = (factor * spectra[m][1]).astype(BF16)
        for m in range(MODES):
            product = jnp.dot(shift[m], negative[...], preferred_element_type=F32)
            back[m, real, :] = product[:, real].astype(BF16)
            back[m, imag, :] = product[:, imag].astype(BF16)
        terms = [0.0, 0.0]
        for m in range(MODES):
            change_real = jnp.dot(positive[real, :], back[m], preferred_element_type=F32)
            change_imag = jnp.dot(positive[imag, :], back[m], preferred_element_type=F32)
            terms[0] = terms[0] + low[m, 0] * change_real + low[m, 1] * change_imag
            terms[1] = terms[1] + low[m, 0] * change_imag - low[m, 1] * change_real
            sums[2 * m] += patch[0] * change_real + patch[1] * change_imag
            sums[2 * m + 1] += patch[0] * change_imag - patch[1] * change_real
        for p in range(2):
            term = terms[p].astype(BF16).astype(F32)
            first = pltpu.roll(term[:, :LANES], turn, 1)
            second = pltpu.roll(term[:, LANES:], turn, 1)
            canvas[p, panel, rows, :] += jnp.where(lane < turn, 0.0, first)
            canvas[p, panel + 1, rows, :] += jnp.where(lane < turn, first, second)
            canvas[p, panel + 2, rows, :] += jnp.where(lane < turn, second, 0.0)

    @pl.loop(0, SIZE // 8)
    def _(i):
        for q in range(PLANES + 1):
            for k in range(2):
                value = sums[q, pl.ds(pl.multiple_of(i * 8, 8), 8), k * LANES : (k + 1) * LANES]
                units[k * 64 + 2 * i, q] = value[0:4]
                units[k * 64 + 2 * i + 1, q] = value[4:8]


def exchange_sums(
    canvas, units, probe, got_v, got_h, got_c, update, peak,
    low_v, low_h, low_c, pair, half, from_x, quarter, from_col,
    send, recv, pair_send, pair_recv, x_send, x_recv, col_send, col_recv,
):
    row, col = lax.axis_index("row"), lax.axis_index("col")
    x, core = row // 2, lax.rem(row, 2)
    sibling = (row + 1 - 2 * core, col)
    x_peers = [(lax.rem(row + 2 * j, N_ROW), col) for j in (1, 2, 3)]
    col_peers = [(row, lax.rem(col + j, N_COL)) for j in range(1, N_COL)]
    tiles = around(row, col)
    others = jnp.where(core == 0, tiles[0][0], tiles[1][0])
    barrier = greet([sibling, (others, col)] + tiles[4:] + x_peers + col_peers)
    pl.semaphore_wait(barrier, 2 + 4 + 3 + N_COL - 1)

    mine = core * 64
    to_pair = remote(units.at[pl.ds(64 - mine, 64)], pair, pair_send.at[0], pair_recv.at[0], sibling)
    to_pair.start()

    @pl.loop(0, TILE // HALF)
    def _(i):
        rows = pl.ds(pl.multiple_of(i * HALF, HALF), HALF)
        at = pl.ds(pl.multiple_of(i * HALF + HALF, HALF), HALF)
        for p in range(2):
            low_h[0, p, rows, :] = canvas[p, 0, at, :].astype(BF16)
            low_h[1, p, rows, :] = canvas[p, PANELS + 1, at, :].astype(BF16)

    for p in range(2):
        for corner in range(4):
            at = slice(0, HALF) if corner < 2 else slice(EXT - HALF, EXT)
            low_c[corner, p] = canvas[p, (corner % 2) * (PANELS + 1), at, :].astype(BF16)
        for k in range(PANELS):
            low_v[0, p, k] = canvas[p, k + 1, 0:HALF, :].astype(BF16)
            low_v[1, p, k] = canvas[p, k + 1, EXT - HALF :, :].astype(BF16)
    rims = rim_copies(
        [low_v.at[0], low_v.at[1], low_h.at[0], low_h.at[1]] + [low_c.at[i] for i in range(4)],
        [got_v.at[0], got_v.at[1], got_h.at[0], got_h.at[1]] + [got_c.at[i] for i in range(4)],
        send,
        recv,
        row,
        col,
    )
    for i in (2, 3, 4, 5, 6, 7, 0, 1):
        rims[i].start()
    squares = probe[0, 0] * probe[0, 0] + probe[0, 1] * probe[0, 1]
    squares = squares + probe[1, 0] * probe[1, 0] + probe[1, 1] * probe[1, 1]
    peak[...] = jnp.broadcast_to(jnp.max(squares, keepdims=True) + 1e-06, peak.shape)

    to_pair.wait()

    @pl.loop(0, 64)
    def _(i):
        half[i] = units[mine + i] + pair[i]

    to_x = [
        remote(half.at[pl.ds(16 * (peer[0] // 2), 16)], from_x.at[j], x_send.at[j], x_recv.at[j], peer)
        for j, peer in enumerate(x_peers)
    ]
    for copy in to_x:
        copy.start()
    for copy in to_x:
        copy.wait()

    @pl.loop(0, 16)
    def _(i):
        quarter[i] = half[16 * x + i] + from_x[0, i] + from_x[1, i] + from_x[2, i]

    to_col = [
        remote(quarter.at[peer[1]], from_col.at[j], col_send.at[j], col_recv.at[j], peer)
        for j, peer in enumerate(col_peers)
    ]
    for copy in to_col:
        copy.start()
    for copy in to_col:
        copy.wait()
    total = quarter[col]
    for j in range(N_COL - 1):
        total = total + from_col[j]
    spread = lax.rsqrt(total[PLANES])
    fresh = jnp.concatenate([total[q] * spread for q in range(PLANES)], 0).astype(BF16)
    unit = mine + 16 * x + col
    update[unit] = fresh
    to_col = [
        remote(update.at[unit], update.at[unit], col_send.at[N_COL - 1 + j], col_recv.at[N_COL - 1 + j], peer)
        for j, peer in enumerate(col_peers)
    ]
    for copy in to_col:
        copy.start()
    for copy in to_col:
        copy.wait()
    block = update.at[pl.ds(mine + 16 * x, 16)]
    to_x = [remote(block, block, x_send.at[3 + j], x_recv.at[3 + j], peer) for j, peer in enumerate(x_peers)]
    for copy in to_x:
        copy.start()
    for copy in to_x:
        copy.wait()
    block = update.at[pl.ds(mine, 64)]
    to_pair = remote(block, block, pair_send.at[1], pair_recv.at[1], sibling)
    to_pair.start()
    to_pair.wait()
    for copy in rims:
        copy.wait()


def write_results(canvas, held, got_v, got_h, got_c, update, peak, probe, new_object, new_probe, stage, store):
    row, col = lax.axis_index("row"), lax.axis_index("col")
    have = inside(row, col)
    scale = 1.0 / peak[0:1, :]

    def keep(i, value):
        return jnp.where(have[i], value.astype(F32), 0.0)

    stores = []
    for k in range(PANELS):
        for p in range(2):
            side = None if k not in (0, PANELS - 1) else (0 if k == 0 else 1)
            for i in range(TILE // HALF):
                rows = slice(i * HALF, (i + 1) * HALF)
                value = canvas[p, k + 1, HALF + i * HALF : 2 * HALF + i * HALF, :]
                if i == 0:
                    value = value + keep(0, got_v[0, p, k])
                if i == TILE // HALF - 1:
                    value = value + keep(1, got_v[1, p, k])
                if side is not None:
                    value = value + keep(2 + side, got_h[side, p, rows, :])
                    if i == 0:
                        value = value + keep(4 + side, got_c[side, p])
                    if i == TILE // HALF - 1:
                        value = value + keep(6 + side, got_c[2 + side, p])
                stage[p, k, rows, :] = held[p, k, rows, :] + value * scale
        copy = pltpu.make_async_copy(stage.at[:, k], new_object.at[:, :, k * LANES : (k + 1) * LANES], store.at[k])
        copy.start()
        stores.append(copy)

    @pl.loop(0, SIZE // 8)
    def _(i):
        rows = pl.ds(pl.multiple_of(i * 8, 8), 8)
        for k in range(2):
            lanes = slice(k * LANES, (k + 1) * LANES)
            first = update[k * 64 + 2 * i].astype(F32)
            second = update[k * 64 + 2 * i + 1].astype(F32)
            for q in range(PLANES):
                value = jnp.concatenate([first[4 * q : 4 * q + 4], second[4 * q : 4 * q + 4]], 0)
                new_probe[q // 2, q % 2, rows, lanes] = probe[q // 2, q % 2, rows, lanes] + value

    for copy in stores:
        copy.wait()


def on_device(object_field, probe_modes, counts, centers, patterns):
    positive, negative = dft_tables()
    dma = pltpu.SemaphoreType.DMA
    probe = pltpu.with_memory_space_constraint(probe_modes, pltpu.VMEM)
    amplitudes = pltpu.with_memory_space_constraint(patterns[0, 0], pltpu.VMEM)
    positive = pltpu.with_memory_space_constraint(jnp.asarray(positive), pltpu.VMEM)
    negative = pltpu.with_memory_space_constraint(jnp.asarray(negative), pltpu.VMEM)
    strips = [
        pltpu.VMEM((2, 2, PANELS, HALF, LANES), BF16),
        pltpu.VMEM((2, 2, TILE, LANES), BF16),
        pltpu.VMEM((4, 2, HALF, LANES), BF16),
    ]

    def inner(*arrays):
        return [pltpu.with_memory_space_constraint(a, pltpu.VMEM) for a in arrays]

    wide, held = pl.pallas_call(
        exchange_object,
        out_shape=[pltpu.VMEM((2, PANELS + 2, EXT, LANES), F32), pltpu.VMEM((2, PANELS, TILE, LANES), F32)],
        in_specs=[ANY],
        out_specs=[VMEM, VMEM],
        scratch_shapes=strips[:2] + strips + [dma((PANELS,)), dma((8,)), dma((8,))],
        compiler_params=pltpu.CompilerParams(collective_id=0, has_side_effects=True, vmem_limit_bytes=LIMIT),
        name="exchange_object",
    )(object_field)
    wide, held = inner(wide, held)
    units, canvas = pl.pallas_call(
        process_slots,
        out_shape=[pltpu.VMEM((UNITS, PLANES + 1, 4, LANES), F32), pltpu.VMEM((2, PANELS + 2, EXT, LANES), F32)],
        in_specs=[SMEM, SMEM, VMEM, VMEM, VMEM, VMEM, VMEM],
        out_specs=[VMEM, VMEM],
        scratch_shapes=[
            pltpu.VMEM((MODES, 2, SIZE, SIZE), F32),
            pltpu.VMEM((PLANES + 1, SIZE, SIZE), F32),
            pltpu.VMEM((2, SIZE, SIZE), F32),
            pltpu.VMEM((MODES, SIZE, 2 * SIZE), BF16),
            pltpu.VMEM((MODES, 2 * SIZE, SIZE), BF16),
            pltpu.VMEM((MODES, SIZE, 2 * SIZE), BF16),
            pltpu.VMEM((MODES, 2 * SIZE, SIZE), BF16),
        ],
        compiler_params=pltpu.CompilerParams(vmem_limit_bytes=LIMIT),
        name="process_slots",
    )(counts, centers[0, 0], wide, probe, amplitudes, positive, negative)
    units, canvas = inner(units, canvas)
    got_v, got_h, got_c, update, peak = pl.pallas_call(
        exchange_sums,
        out_shape=strips + [pltpu.VMEM((UNITS, 16, LANES), BF16), pltpu.VMEM((8, LANES), F32)],
        in_specs=[VMEM] * 3,
        out_specs=[VMEM] * 5,
        scratch_shapes=strips
        + [
            pltpu.VMEM((64, PLANES + 1, 4, LANES), F32),
            pltpu.VMEM((64, PLANES + 1, 4, LANES), F32),
            pltpu.VMEM((3, 16, PLANES + 1, 4, LANES), F32),
            pltpu.VMEM((16, PLANES + 1, 4, LANES), F32),
            pltpu.VMEM((N_COL - 1, PLANES + 1, 4, LANES), F32),
            dma((8,)), dma((8,)), dma((2,)), dma((2,)), dma((6,)), dma((6,)), dma((2 * N_COL - 2,)), dma((2 * N_COL - 2,)),
        ],
        compiler_params=pltpu.CompilerParams(collective_id=1, has_side_effects=True, vmem_limit_bytes=LIMIT),
        name="exchange_sums",
    )(canvas, units, probe)
    new_object, new_probe = pl.pallas_call(
        write_results,
        out_shape=[
            jax.ShapeDtypeStruct(object_field.shape, F32),
            jax.ShapeDtypeStruct(probe_modes.shape, F32),
        ],
        in_specs=[VMEM] * 8,
        out_specs=[ANY, VMEM],
        scratch_shapes=[pltpu.VMEM((2, PANELS, TILE, LANES), F32), dma((PANELS,))],
        compiler_params=pltpu.CompilerParams(vmem_limit_bytes=LIMIT),
        name="write_results",
    )(*inner(canvas, held, got_v, got_h, got_c, update, peak), probe)
    return new_object, new_probe


def solution(mesh):
    placed = (
        P(None, "row", "col"),
        P(),
        P(),
        P("row", "col", None, None),
        P("row", "col", None, None, None),
    )
    return jax.shard_map(
        on_device,
        mesh=mesh,
        in_specs=placed,
        out_specs=(P(None, "row", "col"), P()),
        check_vma=False,
    )
```

time: 502 us -> 91.1 us (0.18)
  local copies, waits for them, and re-layouts: 160 us -> 5.64 us
  waiting for transfers between devices: 154 us -> 0 us
  Pallas kernels: 0 us -> 84.6 us
  other arithmetic: 79.7 us -> 0 us
  loops' own time: 45.7 us -> 0 us
  starting transfers between devices: 27.2 us -> 0 us
  matrix products: 15.3 us -> 0 us
  between operations: 15 us -> 0.72 us
    psum x1 -> x0, waiting for transfers between devices: 138 us -> none  [on_device(): lax.psum((probe_total, cover_total), ('row', 'col'))]
    pallas_call x0 -> x4, Pallas kernels: none -> 84.6 us  [the longest x1 52.1 us: on_device(): pl.pallas_call(exchange_sums, out_shape=strips + [pltpu.VMEM((UNITS, 16,...]
    dynamic_update_slice x12 -> x0, local copies, waits for them, and re-layouts: 77.7 us -> none  [add_single(): return lax.dynamic_update_slice(current_canvas, current + piece, anchor)]
    another operation x3 -> x0, loops' own time: 45.7 us -> none  [the longest x1 45.3 us: place_terms(): return lax.fori_loop(0, object_terms.shape[0], add_single, canvas)]
    gather x36 -> x0, local copies, waits for them, and re-layouts: 44.2 us -> none
    add x20 -> x0, other arithmetic: 27.8 us -> none  [the longest x12 17 us: add_single(): return lax.dynamic_update_slice(current_canvas, current + piece, anchor)]
    ppermute x8 -> x0, starting transfers between devices: 27.1 us -> none  [the longest x4 20.7 us: with_halo(): before = lax.ppermute(last, axis, up)]
    convert_element_type x17 -> x0, other arithmetic: 18.6 us -> none  [the longest x1 6.44 us: on_device(): with_halo(canvas.astype(jnp.bfloat16), (('row', 1), ('col', 2)), half_width)]
  transfers between devices with their start and end apart: 9 -> 0, of which waited for: 6 -> 0; matrix products, arithmetic and copies ran while one was open for 4% -> 0% of each run, Pallas kernels for 0% -> 0%
where the time goes in v1:
time: 91.1 us; the launch traced here: 90.9 us
  Pallas kernels  84.6 us (93%)
  local copies, waits for them, and re-layouts  5.64 us (6%)
    pallas_call x1, Pallas kernels, on_device(): pl.pallas_call(exchange_sums, out_shape=strips + [pltpu.VMEM((UNITS, 16,...  52.1 us
    pallas_call x1, Pallas kernels, on_device(): pl.pallas_call(exchange_object, out_shape=[pltpu.VMEM((2, PANELS + 2, EXT...  21.8 us
    pallas_call x1, Pallas kernels, on_device(): pl.pallas_call(process_slots, out_shape=[pltpu.VMEM((UNITS, PLANES + 1, 4...  7.24 us
    unnamed x18, local copies, waits for them, and re-layouts  5.64 us
    pallas_call x1, Pallas kernels, on_device(): pl.pallas_call(write_results, out_shape=[jax.ShapeDtypeStruct(object_fiel...  3.42 us

profile of v1, /device:TPU:1, one launch (start us, length us, event | category | flops | bytes accessed | tf_op | source)
XLA Modules:
  0.0 90.9 jit_solution(17426971630107720489)
XLA Ops:
  0.6 0.0 copy-start.7
  0.6 0.0 copy-start
  0.7 0.0 copy-start.4
  0.7 21.8 %exchange_object.1 = (f32[2,8,1024,128]{3,2,1,0:T(8,128)S(1)}, f32[2,6,768,128]{3,2,1,0:T(8,128)S(1)}) custom-call(f32[2,768,768]{2,1,0:T(8,128)} %obj.1), custom_call_target="tpu_custom_call" | custom-call | tf_op jit(solution)/shard_map/exchange_object/pallas_call | solution.py:387
  22.5 0.0 copy-start.2
  22.5 2.2 %copy-done.2 = f32[2,6,768,128]{3,2,1,0:T(8,128)} copy-done((f32[2,6,768,128]{3,2,1,0:T(8,128)}, f32[2,6,768,128]{3,2,1,0:T(8,128)S(1)}, u32[]{:S(2)}) %copy-start.2) | copy-done | bytes 4718616
  24.6 0.0 copy-done.7
  24.6 0.0 copy-done
  24.6 0.0 copy-done.4
  24.7 0.0 copy-start.8
  24.7 1.0 %copy-done.8 = bf16[512,512]{1,0:T(8,128)(2,1)S(1)} copy-done((bf16[512,512]{1,0:T(8,128)(2,1)S(1)}, bf16[512,512]{1,0:T(8,128)(2,1)}, u32[]{:S(2)}) %copy-start.8) | copy-done | bytes 524312
  25.7 7.2 %process_slots.1 = (f32[128,5,4,128]{3,2,1,0:T(4,128)S(1)}, f32[2,8,1024,128]{3,2,1,0:T(8,128)S(1)}) custom-call(s32[8,16]{1,0:T(8,128)} %counts.1, s32[2,12]{1,0:T(2,128)} %bitcast.3, f32[2,8,1024,128]{3,2,1,0:T(8,128)S(1)} %get-tuple-element.11.wide, f32[2,2,256,256]{3,2,1,0:T(8,128)S(1)} %copy-done, bf16[12,256,256]{2,1,0:T(8,128)(2,1)S(1)} %bitcast.2, ...), custom_call_target="tpu_custom_call" | custom-call | tf_op jit(solution)/shard_map/process_slots/pallas_call | solution.py:397
  32.9 0.0 copy-start.5
  32.9 1.1 %copy-done.5 = f32[128,5,4,128]{3,2,1,0:T(4,128)} copy-done((f32[128,5,4,128]{3,2,1,0:T(4,128)}, f32[128,5,4,128]{3,2,1,0:T(4,128)S(1)}, u32[]{:S(2)}) %copy-start.5) | copy-done | bytes 1310744
  34.0 0.0 copy-start.6
  34.0 1.3 %copy-done.6 = f32[128,5,4,128]{3,2,1,0:T(4,128)S(1)} copy-done((f32[128,5,4,128]{3,2,1,0:T(4,128)S(1)}, f32[128,5,4,128]{3,2,1,0:T(4,128)}, u32[]{:S(2)}) %copy-start.6) | copy-done | bytes 1310744
  35.3 0.0 copy-start.1
  35.3 0.0 copy-start.3
  35.4 52.1 %exchange_sums.1 = (bf16[2,2,6,128,128]{4,3,2,1,0:T(8,128)(2,1)S(1)}, bf16[2,2,768,128]{3,2,1,0:T(8,128)(2,1)S(1)}, bf16[4,2,128,128]{3,2,1,0:T(8,128)(2,1)S(1)}...) custom-call(f32[2,8,1024,128]{3,2,1,0:T(8,128)S(1)} %get-tuple-element.12.canvas, f32[128,5,4,128]{3,2,1,0:T(4,128)S(1)} %copy-done.6, ...), custom_call_target="tpu_custom_call" | custom-call | tf_op jit(solution)/shard_map/exchange_sums/pallas_call | solution.py:415
  87.5 0.0 copy-done.1
  87.5 0.0 copy-done.3
  87.5 3.4 %write_results.1 = (f32[2,768,768]{2,1,0:T(8,128)}, f32[2,2,256,256]{3,2,1,0:T(8,128)}) custom-call(f32[2,8,1024,128]{3,2,1,0:T(8,128)S(1)} %get-tuple-element.12.canvas, f32[2,6,768,128]{3,2,1,0:T(8,128)S(1)} %copy-done.3, bf16[2,2,6,128,128]{4,3,2,1,0:T(8,128)(2,1)S(1)} %get-tuple-element.15.got_v, bf16[2,2,768,128]{3,2,1,0:T(8,128)(2,1)S(1)} %get-tuple-element.16.got_h, ...), custom_call_target="tpu_custom_call" | custom-call | tf_op jit(solution)/shard_map/write_results/pallas_call | solution.py:432
Async XLA Ops:
  0.6 24.0 %copy-start.7 = (bf16[512,512]{1,0:T(8,128)(2,1)S(1)}, bf16[512,512]{1,0:T(8,128)(2,1)}, u32[]{:S(2)}) copy-start(bf16[512,512]{1,0:T(8,128)(2,1)} %constant.5.clone.negative) | copy-start | bytes 1572868
  0.6 24.0 %copy-start = (f32[2,2,256,256]{3,2,1,0:T(8,128)S(1)}, f32[2,2,256,256]{3,2,1,0:T(8,128)}, u32[]{:S(2)}) copy-start(f32[2,2,256,256]{3,2,1,0:T(8,128)} %probe.5) | copy-start | bytes 3145732
  0.7 24.0 %copy-start.4 = (bf16[1,1,12,256,256]{4,3,2,1,0:T(8,128)(2,1)S(1)}, bf16[1,1,12,256,256]{4,3,2,1,0:T(8,128)(2,1)}, u32[]{:S(2)}) copy-start(bf16[1,1,12,256,256]{4,3,2,1,0:T(8,128)(2,1)} %param.11) | copy-start | bytes 4718596
  22.5 2.2 %copy-start.2 = (f32[2,6,768,128]{3,2,1,0:T(8,128)}, f32[2,6,768,128]{3,2,1,0:T(8,128)S(1)}, u32[]{:S(2)}) copy-start(f32[2,6,768,128]{3,2,1,0:T(8,128)S(1)} %get-tuple-element.13.held) | copy-start | bytes 14155780
  24.7 1.0 %copy-start.8 = (bf16[512,512]{1,0:T(8,128)(2,1)S(1)}, bf16[512,512]{1,0:T(8,128)(2,1)}, u32[]{:S(2)}) copy-start(bf16[512,512]{1,0:T(8,128)(2,1)} %constant.4.clone.positive) | copy-start | bytes 1572868
  32.9 1.1 %copy-start.5 = (f32[128,5,4,128]{3,2,1,0:T(4,128)}, f32[128,5,4,128]{3,2,1,0:T(4,128)S(1)}, u32[]{:S(2)}) copy-start(f32[128,5,4,128]{3,2,1,0:T(4,128)S(1)} %get-tuple-element.14.units) | copy-start | bytes 3932164
  34.0 1.3 %copy-start.6 = (f32[128,5,4,128]{3,2,1,0:T(4,128)S(1)}, f32[128,5,4,128]{3,2,1,0:T(4,128)}, u32[]{:S(2)}) copy-start(f32[128,5,4,128]{3,2,1,0:T(4,128)} %copy-done.5) | copy-start | bytes 3932164
  35.3 52.1 %copy-start.1 = (f32[2,2,256,256]{3,2,1,0:T(8,128)S(1)}, f32[2,2,256,256]{3,2,1,0:T(8,128)}, u32[]{:S(2)}) copy-start(f32[2,2,256,256]{3,2,1,0:T(8,128)} %probe.5) | copy-start | bytes 3145732
  35.3 52.1 %copy-start.3 = (f32[2,6,768,128]{3,2,1,0:T(8,128)S(1)}, f32[2,6,768,128]{3,2,1,0:T(8,128)}, u32[]{:S(2)}) copy-start(f32[2,6,768,128]{3,2,1,0:T(8,128)} %copy-done.2) | copy-start | bytes 14155780

commit v2 on v1

--- a/solution.py
+++ b/solution.py
@@ -21,8 +21,9 @@
 UNITS = 128
 VMEM = pl.BlockSpec(memory_space=pltpu.VMEM)
 SMEM = pl.BlockSpec(memory_space=pltpu.SMEM)
+HBM = pl.BlockSpec(memory_space=pltpu.HBM)
 ANY = pl.BlockSpec(memory_space=pl.ANY)
-LIMIT = 40 * 2**20
+MIB = 2**20
 
 
 def dft_tables():
@@ -30,11 +31,8 @@
     product = indices[:, None] * indices[None, :] % SIZE
     angles = product.astype(np.float32) * np.float32(2.0 * np.pi / SIZE)
     scale = np.float32(1.0 / math.sqrt(SIZE))
-    cosine = (np.cos(angles) * scale).astype(ml_dtypes.bfloat16)
-    sine = (np.sin(angles) * scale).astype(ml_dtypes.bfloat16)
-    positive = np.block([[cosine, -sine], [sine, cosine]])
-    negative = np.block([[cosine, sine], [-sine, cosine]])
-    return positive, negative
+    both = np.stack([np.cos(angles) * scale, np.sin(angles) * scale])
+    return both.astype(ml_dtypes.bfloat16).astype(np.float32)
 
 
 def around(row, col):
@@ -69,7 +67,10 @@
     ]
 
 
-def exchange_object(obj, wide, held, low_v, low_h, got_v, got_h, got_c, load, send, recv):
+def exchange_object(
+    obj, patterns, waves, wide, held, amplitudes, tables, canvas,
+    low_v, low_h, got_v, got_h, got_c, held_waves, load, send, recv,
+):
     row, col = lax.axis_index("row"), lax.axis_index("col")
     order = (0, PANELS - 1) + tuple(range(1, PANELS - 1))
     loads = [
@@ -78,6 +79,12 @@
     ]
     for k in order:
         loads[k].start()
+    fetches = [
+        pltpu.make_async_copy(patterns, amplitudes, load.at[PANELS]),
+        pltpu.make_async_copy(waves, held_waves, load.at[PANELS + 1]),
+    ]
+    for fetch in fetches:
+        fetch.start()
     barrier = greet(around(row, col))
     rims = rim_copies(
         [low_v.at[0], low_v.at[1], low_h.at[0], low_h.at[1]]
@@ -116,6 +123,24 @@
     def keep(i, value):
         return jnp.where(have[i], value.astype(F32), 0.0)
 
+    @pl.loop(0, EXT // 32)
+    def _(i):
+        rows = pl.ds(pl.multiple_of(i * 32, 32), 32)
+        for p in range(2):
+            for k in range(PANELS + 2):
+                canvas[p, k, rows, :] = jnp.zeros((32, LANES), F32)
+
+    for fetch in fetches:
+        fetch.wait()
+    real, imag = slice(0, SIZE), slice(SIZE, 2 * SIZE)
+    cosine, sine = held_waves[0].astype(BF16), held_waves[1].astype(BF16)
+    minus = (-held_waves[1]).astype(BF16)
+    for t in range(2):
+        tables[t, real, real] = cosine
+        tables[t, imag, imag] = cosine
+        tables[t, real, imag] = sine if t else minus
+        tables[t, imag, real] = minus if t else sine
+
     for i in (0, 1, 4, 5, 6, 7, 2, 3):
         rims[i].wait()
     for p in range(2):
@@ -135,15 +160,8 @@
             wide[p, PANELS + 1, to, :] = keep(3, got_h[1, p, rows, :])
 
 
-def process_slots(counts, centers, wide, probe, patterns, positive, negative, units, canvas, low, sums, patch, wave, half, shift, back):
+def process_slots(counts, centers, wide, probe, patterns, tables, blank, units, canvas, low, sums, patch, wave, half, shift, back):
     row_id, col_id = lax.axis_index("row"), lax.axis_index("col")
-
-    @pl.loop(0, EXT // 32)
-    def _(i):
-        rows = pl.ds(pl.multiple_of(i * 32, 32), 32)
-        for p in range(2):
-            for k in range(PANELS + 2):
-                canvas[p, k, rows, :] = jnp.zeros((32, LANES), F32)
 
     low[...] = probe[...].astype(BF16).astype(F32)
     sums[...] = jnp.zeros_like(sums)
@@ -169,15 +187,15 @@
             wave[m, :, real] = (low[m, 0] * field[0] - low[m, 1] * field[1]).astype(BF16)
             wave[m, :, imag] = (low[m, 0] * field[1] + low[m, 1] * field[0]).astype(BF16)
         for m in range(MODES):
-            product = jnp.dot(wave[m], positive[...], preferred_element_type=F32)
+            product = jnp.dot(wave[m], tables[0], preferred_element_type=F32)
             half[m, real, :] = product[:, real].astype(BF16)
             half[m, imag, :] = product[:, imag].astype(BF16)
         spectra = []
         for m in range(MODES):
             spectra.append(
                 (
-                    jnp.dot(negative[real, :], half[m], preferred_element_type=F32),
-                    jnp.dot(negative[imag, :], half[m], preferred_element_type=F32),
+                    jnp.dot(tables[1, real, :], half[m], preferred_element_type=F32),
+                    jnp.dot(tables[1, imag, :], half[m], preferred_element_type=F32),
                 )
             )
         power = (
@@ -191,13 +209,13 @@
             shift[m, :, real] = (factor * spectra[m][0]).astype(BF16)
             shift[m, :, imag] = (factor * spectra[m][1]).astype(BF16)
         for m in range(MODES):
-            product = jnp.dot(shift[m], negative[...], preferred_element_type=F32)
+            product = jnp.dot(shift[m], tables[1], preferred_element_type=F32)
             back[m, real, :] = product[:, real].astype(BF16)
             back[m, imag, :] = product[:, imag].astype(BF16)
         terms = [0.0, 0.0]
         for m in range(MODES):
-            change_real = jnp.dot(positive[real, :], back[m], preferred_element_type=F32)
-            change_imag = jnp.dot(positive[imag, :], back[m], preferred_element_type=F32)
+            change_real = jnp.dot(tables[0, real, :], back[m], preferred_element_type=F32)
+            change_imag = jnp.dot(tables[0, imag, :], back[m], preferred_element_type=F32)
             terms[0] = terms[0] + low[m, 0] * change_real + low[m, 1] * change_imag
             terms[1] = terms[1] + low[m, 0] * change_imag - low[m, 1] * change_real
             sums[2 * m] += patch[0] * change_real + patch[1] * change_imag
@@ -369,12 +387,9 @@
 
 
 def on_device(object_field, probe_modes, counts, centers, patterns):
-    positive, negative = dft_tables()
+    waves = pltpu.with_memory_space_constraint(jnp.asarray(dft_tables()), pltpu.HBM)
     dma = pltpu.SemaphoreType.DMA
     probe = pltpu.with_memory_space_constraint(probe_modes, pltpu.VMEM)
-    amplitudes = pltpu.with_memory_space_constraint(patterns[0, 0], pltpu.VMEM)
-    positive = pltpu.with_memory_space_constraint(jnp.asarray(positive), pltpu.VMEM)
-    negative = pltpu.with_memory_space_constraint(jnp.asarray(negative), pltpu.VMEM)
     strips = [
         pltpu.VMEM((2, 2, PANELS, HALF, LANES), BF16),
         pltpu.VMEM((2, 2, TILE, LANES), BF16),
@@ -384,20 +399,31 @@
     def inner(*arrays):
         return [pltpu.with_memory_space_constraint(a, pltpu.VMEM) for a in arrays]
 
-    wide, held = pl.pallas_call(
+    extended = pltpu.VMEM((2, PANELS + 2, EXT, LANES), F32)
+    wide, held, amplitudes, tables, canvas = pl.pallas_call(
         exchange_object,
-        out_shape=[pltpu.VMEM((2, PANELS + 2, EXT, LANES), F32), pltpu.VMEM((2, PANELS, TILE, LANES), F32)],
-        in_specs=[ANY],
-        out_specs=[VMEM, VMEM],
-        scratch_shapes=strips[:2] + strips + [dma((PANELS,)), dma((8,)), dma((8,))],
-        compiler_params=pltpu.CompilerParams(collective_id=0, has_side_effects=True, vmem_limit_bytes=LIMIT),
+        out_shape=[
+            extended,
+            pltpu.VMEM((2, PANELS, TILE, LANES), F32),
+            pltpu.VMEM(patterns.shape[2:], BF16),
+            pltpu.VMEM((2, 2 * SIZE, 2 * SIZE), BF16),
+            extended,
+        ],
+        in_specs=[HBM] * 3,
+        out_specs=[VMEM] * 5,
+        scratch_shapes=strips[:2] + strips + [pltpu.VMEM((2, SIZE, SIZE), F32), dma((PANELS + 2,)), dma((8,)), dma((8,))],
+        compiler_params=pltpu.CompilerParams(collective_id=0, has_side_effects=True, vmem_limit_bytes=16 * MIB),
         name="exchange_object",
-    )(object_field)
-    wide, held = inner(wide, held)
+    )(
+        pltpu.with_memory_space_constraint(object_field, pltpu.HBM),
+        pltpu.with_memory_space_constraint(patterns[0, 0], pltpu.HBM),
+        waves,
+    )
+    wide, held, amplitudes, tables, canvas = inner(wide, held, amplitudes, tables, canvas)
     units, canvas = pl.pallas_call(
         process_slots,
-        out_shape=[pltpu.VMEM((UNITS, PLANES + 1, 4, LANES), F32), pltpu.VMEM((2, PANELS + 2, EXT, LANES), F32)],
-        in_specs=[SMEM, SMEM, VMEM, VMEM, VMEM, VMEM, VMEM],
+        out_shape=[pltpu.VMEM((UNITS, PLANES + 1, 4, LANES), F32), extended],
+        in_specs=[SMEM, SMEM] + [VMEM] * 5,
         out_specs=[VMEM, VMEM],
         scratch_shapes=[
             pltpu.VMEM((MODES, 2, SIZE, SIZE), F32),
@@ -408,9 +434,10 @@
             pltpu.VMEM((MODES, SIZE, 2 * SIZE), BF16),
             pltpu.VMEM((MODES, 2 * SIZE, SIZE), BF16),
         ],
-        compiler_params=pltpu.CompilerParams(vmem_limit_bytes=LIMIT),
+        input_output_aliases={6: 1},
+        compiler_params=pltpu.CompilerParams(vmem_limit_bytes=24 * MIB),
         name="process_slots",
-    )(counts, centers[0, 0], wide, probe, amplitudes, positive, negative)
+    )(counts, centers[0, 0], wide, probe, amplitudes, tables, canvas)
     units, canvas = inner(units, canvas)
     got_v, got_h, got_c, update, peak = pl.pallas_call(
         exchange_sums,
@@ -426,7 +453,7 @@
             pltpu.VMEM((N_COL - 1, PLANES + 1, 4, LANES), F32),
             dma((8,)), dma((8,)), dma((2,)), dma((2,)), dma((6,)), dma((6,)), dma((2 * N_COL - 2,)), dma((2 * N_COL - 2,)),
         ],
-        compiler_params=pltpu.CompilerParams(collective_id=1, has_side_effects=True, vmem_limit_bytes=LIMIT),
+        compiler_params=pltpu.CompilerParams(collective_id=1, has_side_effects=True, vmem_limit_bytes=16 * MIB),
         name="exchange_sums",
     )(canvas, units, probe)
     new_object, new_probe = pl.pallas_call(
@@ -438,7 +465,7 @@
         in_specs=[VMEM] * 8,
         out_specs=[ANY, VMEM],
         scratch_shapes=[pltpu.VMEM((2, PANELS, TILE, LANES), F32), dma((PANELS,))],
-        compiler_params=pltpu.CompilerParams(vmem_limit_bytes=LIMIT),
+        compiler_params=pltpu.CompilerParams(vmem_limit_bytes=12 * MIB),
         name="write_results",
     )(*inner(canvas, held, got_v, got_h, got_c, update, peak), probe)
     return new_object, new_probe

time: 91.1 us -> 84.9 us (0.932)
  local copies, waits for them, and re-layouts: 5.64 us -> 0.01 us
    unnamed x18 -> x6, local copies, waits for them, and re-layouts: 5.64 us -> 0.01 us
    pallas_call x1, Pallas kernels: 7.24 us -> 4.66 us  [on_device(): pl.pallas_call(process_slots, out_shape=[pltpu.VMEM((UNITS, PLANES + 1, 4...]
    pallas_call x1, Pallas kernels: 52.1 us -> 54.2 us  [on_device(): pl.pallas_call(exchange_sums, out_shape=strips + [pltpu.VMEM((UNITS, 16,...]
where the time goes in v2:
time: 84.9 us; the launch traced here: 84.8 us
  Pallas kernels  84.1 us (99%)
    pallas_call x1, Pallas kernels, on_device(): pl.pallas_call(exchange_sums, out_shape=strips + [pltpu.VMEM((UNITS, 16,...  54.2 us
    pallas_call x1, Pallas kernels, on_device(): pl.pallas_call(exchange_object, out_shape=[extended, pltpu.VMEM((2, PANEL...  21.8 us
    pallas_call x1, Pallas kernels, on_device(): pl.pallas_call(process_slots, out_shape=[pltpu.VMEM((UNITS, PLANES + 1, 4...  4.66 us
    pallas_call x1, Pallas kernels, on_device(): pl.pallas_call(write_results, out_shape=[jax.ShapeDtypeStruct(object_fiel...  3.41 us

profile of v2, /device:TPU:1, one launch (start us, length us, event | category | flops | bytes accessed | tf_op | source)
XLA Modules:
  0.0 84.8 jit_solution(5436138193271846862)
XLA Ops:
  0.6 0.0 copy-start
  0.6 0.0 copy-start.2
  0.7 0.0 copy-start.1
  0.7 21.8 %exchange_object.1 = (f32[2,8,1024,128]{3,2,1,0:T(8,128)S(1)}, f32[2,6,768,128]{3,2,1,0:T(8,128)S(1)}, bf16[12,256,256]{2,1,0:T(8,128)(2,1)S(1)}, bf16[2,512,512...) custom-call(f32[2,768,768]{2,1,0:T(8,128)} %obj.1, bf16[12,256,256]{2,1,0:T(8,128)(2,1)} %bitcast.3, ...), custom_call_target="tpu_custom_call" | custom-call | tf_op jit(solution)/shard_map/exchange_object/pallas_call | solution.py:403
  22.5 0.0 copy-done
  22.5 0.0 copy-done.2
  22.5 0.0 copy-done.1
  22.5 4.7 %process_slots.1 = (f32[128,5,4,128]{3,2,1,0:T(4,128)S(1)}, f32[2,8,1024,128]{3,2,1,0:T(8,128)S(1)}) custom-call(s32[8,16]{1,0:T(8,128)S(1)} %copy-done.1, s32[2,12]{1,0:T(2,128)S(1)} %bitcast.2, f32[2,8,1024,128]{3,2,1,0:T(8,128)S(1)} %get-tuple-element.14.wide, f32[2,2,256,256]{3,2,1,0:T(8,128)S(1)} %copy-done, ...), custom_call_target="tpu_custom_call", output_to_operand_aliasing={{1}: (6, {})} | custom-call | tf_op jit(solution)/shard_map/process_slots/pallas_call | solution.py:423
  27.2 54.2 %exchange_sums.1 = (bf16[2,2,6,128,128]{4,3,2,1,0:T(8,128)(2,1)S(1)}, bf16[2,2,768,128]{3,2,1,0:T(8,128)(2,1)S(1)}, bf16[4,2,128,128]{3,2,1,0:T(8,128)(2,1)S(1)}...) custom-call(f32[2,8,1024,128]{3,2,1,0:T(8,128)S(1)} %get-tuple-element.18.canvas, ...), custom_call_target="tpu_custom_call" | custom-call | tf_op jit(solution)/shard_map/exchange_sums/pallas_call | solution.py:442
  81.4 3.4 %write_results.1 = (f32[2,768,768]{2,1,0:T(8,128)}, f32[2,2,256,256]{3,2,1,0:T(8,128)}) custom-call(f32[2,8,1024,128]{3,2,1,0:T(8,128)S(1)} %get-tuple-element.18.canvas, f32[2,6,768,128]{3,2,1,0:T(8,128)S(1)} %get-tuple-element.19.held, bf16[2,2,6,128,128]{4,3,2,1,0:T(8,128)(2,1)S(1)} %get-tuple-element.21.got_v, ...), custom_call_target="tpu_custom_call" | custom-call | tf_op jit(solution)/shard_map/write_results/pallas_call | solution.py:459
Async XLA Ops:
  0.6 21.8 %copy-start = (f32[2,2,256,256]{3,2,1,0:T(8,128)S(1)}, f32[2,2,256,256]{3,2,1,0:T(8,128)}, u32[]{:S(2)}) copy-start(f32[2,2,256,256]{3,2,1,0:T(8,128)} %probe.5) | copy-start | bytes 3145732
  0.6 21.8 %copy-start.2 = (s32[1,1,2,12]{3,2,1,0:T(2,128)S(1)}, s32[1,1,2,12]{3,2,1,0:T(2,128)}, u32[]{:S(2)}) copy-start(s32[1,1,2,12]{3,2,1,0:T(2,128)} %param.9) | copy-start | bytes 292
  0.7 21.8 %copy-start.1 = (s32[8,16]{1,0:T(8,128)S(1)}, s32[8,16]{1,0:T(8,128)}, u32[]{:S(2)}) copy-start(s32[8,16]{1,0:T(8,128)} %counts.1) | copy-start | bytes 1540

commit v3 on v2

--- a/solution.py
+++ b/solution.py
@@ -19,6 +19,8 @@
 PLANES = 2 * MODES
 N_ROW, N_COL = 8, 16
 UNITS = 128
+UNIT_ROWS = 24
+BATCH = 2
 VMEM = pl.BlockSpec(memory_space=pltpu.VMEM)
 SMEM = pl.BlockSpec(memory_space=pltpu.SMEM)
 HBM = pl.BlockSpec(memory_space=pltpu.HBM)
@@ -160,99 +162,129 @@
             wide[p, PANELS + 1, to, :] = keep(3, got_h[1, p, rows, :])
 
 
-def process_slots(counts, centers, wide, probe, patterns, tables, blank, units, canvas, low, sums, patch, wave, half, shift, back):
-    row_id, col_id = lax.axis_index("row"), lax.axis_index("col")
-
-    low[...] = probe[...].astype(BF16).astype(F32)
-    sums[...] = jnp.zeros_like(sums)
+def transform_slots(slots, low, wide, patterns, tables, sums, patch, wave, half, shift, back):
     lane = lax.broadcasted_iota(jnp.int32, (SIZE, LANES), 1)
     real, imag = slice(0, SIZE), slice(SIZE, 2 * SIZE)
-
-    @pl.loop(0, counts[row_id, col_id])
-    def _(s):
-        row, col = centers[0, s], centers[1, s]
+    covered = 0.0
+    for b, (row, col, s, weight) in enumerate(slots):
         panel = col // LANES
         turn = col - panel * LANES
         rows = pl.ds(row, SIZE)
         field = []
         for p in range(2):
             parts = [pltpu.roll(wide[p, panel + k, rows, :], lax.rem(LANES - turn, LANES), 1) for k in range(3)]
-            whole = jnp.concatenate(
-                [jnp.where(lane < LANES - turn, parts[k], parts[k + 1]) for k in range(2)], 1
-            )
-            patch[p] = whole
+            whole = jnp.concatenate([jnp.where(lane < LANES - turn, parts[k], parts[k + 1]) for k in range(2)], 1)
+            patch[b, p] = whole
             field.append(whole)
-        sums[PLANES] += field[0] * field[0] + field[1] * field[1]
+        covered = covered + weight * (field[0] * field[0] + field[1] * field[1])
         for m in range(MODES):
-            wave[m, :, real] = (low[m, 0] * field[0] - low[m, 1] * field[1]).astype(BF16)
-            wave[m, :, imag] = (low[m, 0] * field[1] + low[m, 1] * field[0]).astype(BF16)
+            wave[b, m, :, real] = (low[m, 0] * field[0] - low[m, 1] * field[1]).astype(BF16)
+            wave[b, m, :, imag] = (low[m, 0] * field[1] + low[m, 1] * field[0]).astype(BF16)
+    sums[PLANES] += covered
+    for b in range(len(slots)):
         for m in range(MODES):
-            product = jnp.dot(wave[m], tables[0], preferred_element_type=F32)
-            half[m, real, :] = product[:, real].astype(BF16)
-            half[m, imag, :] = product[:, imag].astype(BF16)
-        spectra = []
-        for m in range(MODES):
-            spectra.append(
-                (
-                    jnp.dot(tables[1, real, :], half[m], preferred_element_type=F32),
-                    jnp.dot(tables[1, imag, :], half[m], preferred_element_type=F32),
-                )
-            )
+            product = jnp.dot(wave[b, m], tables[0], preferred_element_type=F32)
+            half[b, m, real, :] = product[:, real].astype(BF16)
+            half[b, m, imag, :] = product[:, imag].astype(BF16)
+    for b, (_, _, s, weight) in enumerate(slots):
+        spectra = [
+            [jnp.dot(tables[1, part, :], half[b, m], preferred_element_type=F32) for part in (real, imag)]
+            for m in range(MODES)
+        ]
         power = (
             spectra[0][0] * spectra[0][0]
             + spectra[0][1] * spectra[0][1]
             + spectra[1][0] * spectra[1][0]
             + spectra[1][1] * spectra[1][1]
         )
-        factor = patterns[s].astype(F32) * lax.rsqrt(jnp.maximum(power, 0.5)) - 1.0
+        factor = weight * (patterns[s].astype(F32) * lax.rsqrt(jnp.maximum(power, 0.5)) - 1.0)
         for m in range(MODES):
-            shift[m, :, real] = (factor * spectra[m][0]).astype(BF16)
-            shift[m, :, imag] = (factor * spectra[m][1]).astype(BF16)
+            shift[b, m, :, real] = (factor * spectra[m][0]).astype(BF16)
+            shift[b, m, :, imag] = (factor * spectra[m][1]).astype(BF16)
+    for b in range(len(slots)):
         for m in range(MODES):
-            product = jnp.dot(shift[m], tables[1], preferred_element_type=F32)
-            back[m, real, :] = product[:, real].astype(BF16)
-            back[m, imag, :] = product[:, imag].astype(BF16)
-        terms = [0.0, 0.0]
-        for m in range(MODES):
-            change_real = jnp.dot(tables[0, real, :], back[m], preferred_element_type=F32)
-            change_imag = jnp.dot(tables[0, imag, :], back[m], preferred_element_type=F32)
-            terms[0] = terms[0] + low[m, 0] * change_real + low[m, 1] * change_imag
-            terms[1] = terms[1] + low[m, 0] * change_imag - low[m, 1] * change_real
-            sums[2 * m] += patch[0] * change_real + patch[1] * change_imag
-            sums[2 * m + 1] += patch[0] * change_imag - patch[1] * change_real
-        for p in range(2):
-            term = terms[p].astype(BF16).astype(F32)
-            first = pltpu.roll(term[:, :LANES], turn, 1)
-            second = pltpu.roll(term[:, LANES:], turn, 1)
-            canvas[p, panel, rows, :] += jnp.where(lane < turn, 0.0, first)
-            canvas[p, panel + 1, rows, :] += jnp.where(lane < turn, first, second)
-            canvas[p, panel + 2, rows, :] += jnp.where(lane < turn, second, 0.0)
-
-    @pl.loop(0, SIZE // 8)
+            product = jnp.dot(shift[b, m], tables[1], preferred_element_type=F32)
+            back[b, m, real, :] = product[:, real].astype(BF16)
+            back[b, m, imag, :] = product[:, imag].astype(BF16)
+    terms = [[0.0, 0.0] for _ in slots]
+    for m in range(MODES):
+        gained = [0.0, 0.0]
+        for b in range(len(slots)):
+            change_real = jnp.dot(tables[0, real, :], back[b, m], preferred_element_type=F32)
+            change_imag = jnp.dot(tables[0, imag, :], back[b, m], preferred_element_type=F32)
+            terms[b][0] = terms[b][0] + low[m, 0] * change_real + low[m, 1] * change_imag
+            terms[b][1] = terms[b][1] + low[m, 0] * change_imag - low[m, 1] * change_real
+            gained[0] = gained[0] + patch[b, 0] * change_real + patch[b, 1] * change_imag
+            gained[1] = gained[1] + patch[b, 0] * change_imag - patch[b, 1] * change_real
+        sums[2 * m] += gained[0]
+        sums[2 * m + 1] += gained[1]
+    return terms
+
+
+def place_term(canvas, row, col, term):
+    lane = lax.broadcasted_iota(jnp.int32, (SIZE, LANES), 1)
+    panel = col // LANES
+    turn = col - panel * LANES
+    rows = pl.ds(row, SIZE)
+    for p in range(2):
+        rounded = term[p].astype(BF16).astype(F32)
+        first = pltpu.roll(rounded[:, :LANES], turn, 1)
+        second = pltpu.roll(rounded[:, LANES:], turn, 1)
+        canvas[p, panel, rows, :] += jnp.where(lane < turn, 0.0, first)
+        canvas[p, panel + 1, rows, :] += jnp.where(lane < turn, first, second)
+        canvas[p, panel + 2, rows, :] += jnp.where(lane < turn, second, 0.0)
+
+
+def process_slots(counts, centers, wide, probe, patterns, tables, blank, units, canvas, low, sums, patch, wave, half, shift, back):
+    count = counts[lax.axis_index("row"), lax.axis_index("col")]
+    low[...] = probe[...].astype(BF16).astype(F32)
+    sums[...] = jnp.zeros_like(sums)
+
+    @pl.loop(0, (count + BATCH - 1) // BATCH)
     def _(i):
+        slots = []
+        for b in range(BATCH):
+            s = jnp.minimum(BATCH * i + b, count - 1)
+            weight = jnp.where(BATCH * i + b < count, 1.0, 0.0).astype(F32)
+            slots.append((centers[0, s], centers[1, s], s, weight))
+        terms = transform_slots(slots, low, wide, patterns, tables, sums, patch, wave, half, shift, back)
+        for (row, col, _, _), term in zip(slots, terms):
+            place_term(canvas, row, col, term)
+
+    for k in range(2):
         for q in range(PLANES + 1):
-            for k in range(2):
+
+            @pl.loop(0, SIZE // 8)
+            def _(i, k=k, q=q):
                 value = sums[q, pl.ds(pl.multiple_of(i * 8, 8), 8), k * LANES : (k + 1) * LANES]
-                units[k * 64 + 2 * i, q] = value[0:4]
-                units[k * 64 + 2 * i + 1, q] = value[4:8]
+                units[k * 64 + 2 * i, 4 * q : 4 * q + 4] = value[0:4]
+                units[k * 64 + 2 * i + 1, 4 * q : 4 * q + 4] = value[4:8]
+
+    units[:, 4 * PLANES + 4 :, :] = jnp.zeros((UNITS, UNIT_ROWS - 4 * PLANES - 4, LANES), F32)
 
 
 def exchange_sums(
     canvas, units, probe, got_v, got_h, got_c, update, peak,
-    low_v, low_h, low_c, pair, half, from_x, quarter, from_col,
-    send, recv, pair_send, pair_recv, x_send, x_recv, col_send, col_recv,
+    low_v, low_h, low_c, pair, half, from_all,
+    send, recv, pair_send, pair_recv, in_send, in_recv, out_send, out_recv,
 ):
     row, col = lax.axis_index("row"), lax.axis_index("col")
-    x, core = row // 2, lax.rem(row, 2)
+    x, core, z, y = row // 2, lax.rem(row, 2), col // 4, lax.rem(col, 4)
     sibling = (row + 1 - 2 * core, col)
-    x_peers = [(lax.rem(row + 2 * j, N_ROW), col) for j in (1, 2, 3)]
-    col_peers = [(row, lax.rem(col + j, N_COL)) for j in range(1, N_COL)]
     tiles = around(row, col)
-    others = jnp.where(core == 0, tiles[0][0], tiles[1][0])
-    barrier = greet([sibling, (others, col)] + tiles[4:] + x_peers + col_peers)
-    pl.semaphore_wait(barrier, 2 + 4 + 3 + N_COL - 1)
+    other = jnp.where(core == 0, tiles[0][0], tiles[1][0])
+    along_x = [lax.rem(x + d, 4) for d in range(4)]
+    along_z = [4 * lax.rem(z + d, 4) for d in range(4)]
+    along_y = [lax.rem(y + d, 4) for d in range(4)]
+    cols = [along_z[d // 4] + along_y[d % 4] for d in range(16)]
+    peers = [((2 * along_x[j // 16] + core, cols[j % 16]), 16 * along_x[j // 16] + cols[j % 16]) for j in range(64)]
+    hops = (0, 1, 2, 1)
+    order = sorted(range(1, 64), key=lambda j: -(hops[j // 16] + hops[j // 4 % 4] + hops[j % 4]))
+    barrier = greet([sibling, (other, col)] + tiles[4:] + [peers[j][0] for j in order])
+    pl.semaphore_wait(barrier, 6 + len(order))
 
     mine = core * 64
+    me = 16 * x + col
     to_pair = remote(units.at[pl.ds(64 - mine, 64)], pair, pair_send.at[0], pair_recv.at[0], sibling)
     to_pair.start()
 
@@ -279,60 +311,42 @@
         row,
         col,
     )
-    for i in (2, 3, 4, 5, 6, 7, 0, 1):
-        rims[i].start()
     squares = probe[0, 0] * probe[0, 0] + probe[0, 1] * probe[0, 1]
     squares = squares + probe[1, 0] * probe[1, 0] + probe[1, 1] * probe[1, 1]
     peak[...] = jnp.broadcast_to(jnp.max(squares, keepdims=True) + 1e-06, peak.shape)
 
     to_pair.wait()
 
-    @pl.loop(0, 64)
-    def _(i):
-        half[i] = units[mine + i] + pair[i]
-
-    to_x = [
-        remote(half.at[pl.ds(16 * (peer[0] // 2), 16)], from_x.at[j], x_send.at[j], x_recv.at[j], peer)
-        for j, peer in enumerate(x_peers)
-    ]
-    for copy in to_x:
-        copy.start()
-    for copy in to_x:
-        copy.wait()
-
     @pl.loop(0, 16)
     def _(i):
-        quarter[i] = half[16 * x + i] + from_x[0, i] + from_x[1, i] + from_x[2, i]
-
-    to_col = [
-        remote(quarter.at[peer[1]], from_col.at[j], col_send.at[j], col_recv.at[j], peer)
-        for j, peer in enumerate(col_peers)
-    ]
-    for copy in to_col:
-        copy.start()
-    for copy in to_col:
-        copy.wait()
-    total = quarter[col]
-    for j in range(N_COL - 1):
-        total = total + from_col[j]
-    spread = lax.rsqrt(total[PLANES])
-    fresh = jnp.concatenate([total[q] * spread for q in range(PLANES)], 0).astype(BF16)
-    unit = mine + 16 * x + col
-    update[unit] = fresh
-    to_col = [
-        remote(update.at[unit], update.at[unit], col_send.at[N_COL - 1 + j], col_recv.at[N_COL - 1 + j], peer)
-        for j, peer in enumerate(col_peers)
-    ]
-    for copy in to_col:
-        copy.start()
-    for copy in to_col:
-        copy.wait()
-    block = update.at[pl.ds(mine + 16 * x, 16)]
-    to_x = [remote(block, block, x_send.at[3 + j], x_recv.at[3 + j], peer) for j, peer in enumerate(x_peers)]
-    for copy in to_x:
-        copy.start()
-    for copy in to_x:
-        copy.wait()
+        for k in range(4):
+            half[4 * i + k] = (units[mine + 4 * i + k] + pair[4 * i + k]).astype(BF16)
+
+    inward = {
+        j: remote(half.at[peers[j][1]], from_all.at[j], in_send.at[j], in_recv.at[j], peers[j][0]) for j in order
+    }
+    for j in order:
+        inward[j].start()
+    for i in (2, 3, 4, 5, 6, 7, 0, 1):
+        rims[i].start()
+    from_all[0] = half[me]
+    for j in reversed(order):
+        inward[j].wait()
+
+    def add(i, total):
+        for k in range(8):
+            total = total + from_all[8 * i + k].astype(F32)
+        return total
+
+    total = lax.fori_loop(0, 8, add, jnp.zeros((UNIT_ROWS, LANES), F32))
+    spread = lax.rsqrt(total[4 * PLANES : 4 * PLANES + 4])
+    unit = mine + me
+    update[unit] = (total[0 : 4 * PLANES] * jnp.concatenate([spread] * PLANES, 0)).astype(BF16)
+    outward = {j: remote(update.at[unit], update.at[unit], out_send.at[j], out_recv.at[j], peers[j][0]) for j in order}
+    for j in order:
+        outward[j].start()
+    for j in reversed(order):
+        outward[j].wait()
     block = update.at[pl.ds(mine, 64)]
     to_pair = remote(block, block, pair_send.at[1], pair_recv.at[1], sibling)
     to_pair.start()
@@ -422,17 +436,17 @@
     wide, held, amplitudes, tables, canvas = inner(wide, held, amplitudes, tables, canvas)
     units, canvas = pl.pallas_call(
         process_slots,
-        out_shape=[pltpu.VMEM((UNITS, PLANES + 1, 4, LANES), F32), extended],
+        out_shape=[pltpu.VMEM((UNITS, UNIT_ROWS, LANES), F32), extended],
         in_specs=[SMEM, SMEM] + [VMEM] * 5,
         out_specs=[VMEM, VMEM],
         scratch_shapes=[
             pltpu.VMEM((MODES, 2, SIZE, SIZE), F32),
             pltpu.VMEM((PLANES + 1, SIZE, SIZE), F32),
-            pltpu.VMEM((2, SIZE, SIZE), F32),
-            pltpu.VMEM((MODES, SIZE, 2 * SIZE), BF16),
-            pltpu.VMEM((MODES, 2 * SIZE, SIZE), BF16),
-            pltpu.VMEM((MODES, SIZE, 2 * SIZE), BF16),
-            pltpu.VMEM((MODES, 2 * SIZE, SIZE), BF16),
+            pltpu.VMEM((BATCH, 2, SIZE, SIZE), F32),
+            pltpu.VMEM((BATCH, MODES, SIZE, 2 * SIZE), BF16),
+            pltpu.VMEM((BATCH, MODES, 2 * SIZE, SIZE), BF16),
+            pltpu.VMEM((BATCH, MODES, SIZE, 2 * SIZE), BF16),
+            pltpu.VMEM((BATCH, MODES, 2 * SIZE, SIZE), BF16),
         ],
         input_output_aliases={6: 1},
         compiler_params=pltpu.CompilerParams(vmem_limit_bytes=24 * MIB),
@@ -446,12 +460,10 @@
         out_specs=[VMEM] * 5,
         scratch_shapes=strips
         + [
-            pltpu.VMEM((64, PLANES + 1, 4, LANES), F32),
-            pltpu.VMEM((64, PLANES + 1, 4, LANES), F32),
-            pltpu.VMEM((3, 16, PLANES + 1, 4, LANES), F32),
-            pltpu.VMEM((16, PLANES + 1, 4, LANES), F32),
-            pltpu.VMEM((N_COL - 1, PLANES + 1, 4, LANES), F32),
-            dma((8,)), dma((8,)), dma((2,)), dma((2,)), dma((6,)), dma((6,)), dma((2 * N_COL - 2,)), dma((2 * N_COL - 2,)),
+            pltpu.VMEM((64, UNIT_ROWS, LANES), F32),
+            pltpu.VMEM((64, UNIT_ROWS, LANES), BF16),
+            pltpu.VMEM((64, UNIT_ROWS, LANES), BF16),
+            dma((8,)), dma((8,)), dma((2,)), dma((2,)), dma((64,)), dma((64,)), dma((64,)), dma((64,)),
         ],
         compiler_params=pltpu.CompilerParams(collective_id=1, has_side_effects=True, vmem_limit_bytes=16 * MIB),
         name="exchange_sums",

time: 84.9 us -> 81.3 us (0.958)
  Pallas kernels: 84.1 us -> 80.4 us
    pallas_call x1, Pallas kernels: 54.2 us -> 49.2 us  [on_device(): pl.pallas_call(exchange_sums, out_shape=strips + [pltpu.VMEM((UNITS, 16,...]
    pallas_call x1, Pallas kernels: 4.66 us -> 6.01 us  [on_device(): pl.pallas_call(process_slots, out_shape=[pltpu.VMEM((UNITS, UNIT_ROWS, LA...]
where the time goes in v3:
time: 81.3 us; the launch traced here: 81.2 us
  Pallas kernels  80.4 us (99%)
    pallas_call x1, Pallas kernels, on_device(): pl.pallas_call(exchange_sums, out_shape=strips + [pltpu.VMEM((UNITS, 16,...  49.2 us
    pallas_call x1, Pallas kernels, on_device(): pl.pallas_call(exchange_object, out_shape=[extended, pltpu.VMEM((2, PANEL...  21.8 us
    pallas_call x1, Pallas kernels, on_device(): pl.pallas_call(process_slots, out_shape=[pltpu.VMEM((UNITS, UNIT_ROWS, LA...  6.01 us
    pallas_call x1, Pallas kernels, on_device(): pl.pallas_call(write_results, out_shape=[jax.ShapeDtypeStruct(object_fiel...  3.41 us

profile of v3, /device:TPU:1, one launch (start us, length us, event | category | flops | bytes accessed | tf_op | source)
XLA Modules:
  0.0 81.2 jit_solution(6107391554656615224)
XLA Ops:
  0.6 0.0 copy-start
  0.6 0.0 copy-start.2
  0.7 0.0 copy-start.1
  0.7 21.8 %exchange_object.1 = (f32[2,8,1024,128]{3,2,1,0:T(8,128)S(1)}, f32[2,6,768,128]{3,2,1,0:T(8,128)S(1)}, bf16[12,256,256]{2,1,0:T(8,128)(2,1)S(1)}, bf16[2,512,512...) custom-call(f32[2,768,768]{2,1,0:T(8,128)} %obj.1, bf16[12,256,256]{2,1,0:T(8,128)(2,1)} %bitcast.3, ...), custom_call_target="tpu_custom_call" | custom-call | tf_op jit(solution)/shard_map/exchange_object/pallas_call | solution.py:417
  22.5 0.0 copy-done
  22.5 0.0 copy-done.2
  22.5 0.0 copy-done.1
  22.5 6.0 %process_slots.1 = (f32[128,24,128]{2,1,0:T(8,128)S(1)}, f32[2,8,1024,128]{3,2,1,0:T(8,128)S(1)}) custom-call(s32[8,16]{1,0:T(8,128)S(1)} %copy-done.1, s32[2,12]{1,0:T(2,128)S(1)} %bitcast.2, f32[2,8,1024,128]{3,2,1,0:T(8,128)S(1)} %get-tuple-element.14.wide, f32[2,2,256,256]{3,2,1,0:T(8,128)S(1)} %copy-done, ...), custom_call_target="tpu_custom_call", output_to_operand_aliasing={{1}: (6, {})} | custom-call | tf_op jit(solution)/shard_map/process_slots/pallas_call | solution.py:437
  28.5 49.2 %exchange_sums.1 = (bf16[2,2,6,128,128]{4,3,2,1,0:T(8,128)(2,1)S(1)}, bf16[2,2,768,128]{3,2,1,0:T(8,128)(2,1)S(1)}, bf16[4,2,128,128]{3,2,1,0:T(8,128)(2,1)S(1)}...) custom-call(f32[2,8,1024,128]{3,2,1,0:T(8,128)S(1)} %get-tuple-element.18.canvas, ...), custom_call_target="tpu_custom_call" | custom-call | tf_op jit(solution)/shard_map/exchange_sums/pallas_call | solution.py:456
  77.7 3.4 %write_results.1 = (f32[2,768,768]{2,1,0:T(8,128)}, f32[2,2,256,256]{3,2,1,0:T(8,128)}) custom-call(f32[2,8,1024,128]{3,2,1,0:T(8,128)S(1)} %get-tuple-element.18.canvas, f32[2,6,768,128]{3,2,1,0:T(8,128)S(1)} %get-tuple-element.19.held, bf16[2,2,6,128,128]{4,3,2,1,0:T(8,128)(2,1)S(1)} %get-tuple-element.21.got_v, ...), custom_call_target="tpu_custom_call" | custom-call | tf_op jit(solution)/shard_map/write_results/pallas_call | solution.py:471
Async XLA Ops:
  0.6 21.8 %copy-start = (f32[2,2,256,256]{3,2,1,0:T(8,128)S(1)}, f32[2,2,256,256]{3,2,1,0:T(8,128)}, u32[]{:S(2)}) copy-start(f32[2,2,256,256]{3,2,1,0:T(8,128)} %probe.5) | copy-start | bytes 3145732
  0.6 21.8 %copy-start.2 = (s32[1,1,2,12]{3,2,1,0:T(2,128)S(1)}, s32[1,1,2,12]{3,2,1,0:T(2,128)}, u32[]{:S(2)}) copy-start(s32[1,1,2,12]{3,2,1,0:T(2,128)} %param.9) | copy-start | bytes 292
  0.7 21.8 %copy-start.1 = (s32[8,16]{1,0:T(8,128)S(1)}, s32[8,16]{1,0:T(8,128)}, u32[]{:S(2)}) copy-start(s32[8,16]{1,0:T(8,128)} %counts.1) | copy-start | bytes 1540

commit v4 on v3

--- a/solution.py
+++ b/solution.py
@@ -180,7 +180,8 @@
         for m in range(MODES):
             wave[b, m, :, real] = (low[m, 0] * field[0] - low[m, 1] * field[1]).astype(BF16)
             wave[b, m, :, imag] = (low[m, 0] * field[1] + low[m, 1] * field[0]).astype(BF16)
-    sums[PLANES] += covered
+    for k in range(2):
+        sums[PLANES, k] += covered[:, k * LANES : (k + 1) * LANES]
     for b in range(len(slots)):
         for m in range(MODES):
             product = jnp.dot(wave[b, m], tables[0], preferred_element_type=F32)
@@ -216,8 +217,9 @@
             terms[b][1] = terms[b][1] + low[m, 0] * change_imag - low[m, 1] * change_real
             gained[0] = gained[0] + patch[b, 0] * change_real + patch[b, 1] * change_imag
             gained[1] = gained[1] + patch[b, 0] * change_imag - patch[b, 1] * change_real
-        sums[2 * m] += gained[0]
-        sums[2 * m + 1] += gained[1]
+        for part in range(2):
+            for k in range(2):
+                sums[2 * m + part, k] += gained[part][:, k * LANES : (k + 1) * LANES]
     return terms
 
 
@@ -235,7 +237,7 @@
         canvas[p, panel + 2, rows, :] += jnp.where(lane < turn, second, 0.0)
 
 
-def process_slots(counts, centers, wide, probe, patterns, tables, blank, units, canvas, low, sums, patch, wave, half, shift, back):
+def process_slots(counts, centers, wide, probe, patterns, tables, blank, sums, canvas, low, patch, wave, half, shift, back):
     count = counts[lax.axis_index("row"), lax.axis_index("col")]
     low[...] = probe[...].astype(BF16).astype(F32)
     sums[...] = jnp.zeros_like(sums)
@@ -251,21 +253,10 @@
         for (row, col, _, _), term in zip(slots, terms):
             place_term(canvas, row, col, term)
 
-    for k in range(2):
-        for q in range(PLANES + 1):
-
-            @pl.loop(0, SIZE // 8)
-            def _(i, k=k, q=q):
-                value = sums[q, pl.ds(pl.multiple_of(i * 8, 8), 8), k * LANES : (k + 1) * LANES]
-                units[k * 64 + 2 * i, 4 * q : 4 * q + 4] = value[0:4]
-                units[k * 64 + 2 * i + 1, 4 * q : 4 * q + 4] = value[4:8]
-
-    units[:, 4 * PLANES + 4 :, :] = jnp.zeros((UNITS, UNIT_ROWS - 4 * PLANES - 4, LANES), F32)
-
 
 def exchange_sums(
-    canvas, units, probe, got_v, got_h, got_c, update, peak,
-    low_v, low_h, low_c, pair, half, from_all,
+    canvas, sums, probe, got_v, got_h, got_c, update, peak,
+    low_v, low_h, low_c, pair, half, from_plane, share, from_line,
     send, recv, pair_send, pair_recv, in_send, in_recv, out_send, out_recv,
 ):
     row, col = lax.axis_index("row"), lax.axis_index("col")
@@ -277,15 +268,16 @@
     along_z = [4 * lax.rem(z + d, 4) for d in range(4)]
     along_y = [lax.rem(y + d, 4) for d in range(4)]
     cols = [along_z[d // 4] + along_y[d % 4] for d in range(16)]
-    peers = [((2 * along_x[j // 16] + core, cols[j % 16]), 16 * along_x[j // 16] + cols[j % 16]) for j in range(64)]
+    plane = [((2 * along_x[j // 4] + core, along_z[j % 4] + y), 16 * along_x[j // 4] + along_z[j % 4]) for j in range(16)]
+    line = [((row, 4 * z + along_y[j]), along_y[j]) for j in range(4)]
     hops = (0, 1, 2, 1)
-    order = sorted(range(1, 64), key=lambda j: -(hops[j // 16] + hops[j // 4 % 4] + hops[j % 4]))
-    barrier = greet([sibling, (other, col)] + tiles[4:] + [peers[j][0] for j in order])
-    pl.semaphore_wait(barrier, 6 + len(order))
+    order = sorted(range(1, 16), key=lambda j: -(hops[j // 4] + hops[j % 4]))
+    barrier = greet([sibling, (other, col)] + tiles[2:] + [plane[j][0] for j in order] + [line[j][0] for j in (2, 1, 3)])
+    pl.semaphore_wait(barrier, 26)
 
     mine = core * 64
     me = 16 * x + col
-    to_pair = remote(units.at[pl.ds(64 - mine, 64)], pair, pair_send.at[0], pair_recv.at[0], sibling)
+    to_pair = remote(sums.at[:, 1 - core], pair, pair_send.at[0], pair_recv.at[0], sibling)
     to_pair.start()
 
     @pl.loop(0, TILE // HALF)
@@ -317,40 +309,66 @@
 
     to_pair.wait()
 
-    @pl.loop(0, 16)
-    def _(i):
-        for k in range(4):
-            half[4 * i + k] = (units[mine + 4 * i + k] + pair[4 * i + k]).astype(BF16)
-
-    inward = {
-        j: remote(half.at[peers[j][1]], from_all.at[j], in_send.at[j], in_recv.at[j], peers[j][0]) for j in order
-    }
-    for j in order:
-        inward[j].start()
+    for q in range(PLANES + 1):
+        half[q] = (sums[q, core] + pair[q]).astype(BF16)
+
+    def rows_of(block):
+        return pl.ds(pl.multiple_of(4 * block, 16), 16)
+
+    inward = [
+        remote(half.at[:, rows_of(plane[j][1])], from_plane.at[j - 1], in_send.at[j], in_recv.at[j], plane[j][0])
+        for j in order
+    ]
+    for copy in inward:
+        copy.start()
     for i in (2, 3, 4, 5, 6, 7, 0, 1):
         rims[i].start()
-    from_all[0] = half[me]
-    for j in reversed(order):
-        inward[j].wait()
-
-    def add(i, total):
-        for k in range(8):
-            total = total + from_all[8 * i + k].astype(F32)
-        return total
-
-    total = lax.fori_loop(0, 8, add, jnp.zeros((UNIT_ROWS, LANES), F32))
+    for copy in reversed(inward):
+        copy.wait()
+    parts = []
+    for q in range(PLANES + 1):
+        total = half[q, rows_of(16 * x + 4 * z), :].astype(F32)
+        for j in range(15):
+            total = total + from_plane[j, q].astype(F32)
+        parts.append(total)
+    blank = jnp.zeros((UNIT_ROWS - 4 * PLANES - 4, LANES), F32)
+    for k in range(4):
+        share[k] = jnp.concatenate([part[4 * k : 4 * k + 4] for part in parts] + [blank], 0).astype(BF16)
+    inward = [
+        remote(share.at[line[j][1]], from_line.at[j - 1], in_send.at[15 + j], in_recv.at[15 + j], line[j][0])
+        for j in (2, 1, 3)
+    ]
+    for copy in inward:
+        copy.start()
+    for copy in inward:
+        copy.wait()
+    total = share[y].astype(F32)
+    for j in range(3):
+        total = total + from_line[j].astype(F32)
     spread = lax.rsqrt(total[4 * PLANES : 4 * PLANES + 4])
     unit = mine + me
     update[unit] = (total[0 : 4 * PLANES] * jnp.concatenate([spread] * PLANES, 0)).astype(BF16)
-    outward = {j: remote(update.at[unit], update.at[unit], out_send.at[j], out_recv.at[j], peers[j][0]) for j in order}
+    outward = [
+        remote(update.at[unit], update.at[unit], out_send.at[15 + j], out_recv.at[15 + j], line[j][0]) for j in (2, 1, 3)
+    ]
+    for copy in outward:
+        copy.start()
+    for copy in outward:
+        copy.wait()
+    block = update.at[pl.ds(mine + 16 * x + 4 * z, 4)]
+    outward = {j: remote(block, block, out_send.at[j], out_recv.at[j], plane[j][0]) for j in order}
     for j in order:
         outward[j].start()
-    for j in reversed(order):
-        outward[j].wait()
-    block = update.at[pl.ds(mine, 64)]
-    to_pair = remote(block, block, pair_send.at[1], pair_recv.at[1], sibling)
-    to_pair.start()
-    to_pair.wait()
+    over = []
+    for j in [0] + order[::-1]:
+        came = 4 * ((4 - j // 4) % 4) + (4 - j % 4) % 4
+        block = update.at[pl.ds(mine + plane[came][1], 4)]
+        if j:
+            outward[j].wait()
+        over.append(remote(block, block, pair_send.at[1 + j], pair_recv.at[1 + j], sibling))
+        over[-1].start()
+    for copy in over:
+        copy.wait()
     for copy in rims:
         copy.wait()
 
@@ -434,14 +452,13 @@
         waves,
     )
     wide, held, amplitudes, tables, canvas = inner(wide, held, amplitudes, tables, canvas)
-    units, canvas = pl.pallas_call(
+    sums, canvas = pl.pallas_call(
         process_slots,
-        out_shape=[pltpu.VMEM((UNITS, UNIT_ROWS, LANES), F32), extended],
+        out_shape=[pltpu.VMEM((PLANES + 1, 2, SIZE, LANES), F32), extended],
         in_specs=[SMEM, SMEM] + [VMEM] * 5,
         out_specs=[VMEM, VMEM],
         scratch_shapes=[
             pltpu.VMEM((MODES, 2, SIZE, SIZE), F32),
-            pltpu.VMEM((PLANES + 1, SIZE, SIZE), F32),
             pltpu.VMEM((BATCH, 2, SIZE, SIZE), F32),
             pltpu.VMEM((BATCH, MODES, SIZE, 2 * SIZE), BF16),
             pltpu.VMEM((BATCH, MODES, 2 * SIZE, SIZE), BF16),
@@ -452,7 +469,7 @@
         compiler_params=pltpu.CompilerParams(vmem_limit_bytes=24 * MIB),
         name="process_slots",
     )(counts, centers[0, 0], wide, probe, amplitudes, tables, canvas)
-    units, canvas = inner(units, canvas)
+    sums, canvas = inner(sums, canvas)
     got_v, got_h, got_c, update, peak = pl.pallas_call(
         exchange_sums,
         out_shape=strips + [pltpu.VMEM((UNITS, 16, LANES), BF16), pltpu.VMEM((8, LANES), F32)],
@@ -460,14 +477,16 @@
         out_specs=[VMEM] * 5,
         scratch_shapes=strips
         + [
-            pltpu.VMEM((64, UNIT_ROWS, LANES), F32),
-            pltpu.VMEM((64, UNIT_ROWS, LANES), BF16),
-            pltpu.VMEM((64, UNIT_ROWS, LANES), BF16),
-            dma((8,)), dma((8,)), dma((2,)), dma((2,)), dma((64,)), dma((64,)), dma((64,)), dma((64,)),
+            pltpu.VMEM((PLANES + 1, SIZE, LANES), F32),
+            pltpu.VMEM((PLANES + 1, SIZE, LANES), BF16),
+            pltpu.VMEM((15, PLANES + 1, 16, LANES), BF16),
+            pltpu.VMEM((4, UNIT_ROWS, LANES), BF16),
+            pltpu.VMEM((3, UNIT_ROWS, LANES), BF16),
+            dma((8,)), dma((8,)), dma((17,)), dma((17,)), dma((19,)), dma((19,)), dma((19,)), dma((19,)),
         ],
         compiler_params=pltpu.CompilerParams(collective_id=1, has_side_effects=True, vmem_limit_bytes=16 * MIB),
         name="exchange_sums",
-    )(canvas, units, probe)
+    )(canvas, sums, probe)
     new_object, new_probe = pl.pallas_call(
         write_results,
         out_shape=[

time: 81.3 us -> 81.3 us (level)
    pallas_call x1, Pallas kernels: 49.2 us -> 51.3 us  [on_device(): pl.pallas_call(exchange_sums, out_shape=strips + [pltpu.VMEM((UNITS, 16,...]
    pallas_call x1, Pallas kernels: 6.01 us -> 3.95 us  [on_device(): pl.pallas_call(process_slots, out_shape=[pltpu.VMEM((PLANES + 1, 2, SIZE,...]
where the time goes in v4:
time: 81.3 us; the launch traced here: 81.2 us
  Pallas kernels  80.5 us (99%)
    pallas_call x1, Pallas kernels, on_device(): pl.pallas_call(exchange_sums, out_shape=strips + [pltpu.VMEM((UNITS, 16,...  51.3 us
    pallas_call x1, Pallas kernels, on_device(): pl.pallas_call(exchange_object, out_shape=[extended, pltpu.VMEM((2, PANEL...  21.8 us
    pallas_call x1, Pallas kernels, on_device(): pl.pallas_call(process_slots, out_shape=[pltpu.VMEM((PLANES + 1, 2, SIZE,...  3.95 us
    pallas_call x1, Pallas kernels, on_device(): pl.pallas_call(write_results, out_shape=[jax.ShapeDtypeStruct(object_fiel...  3.41 us

profile of v4, /device:TPU:1, one launch (start us, length us, event | category | flops | bytes accessed | tf_op | source)
XLA Modules:
  0.0 81.2 jit_solution(15720835799452201483)
XLA Ops:
  0.6 0.0 copy-start
  0.6 0.0 copy-start.2
  0.7 0.0 copy-start.1
  0.7 21.8 %exchange_object.1 = (f32[2,8,1024,128]{3,2,1,0:T(8,128)S(1)}, f32[2,6,768,128]{3,2,1,0:T(8,128)S(1)}, bf16[12,256,256]{2,1,0:T(8,128)(2,1)S(1)}, bf16[2,512,512...) custom-call(f32[2,768,768]{2,1,0:T(8,128)} %obj.1, bf16[12,256,256]{2,1,0:T(8,128)(2,1)} %bitcast.3, ...), custom_call_target="tpu_custom_call" | custom-call | tf_op jit(solution)/shard_map/exchange_object/pallas_call | solution.py:435
  22.5 0.0 copy-done
  22.5 0.0 copy-done.2
  22.5 0.0 copy-done.1
  22.5 4.0 %process_slots.1 = (f32[5,2,256,128]{3,2,1,0:T(8,128)S(1)}, f32[2,8,1024,128]{3,2,1,0:T(8,128)S(1)}) custom-call(s32[8,16]{1,0:T(8,128)S(1)} %copy-done.1, s32[2,12]{1,0:T(2,128)S(1)} %bitcast.2, f32[2,8,1024,128]{3,2,1,0:T(8,128)S(1)} %get-tuple-element.14.wide, f32[2,2,256,256]{3,2,1,0:T(8,128)S(1)} %copy-done, ...), custom_call_target="tpu_custom_call", output_to_operand_aliasing={{1}: (6, {})} | custom-call | tf_op jit(solution)/shard_map/process_slots/pallas_call | solution.py:455
  26.5 51.3 %exchange_sums.1 = (bf16[2,2,6,128,128]{4,3,2,1,0:T(8,128)(2,1)S(1)}, bf16[2,2,768,128]{3,2,1,0:T(8,128)(2,1)S(1)}, bf16[4,2,128,128]{3,2,1,0:T(8,128)(2,1)S(1)}...) custom-call(f32[2,8,1024,128]{3,2,1,0:T(8,128)S(1)} %get-tuple-element.18.canvas, ...), custom_call_target="tpu_custom_call" | custom-call | tf_op jit(solution)/shard_map/exchange_sums/pallas_call | solution.py:473
  77.8 3.4 %write_results.1 = (f32[2,768,768]{2,1,0:T(8,128)}, f32[2,2,256,256]{3,2,1,0:T(8,128)}) custom-call(f32[2,8,1024,128]{3,2,1,0:T(8,128)S(1)} %get-tuple-element.18.canvas, f32[2,6,768,128]{3,2,1,0:T(8,128)S(1)} %get-tuple-element.19.held, bf16[2,2,6,128,128]{4,3,2,1,0:T(8,128)(2,1)S(1)} %get-tuple-element.21.got_v, ...), custom_call_target="tpu_custom_call" | custom-call | tf_op jit(solution)/shard_map/write_results/pallas_call | solution.py:490
Async XLA Ops:
  0.6 21.8 %copy-start = (f32[2,2,256,256]{3,2,1,0:T(8,128)S(1)}, f32[2,2,256,256]{3,2,1,0:T(8,128)}, u32[]{:S(2)}) copy-start(f32[2,2,256,256]{3,2,1,0:T(8,128)} %probe.5) | copy-start | bytes 3145732
  0.6 21.8 %copy-start.2 = (s32[1,1,2,12]{3,2,1,0:T(2,128)S(1)}, s32[1,1,2,12]{3,2,1,0:T(2,128)}, u32[]{:S(2)}) copy-start(s32[1,1,2,12]{3,2,1,0:T(2,128)} %param.9) | copy-start | bytes 292
  0.7 21.8 %copy-start.1 = (s32[8,16]{1,0:T(8,128)S(1)}, s32[8,16]{1,0:T(8,128)}, u32[]{:S(2)}) copy-start(s32[8,16]{1,0:T(8,128)} %counts.1) | copy-start | bytes 1540

commit v5 on v4

--- a/solution.py
+++ b/solution.py
@@ -295,18 +295,31 @@
         for k in range(PANELS):
             low_v[0, p, k] = canvas[p, k + 1, 0:HALF, :].astype(BF16)
             low_v[1, p, k] = canvas[p, k + 1, EXT - HALF :, :].astype(BF16)
-    rims = rim_copies(
-        [low_v.at[0], low_v.at[1], low_h.at[0], low_h.at[1]] + [low_c.at[i] for i in range(4)],
-        [got_v.at[0], got_v.at[1], got_h.at[0], got_h.at[1]] + [got_c.at[i] for i in range(4)],
-        send,
-        recv,
-        row,
-        col,
-    )
+    opposite = (1, 0, 3, 2, 7, 6, 5, 4)
+    third, pairs = TILE // 3, PANELS // 3
+    parts = {}
+    for part in range(3):
+        some, few = slice(part * third, (part + 1) * third), slice(part * pairs, (part + 1) * pairs)
+        for i in range(2):
+            parts[i, part] = low_v.at[i, :, few], got_v.at[1 - i, :, few]
+            parts[2 + i, part] = low_h.at[i, :, some], got_h.at[1 - i, :, some]
+    for i in range(4):
+        parts[4 + i, 0] = low_c.at[i], got_c.at[3 - i]
+    places = sorted(parts)
+    rims = []
+
+    def send_rims(*chosen):
+        for i, part in chosen:
+            source, target = parts[i, part]
+            arrival = recv.at[places.index((opposite[i], part))]
+            rims.append(remote(source, target, send.at[places.index((i, part))], arrival, tiles[i]))
+            rims[-1].start()
+
     squares = probe[0, 0] * probe[0, 0] + probe[0, 1] * probe[0, 1]
     squares = squares + probe[1, 0] * probe[1, 0] + probe[1, 1] * probe[1, 1]
     peak[...] = jnp.broadcast_to(jnp.max(squares, keepdims=True) + 1e-06, peak.shape)
 
+    send_rims((2, 0), (3, 0), (0, 0), (1, 0))
     to_pair.wait()
 
     for q in range(PLANES + 1):
@@ -321,25 +334,25 @@
     ]
     for copy in inward:
         copy.start()
-    for i in (2, 3, 4, 5, 6, 7, 0, 1):
-        rims[i].start()
+    send_rims((2, 1), (3, 1), (0, 1), (1, 1))
     for copy in reversed(inward):
         copy.wait()
-    parts = []
+    pieces = []
     for q in range(PLANES + 1):
         total = half[q, rows_of(16 * x + 4 * z), :].astype(F32)
         for j in range(15):
             total = total + from_plane[j, q].astype(F32)
-        parts.append(total)
+        pieces.append(total)
     blank = jnp.zeros((UNIT_ROWS - 4 * PLANES - 4, LANES), F32)
     for k in range(4):
-        share[k] = jnp.concatenate([part[4 * k : 4 * k + 4] for part in parts] + [blank], 0).astype(BF16)
+        share[k] = jnp.concatenate([piece[4 * k : 4 * k + 4] for piece in pieces] + [blank], 0).astype(BF16)
     inward = [
         remote(share.at[line[j][1]], from_line.at[j - 1], in_send.at[15 + j], in_recv.at[15 + j], line[j][0])
         for j in (2, 1, 3)
     ]
     for copy in inward:
         copy.start()
+    send_rims((0, 2), (1, 2), (4, 0), (5, 0))
     for copy in inward:
         copy.wait()
     total = share[y].astype(F32)
@@ -353,12 +366,14 @@
     ]
     for copy in outward:
         copy.start()
+    send_rims((6, 0), (7, 0))
     for copy in outward:
         copy.wait()
     block = update.at[pl.ds(mine + 16 * x + 4 * z, 4)]
     outward = {j: remote(block, block, out_send.at[j], out_recv.at[j], plane[j][0]) for j in order}
     for j in order:
         outward[j].start()
+    send_rims((2, 2), (3, 2))
     over = []
     for j in [0] + order[::-1]:
         came = 4 * ((4 - j // 4) % 4) + (4 - j % 4) % 4
@@ -482,7 +497,7 @@
             pltpu.VMEM((15, PLANES + 1, 16, LANES), BF16),
             pltpu.VMEM((4, UNIT_ROWS, LANES), BF16),
             pltpu.VMEM((3, UNIT_ROWS, LANES), BF16),
-            dma((8,)), dma((8,)), dma((17,)), dma((17,)), dma((19,)), dma((19,)), dma((19,)), dma((19,)),
+            dma((16,)), dma((16,)), dma((17,)), dma((17,)), dma((19,)), dma((19,)), dma((19,)), dma((19,)),
         ],
         compiler_params=pltpu.CompilerParams(collective_id=1, has_side_effects=True, vmem_limit_bytes=16 * MIB),
         name="exchange_sums",

time: 81.3 us -> 78.9 us (0.970)
  Pallas kernels: 80.5 us -> 78.1 us
    pallas_call x1, Pallas kernels: 51.3 us -> 48.9 us  [on_device(): pl.pallas_call(exchange_sums, out_shape=strips + [pltpu.VMEM((UNITS, 16,...]
where the time goes in v5:
time: 78.9 us; the launch traced here: 78.8 us
  Pallas kernels  78.1 us (99%)
    pallas_call x1, Pallas kernels, on_device(): pl.pallas_call(exchange_sums, out_shape=strips + [pltpu.VMEM((UNITS, 16,...  48.9 us
    pallas_call x1, Pallas kernels, on_device(): pl.pallas_call(exchange_object, out_shape=[extended, pltpu.VMEM((2, PANEL...  21.8 us
    pallas_call x1, Pallas kernels, on_device(): pl.pallas_call(process_slots, out_shape=[pltpu.VMEM((PLANES + 1, 2, SIZE,...  3.95 us
    pallas_call x1, Pallas kernels, on_device(): pl.pallas_call(write_results, out_shape=[jax.ShapeDtypeStruct(object_fiel...  3.41 us

profile of v5, /device:TPU:1, one launch (start us, length us, event | category | flops | bytes accessed | tf_op | source)
XLA Modules:
  0.0 78.8 jit_solution(5186279530746461696)
XLA Ops:
  0.6 0.0 copy-start
  0.6 0.0 copy-start.2
  0.7 0.0 copy-start.1
  0.7 21.8 %exchange_object.1 = (f32[2,8,1024,128]{3,2,1,0:T(8,128)S(1)}, f32[2,6,768,128]{3,2,1,0:T(8,128)S(1)}, bf16[12,256,256]{2,1,0:T(8,128)(2,1)S(1)}, bf16[2,512,512...) custom-call(f32[2,768,768]{2,1,0:T(8,128)} %obj.1, bf16[12,256,256]{2,1,0:T(8,128)(2,1)} %bitcast.3, ...), custom_call_target="tpu_custom_call" | custom-call | tf_op jit(solution)/shard_map/exchange_object/pallas_call | solution.py:450
  22.5 0.0 copy-done
  22.5 0.0 copy-done.2
  22.5 0.0 copy-done.1
  22.5 4.0 %process_slots.1 = (f32[5,2,256,128]{3,2,1,0:T(8,128)S(1)}, f32[2,8,1024,128]{3,2,1,0:T(8,128)S(1)}) custom-call(s32[8,16]{1,0:T(8,128)S(1)} %copy-done.1, s32[2,12]{1,0:T(2,128)S(1)} %bitcast.2, f32[2,8,1024,128]{3,2,1,0:T(8,128)S(1)} %get-tuple-element.14.wide, f32[2,2,256,256]{3,2,1,0:T(8,128)S(1)} %copy-done, ...), custom_call_target="tpu_custom_call", output_to_operand_aliasing={{1}: (6, {})} | custom-call | tf_op jit(solution)/shard_map/process_slots/pallas_call | solution.py:470
  26.5 48.9 %exchange_sums.1 = (bf16[2,2,6,128,128]{4,3,2,1,0:T(8,128)(2,1)S(1)}, bf16[2,2,768,128]{3,2,1,0:T(8,128)(2,1)S(1)}, bf16[4,2,128,128]{3,2,1,0:T(8,128)(2,1)S(1)}...) custom-call(f32[2,8,1024,128]{3,2,1,0:T(8,128)S(1)} %get-tuple-element.18.canvas, ...), custom_call_target="tpu_custom_call" | custom-call | tf_op jit(solution)/shard_map/exchange_sums/pallas_call | solution.py:488
  75.4 3.4 %write_results.1 = (f32[2,768,768]{2,1,0:T(8,128)}, f32[2,2,256,256]{3,2,1,0:T(8,128)}) custom-call(f32[2,8,1024,128]{3,2,1,0:T(8,128)S(1)} %get-tuple-element.18.canvas, f32[2,6,768,128]{3,2,1,0:T(8,128)S(1)} %get-tuple-element.19.held, bf16[2,2,6,128,128]{4,3,2,1,0:T(8,128)(2,1)S(1)} %get-tuple-element.21.got_v, ...), custom_call_target="tpu_custom_call" | custom-call | tf_op jit(solution)/shard_map/write_results/pallas_call | solution.py:505
Async XLA Ops:
  0.6 21.8 %copy-start = (f32[2,2,256,256]{3,2,1,0:T(8,128)S(1)}, f32[2,2,256,256]{3,2,1,0:T(8,128)}, u32[]{:S(2)}) copy-start(f32[2,2,256,256]{3,2,1,0:T(8,128)} %probe.5) | copy-start | bytes 3145732
  0.6 21.8 %copy-start.2 = (s32[1,1,2,12]{3,2,1,0:T(2,128)S(1)}, s32[1,1,2,12]{3,2,1,0:T(2,128)}, u32[]{:S(2)}) copy-start(s32[1,1,2,12]{3,2,1,0:T(2,128)} %param.9) | copy-start | bytes 292
  0.7 21.8 %copy-start.1 = (s32[8,16]{1,0:T(8,128)S(1)}, s32[8,16]{1,0:T(8,128)}, u32[]{:S(2)}) copy-start(s32[8,16]{1,0:T(8,128)} %counts.1) | copy-start | bytes 1540

commit v6 on v5

--- a/solution.py
+++ b/solution.py
@@ -18,6 +18,7 @@
 MODES = 2
 PLANES = 2 * MODES
 N_ROW, N_COL = 8, 16
+SLOTS = 12
 UNITS = 128
 UNIT_ROWS = 24
 BATCH = 2
@@ -69,9 +70,36 @@
     ]
 
 
+def choose_slots(counts, centers):
+    count = counts[lax.axis_index("row"), lax.axis_index("col")]
+    picks, found, taken = [0] * 4, [0] * 4, []
+    inner_seen, calm_seen = 0, 0
+    for s in range(SLOTS):
+        row, col = centers[0, s], centers[1, s]
+        live = jnp.where(s < count, 1, 0)
+        calm = live * jnp.where(col >= HALF, 1, 0) * jnp.where(col <= TILE - HALF, 1, 0)
+        inner = calm * jnp.where(row >= HALF, 1, 0) * jnp.where(row <= TILE - HALF, 1, 0)
+        first = inner * jnp.where(inner_seen < 2, 1, 0)
+        second = (calm - first) * jnp.where(calm_seen < 2, 1, 0)
+        for i in range(2):
+            here = first * jnp.where(inner_seen == i, 1, 0)
+            picks[i], found[i] = picks[i] + s * here, found[i] + here
+            here = second * jnp.where(calm_seen == i, 1, 0)
+            picks[2 + i], found[2 + i] = picks[2 + i] + s * here, found[2 + i] + here
+        inner_seen, calm_seen = inner_seen + first, calm_seen + second
+        taken.append((live, first + second))
+    slots = []
+    for s, flag in zip(picks, found):
+        row = jnp.where(flag == 1, centers[0, s], HALF)
+        col = jnp.where(flag == 1, centers[1, s], HALF)
+        slots.append((row, col, s, jnp.where(flag == 1, 1.0, 0.0).astype(F32)))
+    return slots, taken
+
+
 def exchange_object(
-    obj, patterns, waves, wide, held, amplitudes, tables, canvas,
-    low_v, low_h, got_v, got_h, got_c, held_waves, load, send, recv,
+    all_counts, all_centers, obj, patterns, waves, probe, wide, held, amplitudes, tables, canvas, low, sums, terms,
+    low_v, low_h, got_v, got_h, got_c, held_waves, held_probe, counts, centers, patch, wave, half, shift, back,
+    load, send, recv,
 ):
     row, col = lax.axis_index("row"), lax.axis_index("col")
     order = (0, PANELS - 1) + tuple(range(1, PANELS - 1))
@@ -82,8 +110,11 @@
     for k in order:
         loads[k].start()
     fetches = [
-        pltpu.make_async_copy(patterns, amplitudes, load.at[PANELS]),
-        pltpu.make_async_copy(waves, held_waves, load.at[PANELS + 1]),
+        pltpu.make_async_copy(waves, held_waves, load.at[PANELS]),
+        pltpu.make_async_copy(probe, held_probe, load.at[PANELS + 1]),
+        pltpu.make_async_copy(patterns, amplitudes, load.at[PANELS + 2]),
+        pltpu.make_async_copy(all_counts, counts, load.at[PANELS + 3]),
+        pltpu.make_async_copy(all_centers, centers, load.at[PANELS + 4]),
     ]
     for fetch in fetches:
         fetch.start()
@@ -104,12 +135,12 @@
         def _(i, k=k):
             rows = pl.ds(pl.multiple_of(i * HALF, HALF), HALF)
             for p in range(2):
-                low = held[p, k, rows, :].astype(BF16)
-                wide[p, k + 1, pl.ds(pl.multiple_of(i * HALF + HALF, HALF), HALF), :] = low.astype(F32)
+                rounded = held[p, k, rows, :].astype(BF16)
+                wide[p, k + 1, pl.ds(pl.multiple_of(i * HALF + HALF, HALF), HALF), :] = rounded.astype(F32)
                 if k == 0:
-                    low_h[0, p, rows, :] = low
+                    low_h[0, p, rows, :] = rounded
                 if k == PANELS - 1:
-                    low_h[1, p, rows, :] = low
+                    low_h[1, p, rows, :] = rounded
 
         for p in range(2):
             low_v[0, p, k] = held[p, k, 0:HALF, :].astype(BF16)
@@ -125,13 +156,6 @@
     def keep(i, value):
         return jnp.where(have[i], value.astype(F32), 0.0)
 
-    @pl.loop(0, EXT // 32)
-    def _(i):
-        rows = pl.ds(pl.multiple_of(i * 32, 32), 32)
-        for p in range(2):
-            for k in range(PANELS + 2):
-                canvas[p, k, rows, :] = jnp.zeros((32, LANES), F32)
-
     for fetch in fetches:
         fetch.wait()
     real, imag = slice(0, SIZE), slice(SIZE, 2 * SIZE)
@@ -142,13 +166,37 @@
         tables[t, imag, imag] = cosine
         tables[t, real, imag] = sine if t else minus
         tables[t, imag, real] = minus if t else sine
-
-    for i in (0, 1, 4, 5, 6, 7, 2, 3):
+    low[...] = held_probe[...].astype(BF16).astype(F32)
+    sums[...] = jnp.zeros_like(sums)
+    slots, _ = choose_slots(counts, centers)
+
+    def run(i):
+        made = transform_slots(
+            slots[i : i + 2], low, wide, amplitudes, tables, sums, patch, wave, half, shift, back
+        )
+        for b in range(2):
+            for p in range(2):
+                terms[i + b, p] = made[b][p].astype(BF16).astype(F32)
+
+    run(0)
+    for i in (0, 1):
         rims[i].wait()
     for p in range(2):
         for k in range(PANELS):
             wide[p, k + 1, 0:HALF, :] = keep(0, got_v[0, p, k])
             wide[p, k + 1, EXT - HALF :, :] = keep(1, got_v[1, p, k])
+    run(2)
+
+    @pl.loop(0, EXT // 32)
+    def _(i):
+        rows = pl.ds(pl.multiple_of(i * 32, 32), 32)
+        for p in range(2):
+            for k in range(PANELS + 2):
+                canvas[p, k, rows, :] = jnp.zeros((32, LANES), F32)
+
+    for i in (4, 5, 6, 7, 2, 3):
+        rims[i].wait()
+    for p in range(2):
         for corner in range(4):
             rows = slice(0, HALF) if corner < 2 else slice(EXT - HALF, EXT)
             wide[p, (corner % 2) * (PANELS + 1), rows, :] = keep(4 + corner, got_c[corner, p])
@@ -237,20 +285,26 @@
         canvas[p, panel + 2, rows, :] += jnp.where(lane < turn, second, 0.0)
 
 
-def process_slots(counts, centers, wide, probe, patterns, tables, blank, sums, canvas, low, patch, wave, half, shift, back):
-    count = counts[lax.axis_index("row"), lax.axis_index("col")]
-    low[...] = probe[...].astype(BF16).astype(F32)
-    sums[...] = jnp.zeros_like(sums)
+def process_slots(
+    counts, centers, wide, low, patterns, tables, terms, blank, begun, sums, canvas, left, patch, wave, half, shift, back
+):
+    slots, taken = choose_slots(counts, centers)
+    for i, (row, col, _, _) in enumerate(slots):
+        place_term(canvas, row, col, terms[i])
+    count = 0
+    for s, (live, done) in enumerate(taken):
+        left[count] = s
+        count = count + live - done
 
     @pl.loop(0, (count + BATCH - 1) // BATCH)
     def _(i):
         slots = []
         for b in range(BATCH):
-            s = jnp.minimum(BATCH * i + b, count - 1)
+            s = left[jnp.minimum(BATCH * i + b, count - 1)]
             weight = jnp.where(BATCH * i + b < count, 1.0, 0.0).astype(F32)
             slots.append((centers[0, s], centers[1, s], s, weight))
-        terms = transform_slots(slots, low, wide, patterns, tables, sums, patch, wave, half, shift, back)
-        for (row, col, _, _), term in zip(slots, terms):
+        made = transform_slots(slots, low, wide, patterns, tables, sums, patch, wave, half, shift, back)
+        for (row, col, _, _), term in zip(slots, made):
             place_term(canvas, row, col, term)
 
 
@@ -447,7 +501,16 @@
         return [pltpu.with_memory_space_constraint(a, pltpu.VMEM) for a in arrays]
 
     extended = pltpu.VMEM((2, PANELS + 2, EXT, LANES), F32)
-    wide, held, amplitudes, tables, canvas = pl.pallas_call(
+    summed = pltpu.VMEM((PLANES + 1, 2, SIZE, LANES), F32)
+    work = [
+        pltpu.VMEM((BATCH, 2, SIZE, SIZE), F32),
+        pltpu.VMEM((BATCH, MODES, SIZE, 2 * SIZE), BF16),
+        pltpu.VMEM((BATCH, MODES, 2 * SIZE, SIZE), BF16),
+        pltpu.VMEM((BATCH, MODES, SIZE, 2 * SIZE), BF16),
+        pltpu.VMEM((BATCH, MODES, 2 * SIZE, SIZE), BF16),
+    ]
+    spots = centers[0, 0]
+    wide, held, amplitudes, tables, canvas, low, sums, terms = pl.pallas_call(
         exchange_object,
         out_shape=[
             extended,
@@ -455,35 +518,41 @@
             pltpu.VMEM(patterns.shape[2:], BF16),
             pltpu.VMEM((2, 2 * SIZE, 2 * SIZE), BF16),
             extended,
+            pltpu.VMEM(probe_modes.shape, F32),
+            summed,
+            pltpu.VMEM((4, 2, SIZE, SIZE), F32),
         ],
-        in_specs=[HBM] * 3,
-        out_specs=[VMEM] * 5,
-        scratch_shapes=strips[:2] + strips + [pltpu.VMEM((2, SIZE, SIZE), F32), dma((PANELS + 2,)), dma((8,)), dma((8,))],
-        compiler_params=pltpu.CompilerParams(collective_id=0, has_side_effects=True, vmem_limit_bytes=16 * MIB),
+        in_specs=[HBM] * 6,
+        out_specs=[VMEM] * 8,
+        scratch_shapes=strips[:2]
+        + strips
+        + [pltpu.VMEM((2, SIZE, SIZE), F32), pltpu.VMEM(probe_modes.shape, F32)]
+        + [pltpu.SMEM(counts.shape, jnp.int32), pltpu.SMEM(spots.shape, jnp.int32)]
+        + work
+        + [dma((PANELS + 5,)), dma((8,)), dma((8,))],
+        compiler_params=pltpu.CompilerParams(collective_id=0, has_side_effects=True, vmem_limit_bytes=14 * MIB),
         name="exchange_object",
     )(
+        pltpu.with_memory_space_constraint(counts, pltpu.HBM),
+        pltpu.with_memory_space_constraint(spots, pltpu.HBM),
         pltpu.with_memory_space_constraint(object_field, pltpu.HBM),
         pltpu.with_memory_space_constraint(patterns[0, 0], pltpu.HBM),
         waves,
+        pltpu.with_memory_space_constraint(probe_modes, pltpu.HBM),
     )
-    wide, held, amplitudes, tables, canvas = inner(wide, held, amplitudes, tables, canvas)
+    wide, held, amplitudes, tables, canvas, low, sums, terms = inner(
+        wide, held, amplitudes, tables, canvas, low, sums, terms
+    )
     sums, canvas = pl.pallas_call(
         process_slots,
-        out_shape=[pltpu.VMEM((PLANES + 1, 2, SIZE, LANES), F32), extended],
-        in_specs=[SMEM, SMEM] + [VMEM] * 5,
+        out_shape=[summed, extended],
+        in_specs=[SMEM, SMEM] + [VMEM] * 7,
         out_specs=[VMEM, VMEM],
-        scratch_shapes=[
-            pltpu.VMEM((MODES, 2, SIZE, SIZE), F32),
-            pltpu.VMEM((BATCH, 2, SIZE, SIZE), F32),
-            pltpu.VMEM((BATCH, MODES, SIZE, 2 * SIZE), BF16),
-            pltpu.VMEM((BATCH, MODES, 2 * SIZE, SIZE), BF16),
-            pltpu.VMEM((BATCH, MODES, SIZE, 2 * SIZE), BF16),
-            pltpu.VMEM((BATCH, MODES, 2 * SIZE, SIZE), BF16),
-        ],
-        input_output_aliases={6: 1},
-        compiler_params=pltpu.CompilerParams(vmem_limit_bytes=24 * MIB),
+        scratch_shapes=[pltpu.SMEM((SLOTS + 1,), jnp.int32)] + work,
+        input_output_aliases={7: 1, 8: 0},
+        compiler_params=pltpu.CompilerParams(vmem_limit_bytes=10 * MIB),
         name="process_slots",
-    )(counts, centers[0, 0], wide, probe, amplitudes, tables, canvas)
+    )(counts, spots, wide, low, amplitudes, tables, terms, canvas, sums)
     sums, canvas = inner(sums, canvas)
     got_v, got_h, got_c, update, peak = pl.pallas_call(
         exchange_sums,
@@ -499,7 +568,7 @@
             pltpu.VMEM((3, UNIT_ROWS, LANES), BF16),
             dma((16,)), dma((16,)), dma((17,)), dma((17,)), dma((19,)), dma((19,)), dma((19,)), dma((19,)),
         ],
-        compiler_params=pltpu.CompilerParams(collective_id=1, has_side_effects=True, vmem_limit_bytes=16 * MIB),
+        compiler_params=pltpu.CompilerParams(collective_id=1, has_side_effects=True, vmem_limit_bytes=9 * MIB),
         name="exchange_sums",
     )(canvas, sums, probe)
     new_object, new_probe = pl.pallas_call(
@@ -511,7 +580,7 @@
         in_specs=[VMEM] * 8,
         out_specs=[ANY, VMEM],
         scratch_shapes=[pltpu.VMEM((2, PANELS, TILE, LANES), F32), dma((PANELS,))],
-        compiler_params=pltpu.CompilerParams(vmem_limit_bytes=12 * MIB),
+        compiler_params=pltpu.CompilerParams(vmem_limit_bytes=8 * MIB),
         name="write_results",
     )(*inner(canvas, held, got_v, got_h, got_c, update, peak), probe)
     return new_object, new_probe

time: 78.9 us -> 73.3 us (0.929)
  Pallas kernels: 78.1 us -> 72.5 us
    pallas_call x1, Pallas kernels: 48.9 us -> 42.7 us  [on_device(): pl.pallas_call(exchange_sums, out_shape=strips + [pltpu.VMEM((UNITS, 16,...]
where the time goes in v6:
time: 73.3 us; the launch traced here: 73.2 us
  Pallas kernels  72.5 us (99%)
    pallas_call x1, Pallas kernels, on_device(): pl.pallas_call(exchange_sums, out_shape=strips + [pltpu.VMEM((UNITS, 16,...  42.7 us
    pallas_call x1, Pallas kernels, on_device(): pl.pallas_call(exchange_object, out_shape=[extended, pltpu.VMEM((2, PANEL...  21.8 us
    pallas_call x1, Pallas kernels, on_device(): pl.pallas_call(process_slots, out_shape=[summed, extended], in_specs=[SME...  4.66 us
    pallas_call x1, Pallas kernels, on_device(): pl.pallas_call(write_results, out_shape=[jax.ShapeDtypeStruct(object_fiel...  3.4 us

profile of v6, /device:TPU:1, one launch (start us, length us, event | category | flops | bytes accessed | tf_op | source)
XLA Modules:
  0.0 73.2 jit_solution(6099875411169696852)
XLA Ops:
  0.6 0.0 copy-start.1
  0.6 0.0 copy-start.2
  0.7 21.8 %exchange_object.1 = (f32[2,8,1024,128]{3,2,1,0:T(8,128)S(1)}, f32[2,6,768,128]{3,2,1,0:T(8,128)S(1)}, bf16[12,256,256]{2,1,0:T(8,128)(2,1)S(1)}, bf16[2,512,512...) custom-call(s32[8,16]{1,0:T(8,128)} %counts.1, ...), custom_call_target="tpu_custom_call" | custom-call | tf_op jit(solution)/shard_map/exchange_object/pallas_call | solution.py:513
  22.4 0.0 copy-done.1
  22.4 0.0 copy-done.2
  22.4 0.0 copy-start
  22.4 4.7 %process_slots.1 = (f32[5,2,256,128]{3,2,1,0:T(8,128)S(1)}, f32[2,8,1024,128]{3,2,1,0:T(8,128)S(1)}) custom-call(s32[8,16]{1,0:T(8,128)S(1)} %copy-done.1, s32[2,12]{1,0:T(2,128)S(1)} %bitcast.3, f32[2,8,1024,128]{3,2,1,0:T(8,128)S(1)} %get-tuple-element.17.wide, ...), custom_call_target="tpu_custom_call", output_to_operand_aliasing={{1}: (7, {}), {0}: (8, {})} | custom-call | tf_op jit(solution)/shard_map/process_slots/pallas_call | solution.py:546
  27.1 0.0 copy-done
  27.1 42.7 %exchange_sums.1 = (bf16[2,2,6,128,128]{4,3,2,1,0:T(8,128)(2,1)S(1)}, bf16[2,2,768,128]{3,2,1,0:T(8,128)(2,1)S(1)}, bf16[4,2,128,128]{3,2,1,0:T(8,128)(2,1)S(1)}...) custom-call(f32[2,8,1024,128]{3,2,1,0:T(8,128)S(1)} %get-tuple-element.24.canvas, ...), custom_call_target="tpu_custom_call" | custom-call | tf_op jit(solution)/shard_map/exchange_sums/pallas_call | solution.py:557
  69.8 3.4 %write_results.1 = (f32[2,768,768]{2,1,0:T(8,128)}, f32[2,2,256,256]{3,2,1,0:T(8,128)}) custom-call(f32[2,8,1024,128]{3,2,1,0:T(8,128)S(1)} %get-tuple-element.24.canvas, f32[2,6,768,128]{3,2,1,0:T(8,128)S(1)} %get-tuple-element.25.held, bf16[2,2,6,128,128]{4,3,2,1,0:T(8,128)(2,1)S(1)} %get-tuple-element.27.got_v, ...), custom_call_target="tpu_custom_call" | custom-call | tf_op jit(solution)/shard_map/write_results/pallas_call | solution.py:574
Async XLA Ops:
  0.6 21.8 %copy-start.1 = (s32[8,16]{1,0:T(8,128)S(1)}, s32[8,16]{1,0:T(8,128)}, u32[]{:S(2)}) copy-start(s32[8,16]{1,0:T(8,128)} %counts.1) | copy-start | bytes 1540
  0.6 21.8 %copy-start.2 = (s32[1,1,2,12]{3,2,1,0:T(2,128)S(1)}, s32[1,1,2,12]{3,2,1,0:T(2,128)}, u32[]{:S(2)}) copy-start(s32[1,1,2,12]{3,2,1,0:T(2,128)} %param.9) | copy-start | bytes 292
  22.4 4.7 %copy-start = (f32[2,2,256,256]{3,2,1,0:T(8,128)S(1)}, f32[2,2,256,256]{3,2,1,0:T(8,128)}, u32[]{:S(2)}) copy-start(f32[2,2,256,256]{3,2,1,0:T(8,128)} %probe.5) | copy-start | bytes 3145732

commit v7 on v6

--- a/solution.py
+++ b/solution.py
@@ -19,8 +19,7 @@
 PLANES = 2 * MODES
 N_ROW, N_COL = 8, 16
 SLOTS = 12
-UNITS = 128
-UNIT_ROWS = 24
+BLOCKS = 32
 BATCH = 2
 VMEM = pl.BlockSpec(memory_space=pltpu.VMEM)
 SMEM = pl.BlockSpec(memory_space=pltpu.SMEM)
@@ -60,14 +59,6 @@
 def inside(row, col):
     up, down, left, right = row > 0, row < N_ROW - 1, col > 0, col < N_COL - 1
     return [up, down, left, right, up & left, up & right, down & left, down & right]
-
-
-def rim_copies(out, got, send, recv, row, col):
-    opposite = (1, 0, 3, 2, 7, 6, 5, 4)
-    return [
-        remote(out[i], got[opposite[i]], send.at[i], recv.at[opposite[i]], target)
-        for i, target in enumerate(around(row, col))
-    ]
 
 
 def choose_slots(counts, centers):
@@ -118,16 +109,24 @@
     ]
     for fetch in fetches:
         fetch.start()
-    barrier = greet(around(row, col))
-    rims = rim_copies(
-        [low_v.at[0], low_v.at[1], low_h.at[0], low_h.at[1]]
-        + [low_h.at[0, :, 0:HALF], low_h.at[1, :, 0:HALF], low_h.at[0, :, TILE - HALF :], low_h.at[1, :, TILE - HALF :]],
-        [got_v.at[0], got_v.at[1], got_h.at[0], got_h.at[1]] + [got_c.at[i] for i in range(4)],
-        send,
-        recv,
-        row,
-        col,
-    )
+    tiles = around(row, col)
+    barrier = greet(tiles[:4])
+    ends = (slice(0, HALF), slice(TILE - HALF, TILE), slice(HALF, TILE - HALF))
+    upright = [
+        remote(low_v.at[i], got_v.at[1 - i], send.at[i], recv.at[1 - i], tiles[i]) for i in range(2)
+    ]
+    sides = [
+        remote(
+            low_h.at[i, :, ends[part]], got_h.at[1 - i, :, ends[part]],
+            send.at[2 + 3 * i + part], recv.at[5 - 3 * i + part], tiles[2 + i],
+        )
+        for part in range(3)
+        for i in range(2)
+    ]
+    corners = [
+        remote(got_h.at[c % 2, :, ends[1 - c // 2]], got_c.at[c], send.at[8 + c], recv.at[8 + c], tiles[1 - c // 2])
+        for c in range(4)
+    ]
     for step, k in enumerate(order):
         loads[k].wait()
 
@@ -146,11 +145,11 @@
             low_v[0, p, k] = held[p, k, 0:HALF, :].astype(BF16)
             low_v[1, p, k] = held[p, k, TILE - HALF :, :].astype(BF16)
         if step == 1:
-            pl.semaphore_wait(barrier, 8)
-            for i in (2, 3, 4, 5, 6, 7):
-                rims[i].start()
-    for i in (0, 1):
-        rims[i].start()
+            pl.semaphore_wait(barrier, 4)
+            for copy in sides:
+                copy.start()
+    for copy in upright:
+        copy.start()
     have = inside(row, col)
 
     def keep(i, value):
@@ -179,8 +178,12 @@
                 terms[i + b, p] = made[b][p].astype(BF16).astype(F32)
 
     run(0)
-    for i in (0, 1):
-        rims[i].wait()
+    for copy in sides[:4]:
+        copy.wait()
+    for copy in corners:
+        copy.start()
+    for copy in upright:
+        copy.wait()
     for p in range(2):
         for k in range(PANELS):
             wide[p, k + 1, 0:HALF, :] = keep(0, got_v[0, p, k])
@@ -194,8 +197,8 @@
             for k in range(PANELS + 2):
                 canvas[p, k, rows, :] = jnp.zeros((32, LANES), F32)
 
-    for i in (4, 5, 6, 7, 2, 3):
-        rims[i].wait()
+    for copy in corners + sides[4:]:
+        copy.wait()
     for p in range(2):
         for corner in range(4):
             rows = slice(0, HALF) if corner < 2 else slice(EXT - HALF, EXT)
@@ -310,7 +313,7 @@
 
 def exchange_sums(
     canvas, sums, probe, got_v, got_h, got_c, update, peak,
-    low_v, low_h, low_c, pair, half, from_plane, share, from_line,
+    low_v, low_h, low_c, pair, half, from_plane, lines,
     send, recv, pair_send, pair_recv, in_send, in_recv, out_send, out_recv,
 ):
     row, col = lax.axis_index("row"), lax.axis_index("col")
@@ -322,15 +325,14 @@
     along_z = [4 * lax.rem(z + d, 4) for d in range(4)]
     along_y = [lax.rem(y + d, 4) for d in range(4)]
     cols = [along_z[d // 4] + along_y[d % 4] for d in range(16)]
-    plane = [((2 * along_x[j // 4] + core, along_z[j % 4] + y), 16 * along_x[j // 4] + along_z[j % 4]) for j in range(16)]
-    line = [((row, 4 * z + along_y[j]), along_y[j]) for j in range(4)]
+    plane = [((2 * along_x[j // 4] + core, along_z[j % 4] + y), 4 * along_x[j // 4] + along_z[j % 4] // 4) for j in range(16)]
+    line = [(row, 4 * z + along_y[j]) for j in range(4)]
     hops = (0, 1, 2, 1)
     order = sorted(range(1, 16), key=lambda j: -(hops[j // 4] + hops[j % 4]))
-    barrier = greet([sibling, (other, col)] + tiles[2:] + [plane[j][0] for j in order] + [line[j][0] for j in (2, 1, 3)])
+    barrier = greet([sibling, (other, col)] + tiles[2:] + [plane[j][0] for j in order] + [line[j] for j in (2, 1, 3)])
     pl.semaphore_wait(barrier, 26)
 
-    mine = core * 64
-    me = 16 * x + col
+    mine = 16 * core + 4 * x + z
     to_pair = remote(sums.at[:, 1 - core], pair, pair_send.at[0], pair_recv.at[0], sibling)
     to_pair.start()
 
@@ -380,7 +382,7 @@
         half[q] = (sums[q, core] + pair[q]).astype(BF16)
 
     def rows_of(block):
-        return pl.ds(pl.multiple_of(4 * block, 16), 16)
+        return pl.ds(pl.multiple_of(16 * block, 16), 16)
 
     inward = [
         remote(half.at[:, rows_of(plane[j][1])], from_plane.at[j - 1], in_send.at[j], in_recv.at[j], plane[j][0])
@@ -391,47 +393,37 @@
     send_rims((2, 1), (3, 1), (0, 1), (1, 1))
     for copy in reversed(inward):
         copy.wait()
-    pieces = []
     for q in range(PLANES + 1):
-        total = half[q, rows_of(16 * x + 4 * z), :].astype(F32)
+        total = half[q, rows_of(4 * x + z), :].astype(F32)
         for j in range(15):
             total = total + from_plane[j, q].astype(F32)
-        pieces.append(total)
-    blank = jnp.zeros((UNIT_ROWS - 4 * PLANES - 4, LANES), F32)
-    for k in range(4):
-        share[k] = jnp.concatenate([piece[4 * k : 4 * k + 4] for piece in pieces] + [blank], 0).astype(BF16)
-    inward = [
-        remote(share.at[line[j][1]], from_line.at[j - 1], in_send.at[15 + j], in_recv.at[15 + j], line[j][0])
-        for j in (2, 1, 3)
-    ]
-    for copy in inward:
+        lines[y, q] = total.astype(BF16)
+    across = [
+        remote(lines.at[y], lines.at[y], in_send.at[15 + j], in_recv.at[15 + j], line[j]) for j in (2, 1, 3)
+    ]
+    for copy in across:
         copy.start()
     send_rims((0, 2), (1, 2), (4, 0), (5, 0))
-    for copy in inward:
-        copy.wait()
-    total = share[y].astype(F32)
-    for j in range(3):
-        total = total + from_line[j].astype(F32)
-    spread = lax.rsqrt(total[4 * PLANES : 4 * PLANES + 4])
-    unit = mine + me
-    update[unit] = (total[0 : 4 * PLANES] * jnp.concatenate([spread] * PLANES, 0)).astype(BF16)
-    outward = [
-        remote(update.at[unit], update.at[unit], out_send.at[15 + j], out_recv.at[15 + j], line[j][0]) for j in (2, 1, 3)
-    ]
-    for copy in outward:
-        copy.start()
-    send_rims((6, 0), (7, 0))
-    for copy in outward:
-        copy.wait()
-    block = update.at[pl.ds(mine + 16 * x + 4 * z, 4)]
+    for copy in across:
+        copy.wait()
+    sums_here = []
+    for q in range(PLANES + 1):
+        total = lines[0, q].astype(F32)
+        for j in range(1, 4):
+            total = total + lines[j, q].astype(F32)
+        sums_here.append(total)
+    spread = lax.rsqrt(sums_here[PLANES])
+    for q in range(PLANES):
+        update[mine, q] = (sums_here[q] * spread).astype(BF16)
+    block = update.at[mine]
     outward = {j: remote(block, block, out_send.at[j], out_recv.at[j], plane[j][0]) for j in order}
     for j in order:
         outward[j].start()
-    send_rims((2, 2), (3, 2))
+    send_rims((6, 0), (7, 0), (2, 2), (3, 2))
     over = []
     for j in [0] + order[::-1]:
         came = 4 * ((4 - j // 4) % 4) + (4 - j % 4) % 4
-        block = update.at[pl.ds(mine + plane[came][1], 4)]
+        block = update.at[16 * core + plane[came][1]]
         if j:
             outward[j].wait()
         over.append(remote(block, block, pair_send.at[1 + j], pair_recv.at[1 + j], sibling))
@@ -472,16 +464,14 @@
         copy.start()
         stores.append(copy)
 
-    @pl.loop(0, SIZE // 8)
+    @pl.loop(0, SIZE // 16)
     def _(i):
-        rows = pl.ds(pl.multiple_of(i * 8, 8), 8)
+        rows = pl.ds(pl.multiple_of(i * 16, 16), 16)
         for k in range(2):
             lanes = slice(k * LANES, (k + 1) * LANES)
-            first = update[k * 64 + 2 * i].astype(F32)
-            second = update[k * 64 + 2 * i + 1].astype(F32)
             for q in range(PLANES):
-                value = jnp.concatenate([first[4 * q : 4 * q + 4], second[4 * q : 4 * q + 4]], 0)
-                new_probe[q // 2, q % 2, rows, lanes] = probe[q // 2, q % 2, rows, lanes] + value
+                gained = update[k * 16 + i, q].astype(F32)
+                new_probe[q // 2, q % 2, rows, lanes] = probe[q // 2, q % 2, rows, lanes] + gained
 
     for copy in stores:
         copy.wait()
@@ -529,7 +519,7 @@
         + [pltpu.VMEM((2, SIZE, SIZE), F32), pltpu.VMEM(probe_modes.shape, F32)]
         + [pltpu.SMEM(counts.shape, jnp.int32), pltpu.SMEM(spots.shape, jnp.int32)]
         + work
-        + [dma((PANELS + 5,)), dma((8,)), dma((8,))],
+        + [dma((PANELS + 5,)), dma((12,)), dma((12,))],
         compiler_params=pltpu.CompilerParams(collective_id=0, has_side_effects=True, vmem_limit_bytes=14 * MIB),
         name="exchange_object",
     )(
@@ -556,7 +546,7 @@
     sums, canvas = inner(sums, canvas)
     got_v, got_h, got_c, update, peak = pl.pallas_call(
         exchange_sums,
-        out_shape=strips + [pltpu.VMEM((UNITS, 16, LANES), BF16), pltpu.VMEM((8, LANES), F32)],
+        out_shape=strips + [pltpu.VMEM((BLOCKS, PLANES, 16, LANES), BF16), pltpu.VMEM((8, LANES), F32)],
         in_specs=[VMEM] * 3,
         out_specs=[VMEM] * 5,
         scratch_shapes=strips
@@ -564,9 +554,8 @@
             pltpu.VMEM((PLANES + 1, SIZE, LANES), F32),
             pltpu.VMEM((PLANES + 1, SIZE, LANES), BF16),
             pltpu.VMEM((15, PLANES + 1, 16, LANES), BF16),
-            pltpu.VMEM((4, UNIT_ROWS, LANES), BF16),
-            pltpu.VMEM((3, UNIT_ROWS, LANES), BF16),
-            dma((16,)), dma((16,)), dma((17,)), dma((17,)), dma((19,)), dma((19,)), dma((19,)), dma((19,)),
+            pltpu.VMEM((4, PLANES + 1, 16, LANES), BF16),
+            dma((16,)), dma((16,)), dma((17,)), dma((17,)), dma((19,)), dma((19,)), dma((16,)), dma((16,)),
         ],
         compiler_params=pltpu.CompilerParams(collective_id=1, has_side_effects=True, vmem_limit_bytes=9 * MIB),
         name="exchange_sums",

time: 73.3 us -> 69.9 us (0.954)
  Pallas kernels: 72.5 us -> 69.1 us
    pallas_call x1, Pallas kernels: 4.66 us -> 1.22 us  [on_device(): pl.pallas_call(process_slots, out_shape=[summed, extended], in_specs=[SME...]
    pallas_call x1, Pallas kernels: 42.7 us -> 44.6 us  [on_device(): pl.pallas_call(exchange_sums, out_shape=strips + [pltpu.VMEM((BLOCKS, PLA...]
    pallas_call x1, Pallas kernels: 21.8 us -> 19.8 us  [on_device(): pl.pallas_call(exchange_object, out_shape=[extended, pltpu.VMEM((2, PANEL...]
where the time goes in v7:
time: 69.9 us; the launch traced here: 69.8 us
  Pallas kernels  69.1 us (99%)
  between operations  0.7 us (1%)
    pallas_call x1, Pallas kernels, on_device(): pl.pallas_call(exchange_sums, out_shape=strips + [pltpu.VMEM((BLOCKS, PLA...  44.6 us
    pallas_call x1, Pallas kernels, on_device(): pl.pallas_call(exchange_object, out_shape=[extended, pltpu.VMEM((2, PANEL...  19.8 us
    pallas_call x1, Pallas kernels, on_device(): pl.pallas_call(write_results, out_shape=[jax.ShapeDtypeStruct(object_fiel...  3.4 us

profile of v7, /device:TPU:1, one launch (start us, length us, event | category | flops | bytes accessed | tf_op | source)
XLA Modules:
  0.0 69.8 jit_solution(5822473876624465870)
XLA Ops:
  0.6 0.0 copy-start.1
  0.6 0.0 copy-start.2
  0.7 19.8 %exchange_object.1 = (f32[2,8,1024,128]{3,2,1,0:T(8,128)S(1)}, f32[2,6,768,128]{3,2,1,0:T(8,128)S(1)}, bf16[12,256,256]{2,1,0:T(8,128)(2,1)S(1)}, bf16[2,512,512...) custom-call(s32[8,16]{1,0:T(8,128)} %counts.1, ...), custom_call_target="tpu_custom_call" | custom-call | tf_op jit(solution)/shard_map/exchange_object/pallas_call | solution.py:503
  20.5 0.0 copy-done.1
  20.5 0.0 copy-done.2
  20.5 0.0 copy-start
  20.5 1.2 %process_slots.1 = (f32[5,2,256,128]{3,2,1,0:T(8,128)S(1)}, f32[2,8,1024,128]{3,2,1,0:T(8,128)S(1)}) custom-call(s32[8,16]{1,0:T(8,128)S(1)} %copy-done.1, s32[2,12]{1,0:T(2,128)S(1)} %bitcast.3, f32[2,8,1024,128]{3,2,1,0:T(8,128)S(1)} %get-tuple-element.17.wide, ...), custom_call_target="tpu_custom_call", output_to_operand_aliasing={{1}: (7, {}), {0}: (8, {})} | custom-call | tf_op jit(solution)/shard_map/process_slots/pallas_call | solution.py:536
  21.8 0.0 copy-done
  21.8 44.6 %exchange_sums.1 = (bf16[2,2,6,128,128]{4,3,2,1,0:T(8,128)(2,1)S(1)}, bf16[2,2,768,128]{3,2,1,0:T(8,128)(2,1)S(1)}, bf16[4,2,128,128]{3,2,1,0:T(8,128)(2,1)S(1)}...) custom-call(f32[2,8,1024,128]{3,2,1,0:T(8,128)S(1)} %get-tuple-element.24.canvas, ...), custom_call_target="tpu_custom_call" | custom-call | tf_op jit(solution)/shard_map/exchange_sums/pallas_call | solution.py:547
  66.4 3.4 %write_results.1 = (f32[2,768,768]{2,1,0:T(8,128)}, f32[2,2,256,256]{3,2,1,0:T(8,128)}) custom-call(f32[2,8,1024,128]{3,2,1,0:T(8,128)S(1)} %get-tuple-element.24.canvas, f32[2,6,768,128]{3,2,1,0:T(8,128)S(1)} %get-tuple-element.25.held, bf16[2,2,6,128,128]{4,3,2,1,0:T(8,128)(2,1)S(1)} %get-tuple-element.27.got_v, ...), custom_call_target="tpu_custom_call" | custom-call | tf_op jit(solution)/shard_map/write_results/pallas_call | solution.py:563
Async XLA Ops:
  0.6 19.9 %copy-start.1 = (s32[8,16]{1,0:T(8,128)S(1)}, s32[8,16]{1,0:T(8,128)}, u32[]{:S(2)}) copy-start(s32[8,16]{1,0:T(8,128)} %counts.1) | copy-start | bytes 1540
  0.6 19.9 %copy-start.2 = (s32[1,1,2,12]{3,2,1,0:T(2,128)S(1)}, s32[1,1,2,12]{3,2,1,0:T(2,128)}, u32[]{:S(2)}) copy-start(s32[1,1,2,12]{3,2,1,0:T(2,128)} %param.9) | copy-start | bytes 292
  20.5 1.2 %copy-start = (f32[2,2,256,256]{3,2,1,0:T(8,128)S(1)}, f32[2,2,256,256]{3,2,1,0:T(8,128)}, u32[]{:S(2)}) copy-start(f32[2,2,256,256]{3,2,1,0:T(8,128)} %probe.5) | copy-start | bytes 3145732

commit v8 on v7

--- a/solution.py
+++ b/solution.py
@@ -24,7 +24,6 @@
 VMEM = pl.BlockSpec(memory_space=pltpu.VMEM)
 SMEM = pl.BlockSpec(memory_space=pltpu.SMEM)
 HBM = pl.BlockSpec(memory_space=pltpu.HBM)
-ANY = pl.BlockSpec(memory_space=pl.ANY)
 MIB = 2**20
 
 
@@ -312,8 +311,8 @@
 
 
 def exchange_sums(
-    canvas, sums, probe, got_v, got_h, got_c, update, peak,
-    low_v, low_h, low_c, pair, half, from_plane, lines,
+    canvas, sums, probe, held, got_v, got_h, update, peak, ahead,
+    low_v, low_h, low_c, got_c, pair, half, from_plane, lines,
     send, recv, pair_send, pair_recv, in_send, in_recv, out_send, out_recv,
 ):
     row, col = lax.axis_index("row"), lax.axis_index("col")
@@ -329,12 +328,17 @@
     line = [(row, 4 * z + along_y[j]) for j in range(4)]
     hops = (0, 1, 2, 1)
     order = sorted(range(1, 16), key=lambda j: -(hops[j // 4] + hops[j % 4]))
-    barrier = greet([sibling, (other, col)] + tiles[2:] + [plane[j][0] for j in order] + [line[j] for j in (2, 1, 3)])
-    pl.semaphore_wait(barrier, 26)
+    barrier = greet([sibling, (other, col)] + tiles[2:4] + [plane[j][0] for j in order] + [line[j] for j in (2, 1, 3)])
+    pl.semaphore_wait(barrier, 22)
 
     mine = 16 * core + 4 * x + z
-    to_pair = remote(sums.at[:, 1 - core], pair, pair_send.at[0], pair_recv.at[0], sibling)
-    to_pair.start()
+    quarters = [pl.ds(pl.multiple_of(64 * along_x[d], 64), 64) for d in (2, 1, 3, 0)]
+    to_pair = [
+        remote(sums.at[:, 1 - core, rows], pair.at[:, rows], pair_send.at[16 + i], pair_recv.at[16 + i], sibling)
+        for i, rows in enumerate(quarters)
+    ]
+    for copy in to_pair:
+        copy.start()
 
     @pl.loop(0, TILE // HALF)
     def _(i):
@@ -360,37 +364,60 @@
             parts[i, part] = low_v.at[i, :, few], got_v.at[1 - i, :, few]
             parts[2 + i, part] = low_h.at[i, :, some], got_h.at[1 - i, :, some]
     for i in range(4):
-        parts[4 + i, 0] = low_c.at[i], got_c.at[3 - i]
+        parts[i // 2, 3 + i % 2] = low_c.at[i], got_c.at[i]
     places = sorted(parts)
     rims = []
 
     def send_rims(*chosen):
         for i, part in chosen:
             source, target = parts[i, part]
-            arrival = recv.at[places.index((opposite[i], part))]
+            arrival = recv.at[places.index((1 - i if part > 2 else opposite[i], part))]
             rims.append(remote(source, target, send.at[places.index((i, part))], arrival, tiles[i]))
             rims[-1].start()
 
     squares = probe[0, 0] * probe[0, 0] + probe[0, 1] * probe[0, 1]
     squares = squares + probe[1, 0] * probe[1, 0] + probe[1, 1] * probe[1, 1]
-    peak[...] = jnp.broadcast_to(jnp.max(squares, keepdims=True) + 1e-06, peak.shape)
-
-    send_rims((2, 0), (3, 0), (0, 0), (1, 0))
-    to_pair.wait()
-
-    for q in range(PLANES + 1):
-        half[q] = (sums[q, core] + pair[q]).astype(BF16)
+    most = jnp.max(squares, keepdims=True) + 1e-06
+    peak[...] = jnp.broadcast_to(most, peak.shape)
+
+    send_rims((0, 3), (0, 4), (1, 3), (1, 4), (2, 1), (3, 1), (0, 0), (1, 0))
 
     def rows_of(block):
         return pl.ds(pl.multiple_of(16 * block, 16), 16)
 
-    inward = [
-        remote(half.at[:, rows_of(plane[j][1])], from_plane.at[j - 1], in_send.at[j], in_recv.at[j], plane[j][0])
-        for j in order
-    ]
-    for copy in inward:
-        copy.start()
-    send_rims((2, 1), (3, 1), (0, 1), (1, 1))
+    inward = []
+    for i, d in enumerate((2, 1, 3, 0)):
+        to_pair[i].wait()
+        for q in range(PLANES + 1):
+            half[q, quarters[i], :] = (sums[q, core, quarters[i], :] + pair[q, quarters[i], :]).astype(BF16)
+        for e in (2, 1, 3, 0):
+            j = 4 * d + e
+            if j:
+                block = half.at[:, rows_of(plane[j][1])]
+                copy = remote(block, from_plane.at[j - 1], in_send.at[j], in_recv.at[j], plane[j][0])
+                copy.start()
+                inward.append(copy)
+    for copy in rims[:4]:
+        copy.wait()
+    have = inside(row, col)
+    for p in range(2):
+        for side in range(2):
+            k = side * (PANELS + 1)
+            above = jnp.where(have[0], got_c[2 + side, p].astype(F32), 0.0)
+            below = jnp.where(have[1], got_c[side, p].astype(F32), 0.0)
+            low_h[side, p, 0:HALF, :] = (canvas[p, k, HALF : 2 * HALF, :] + above).astype(BF16)
+            low_h[side, p, TILE - HALF :, :] = (canvas[p, k, TILE : TILE + HALF, :] + below).astype(BF16)
+    send_rims((2, 0), (3, 0), (0, 1), (1, 1))
+    scale = jnp.broadcast_to(1.0 / most, (1, LANES))
+
+    @pl.loop(0, TILE // HALF)
+    def _(i):
+        rows = pl.ds(pl.multiple_of(i * HALF, HALF), HALF)
+        at = pl.ds(pl.multiple_of(i * HALF + HALF, HALF), HALF)
+        for p in range(2):
+            for k in range(PANELS):
+                ahead[p, k, rows, :] = held[p, k, rows, :] + canvas[p, k + 1, at, :] * scale
+
     for copy in reversed(inward):
         copy.wait()
     for q in range(PLANES + 1):
@@ -403,7 +430,7 @@
     ]
     for copy in across:
         copy.start()
-    send_rims((0, 2), (1, 2), (4, 0), (5, 0))
+    send_rims((0, 2), (1, 2))
     for copy in across:
         copy.wait()
     sums_here = []
@@ -419,60 +446,65 @@
     outward = {j: remote(block, block, out_send.at[j], out_recv.at[j], plane[j][0]) for j in order}
     for j in order:
         outward[j].start()
-    send_rims((6, 0), (7, 0), (2, 2), (3, 2))
+    send_rims((2, 2), (3, 2))
     over = []
     for j in [0] + order[::-1]:
         came = 4 * ((4 - j // 4) % 4) + (4 - j % 4) % 4
         block = update.at[16 * core + plane[came][1]]
         if j:
             outward[j].wait()
-        over.append(remote(block, block, pair_send.at[1 + j], pair_recv.at[1 + j], sibling))
+        over.append(remote(block, block, pair_send.at[j], pair_recv.at[j], sibling))
         over[-1].start()
     for copy in over:
         copy.wait()
-    for copy in rims:
-        copy.wait()
-
-
-def write_results(canvas, held, got_v, got_h, got_c, update, peak, probe, new_object, new_probe, stage, store):
+    for copy in rims[4:]:
+        copy.wait()
+
+
+def write_results(ahead, got_v, got_h, update, peak, probe, new_object, new_probe, rows_out, sides_out, probe_out, store):
     row, col = lax.axis_index("row"), lax.axis_index("col")
     have = inside(row, col)
     scale = 1.0 / peak[0:1, :]
-
-    def keep(i, value):
-        return jnp.where(have[i], value.astype(F32), 0.0)
-
+    low_edge, high_edge = HALF, TILE - HALF
     stores = []
-    for k in range(PANELS):
-        for p in range(2):
-            side = None if k not in (0, PANELS - 1) else (0 if k == 0 else 1)
-            for i in range(TILE // HALF):
-                rows = slice(i * HALF, (i + 1) * HALF)
-                value = canvas[p, k + 1, HALF + i * HALF : 2 * HALF + i * HALF, :]
-                if i == 0:
-                    value = value + keep(0, got_v[0, p, k])
-                if i == TILE // HALF - 1:
-                    value = value + keep(1, got_v[1, p, k])
-                if side is not None:
-                    value = value + keep(2 + side, got_h[side, p, rows, :])
-                    if i == 0:
-                        value = value + keep(4 + side, got_c[side, p])
-                    if i == TILE // HALF - 1:
-                        value = value + keep(6 + side, got_c[2 + side, p])
-                stage[p, k, rows, :] = held[p, k, rows, :] + value * scale
-        copy = pltpu.make_async_copy(stage.at[:, k], new_object.at[:, :, k * LANES : (k + 1) * LANES], store.at[k])
+
+    def write(source, target):
+        copy = pltpu.make_async_copy(source, target, store.at[len(stores)])
         copy.start()
         stores.append(copy)
+
+    def lanes_of(k):
+        return slice(k * LANES, (k + 1) * LANES)
+
+    def keep(i, value):
+        return jnp.where(have[i], value.astype(F32), 0.0) * scale
+
+    for k in range(1, PANELS - 1):
+        write(ahead.at[:, k, low_edge:high_edge], new_object.at[:, low_edge:high_edge, lanes_of(k)])
+    for side, k in ((0, 0), (1, PANELS - 1)):
+        for p in range(2):
+            sides_out[side, p] = ahead[p, k, low_edge:high_edge, :] + keep(2 + side, got_h[side, p, low_edge:high_edge, :])
+        write(sides_out.at[side], new_object.at[:, low_edge:high_edge, lanes_of(k)])
+    for end, rows in ((0, slice(0, HALF)), (1, slice(high_edge, TILE))):
+        for k in range(PANELS):
+            for p in range(2):
+                value = ahead[p, k, rows, :] + keep(end, got_v[end, p, k])
+                if k == 0:
+                    value = value + keep(2, got_h[0, p, rows, :])
+                if k == PANELS - 1:
+                    value = value + keep(3, got_h[1, p, rows, :])
+                rows_out[end, p, k] = value
+            write(rows_out.at[end, :, k], new_object.at[:, rows, lanes_of(k)])
 
     @pl.loop(0, SIZE // 16)
     def _(i):
         rows = pl.ds(pl.multiple_of(i * 16, 16), 16)
         for k in range(2):
-            lanes = slice(k * LANES, (k + 1) * LANES)
             for q in range(PLANES):
                 gained = update[k * 16 + i, q].astype(F32)
-                new_probe[q // 2, q % 2, rows, lanes] = probe[q // 2, q % 2, rows, lanes] + gained
-
+                probe_out[q // 2, q % 2, rows, lanes_of(k)] = probe[q // 2, q % 2, rows, lanes_of(k)] + gained
+
+    write(probe_out, new_probe)
     for copy in stores:
         copy.wait()
 
@@ -544,34 +576,45 @@
         name="process_slots",
     )(counts, spots, wide, low, amplitudes, tables, terms, canvas, sums)
     sums, canvas = inner(sums, canvas)
-    got_v, got_h, got_c, update, peak = pl.pallas_call(
+    got_v, got_h, update, peak, ahead = pl.pallas_call(
         exchange_sums,
-        out_shape=strips + [pltpu.VMEM((BLOCKS, PLANES, 16, LANES), BF16), pltpu.VMEM((8, LANES), F32)],
-        in_specs=[VMEM] * 3,
+        out_shape=strips[:2]
+        + [
+            pltpu.VMEM((BLOCKS, PLANES, 16, LANES), BF16),
+            pltpu.VMEM((8, LANES), F32),
+            pltpu.VMEM((2, PANELS, TILE, LANES), F32),
+        ],
+        in_specs=[VMEM] * 4,
         out_specs=[VMEM] * 5,
         scratch_shapes=strips
         + [
+            strips[2],
             pltpu.VMEM((PLANES + 1, SIZE, LANES), F32),
             pltpu.VMEM((PLANES + 1, SIZE, LANES), BF16),
             pltpu.VMEM((15, PLANES + 1, 16, LANES), BF16),
             pltpu.VMEM((4, PLANES + 1, 16, LANES), BF16),
-            dma((16,)), dma((16,)), dma((17,)), dma((17,)), dma((19,)), dma((19,)), dma((16,)), dma((16,)),
+            dma((16,)), dma((16,)), dma((20,)), dma((20,)), dma((19,)), dma((19,)), dma((16,)), dma((16,)),
         ],
         compiler_params=pltpu.CompilerParams(collective_id=1, has_side_effects=True, vmem_limit_bytes=9 * MIB),
         name="exchange_sums",
-    )(canvas, sums, probe)
+    )(canvas, sums, probe, held)
     new_object, new_probe = pl.pallas_call(
         write_results,
         out_shape=[
             jax.ShapeDtypeStruct(object_field.shape, F32),
             jax.ShapeDtypeStruct(probe_modes.shape, F32),
         ],
-        in_specs=[VMEM] * 8,
-        out_specs=[ANY, VMEM],
-        scratch_shapes=[pltpu.VMEM((2, PANELS, TILE, LANES), F32), dma((PANELS,))],
+        in_specs=[VMEM] * 6,
+        out_specs=[HBM, HBM],
+        scratch_shapes=[
+            pltpu.VMEM((2, 2, PANELS, HALF, LANES), F32),
+            pltpu.VMEM((2, 2, TILE - 2 * HALF, LANES), F32),
+            pltpu.VMEM(probe_modes.shape, F32),
+            dma((3 * PANELS + 1,)),
+        ],
         compiler_params=pltpu.CompilerParams(vmem_limit_bytes=8 * MIB),
         name="write_results",
-    )(*inner(canvas, held, got_v, got_h, got_c, update, peak), probe)
+    )(*inner(ahead, got_v, got_h, update, peak), probe)
     return new_object, new_probe
 
 

time: 69.9 us -> 63 us (0.901)
  Pallas kernels: 69.1 us -> 62.2 us
    pallas_call x1, Pallas kernels: 44.6 us -> 35.7 us  [on_device(): pl.pallas_call(exchange_sums, out_shape=strips[:2] + [pltpu.VMEM((BLOCKS,...]
    pallas_call x1, Pallas kernels: 1.22 us -> 4.33 us  [on_device(): pl.pallas_call(process_slots, out_shape=[summed, extended], in_specs=[SME...]
    pallas_call x1, Pallas kernels: 3.4 us -> 2.68 us  [on_device(): pl.pallas_call(write_results, out_shape=[jax.ShapeDtypeStruct(object_fiel...]
where the time goes in v8:
time: 63 us; the launch traced here: 62.9 us
  Pallas kernels  62.2 us (99%)
  between operations  0.7 us (1%)
    pallas_call x1, Pallas kernels, on_device(): pl.pallas_call(exchange_sums, out_shape=strips[:2] + [pltpu.VMEM((BLOCKS,...  35.7 us
    pallas_call x1, Pallas kernels, on_device(): pl.pallas_call(exchange_object, out_shape=[extended, pltpu.VMEM((2, PANEL...  19.5 us
    pallas_call x1, Pallas kernels, on_device(): pl.pallas_call(process_slots, out_shape=[summed, extended], in_specs=[SME...  4.33 us
    pallas_call x1, Pallas kernels, on_device(): pl.pallas_call(write_results, out_shape=[jax.ShapeDtypeStruct(object_fiel...  2.68 us

profile of v8, /device:TPU:1, one launch (start us, length us, event | category | flops | bytes accessed | tf_op | source)
XLA Modules:
  0.0 62.9 jit_solution(3484587730227526002)
XLA Ops:
  0.6 0.0 copy-start.1
  0.6 0.0 copy-start.2
  0.7 19.5 %exchange_object.1 = (f32[2,8,1024,128]{3,2,1,0:T(8,128)S(1)}, f32[2,6,768,128]{3,2,1,0:T(8,128)S(1)}, bf16[12,256,256]{2,1,0:T(8,128)(2,1)S(1)}, bf16[2,512,512...) custom-call(s32[8,16]{1,0:T(8,128)} %counts.1, ...), custom_call_target="tpu_custom_call" | custom-call | tf_op jit(solution)/shard_map/exchange_object/pallas_call | solution.py:535
  20.2 0.0 copy-done.1
  20.2 0.0 copy-done.2
  20.2 0.0 copy-start
  20.2 4.3 %process_slots.1 = (f32[5,2,256,128]{3,2,1,0:T(8,128)S(1)}, f32[2,8,1024,128]{3,2,1,0:T(8,128)S(1)}) custom-call(s32[8,16]{1,0:T(8,128)S(1)} %copy-done.1, s32[2,12]{1,0:T(2,128)S(1)} %bitcast.3, f32[2,8,1024,128]{3,2,1,0:T(8,128)S(1)} %get-tuple-element.17.wide, ...), custom_call_target="tpu_custom_call", output_to_operand_aliasing={{1}: (7, {}), {0}: (8, {})} | custom-call | tf_op jit(solution)/shard_map/process_slots/pallas_call | solution.py:568
  24.5 0.0 copy-done
  24.5 35.7 %exchange_sums.1 = (bf16[2,2,6,128,128]{4,3,2,1,0:T(8,128)(2,1)S(1)}, bf16[2,2,768,128]{3,2,1,0:T(8,128)(2,1)S(1)}, bf16[32,4,16,128]{3,2,1,0:T(8,128)(2,1)S(1)}...) custom-call(f32[2,8,1024,128]{3,2,1,0:T(8,128)S(1)} %get-tuple-element.24.canvas, ...), custom_call_target="tpu_custom_call" | custom-call | tf_op jit(solution)/shard_map/exchange_sums/pallas_call | solution.py:579
  60.3 2.7 %write_results.1 = (f32[2,768,768]{2,1,0:T(8,128)}, f32[2,2,256,256]{3,2,1,0:T(8,128)}) custom-call(f32[2,6,768,128]{3,2,1,0:T(8,128)S(1)} %get-tuple-element.27.ahead, bf16[2,2,6,128,128]{4,3,2,1,0:T(8,128)(2,1)S(1)} %get-tuple-element.28.got_v, bf16[2,2,768,128]{3,2,1,0:T(8,128)(2,1)S(1)} %get-tuple-element.29.got_h, ...), custom_call_target="tpu_custom_call" | custom-call | tf_op jit(solution)/shard_map/write_results/pallas_call | solution.py:601
Async XLA Ops:
  0.6 19.5 %copy-start.1 = (s32[8,16]{1,0:T(8,128)S(1)}, s32[8,16]{1,0:T(8,128)}, u32[]{:S(2)}) copy-start(s32[8,16]{1,0:T(8,128)} %counts.1) | copy-start | bytes 1540
  0.6 19.5 %copy-start.2 = (s32[1,1,2,12]{3,2,1,0:T(2,128)S(1)}, s32[1,1,2,12]{3,2,1,0:T(2,128)}, u32[]{:S(2)}) copy-start(s32[1,1,2,12]{3,2,1,0:T(2,128)} %param.9) | copy-start | bytes 292
  20.2 4.3 %copy-start = (f32[2,2,256,256]{3,2,1,0:T(8,128)S(1)}, f32[2,2,256,256]{3,2,1,0:T(8,128)}, u32[]{:S(2)}) copy-start(f32[2,2,256,256]{3,2,1,0:T(8,128)} %probe.5) | copy-start | bytes 3145732

commit v9 on v8

--- a/solution.py
+++ b/solution.py
@@ -126,6 +126,14 @@
         remote(got_h.at[c % 2, :, ends[1 - c // 2]], got_c.at[c], send.at[8 + c], recv.at[8 + c], tiles[1 - c // 2])
         for c in range(4)
     ]
+    @pl.loop(0, EXT // 32)
+    def _(i):
+        rows = pl.ds(pl.multiple_of(i * 32, 32), 32)
+        for p in range(2):
+            for k in range(PANELS + 2):
+                canvas[p, k, rows, :] = jnp.zeros((32, LANES), F32)
+
+    sums[...] = jnp.zeros_like(sums)
     for step, k in enumerate(order):
         loads[k].wait()
 
@@ -165,7 +173,6 @@
         tables[t, real, imag] = sine if t else minus
         tables[t, imag, real] = minus if t else sine
     low[...] = held_probe[...].astype(BF16).astype(F32)
-    sums[...] = jnp.zeros_like(sums)
     slots, _ = choose_slots(counts, centers)
 
     def run(i):
@@ -188,13 +195,6 @@
             wide[p, k + 1, 0:HALF, :] = keep(0, got_v[0, p, k])
             wide[p, k + 1, EXT - HALF :, :] = keep(1, got_v[1, p, k])
     run(2)
-
-    @pl.loop(0, EXT // 32)
-    def _(i):
-        rows = pl.ds(pl.multiple_of(i * 32, 32), 32)
-        for p in range(2):
-            for k in range(PANELS + 2):
-                canvas[p, k, rows, :] = jnp.zeros((32, LANES), F32)
 
     for copy in corners + sides[4:]:
         copy.wait()

time: 63 us -> 63.8 us (1.013); the launches traced: 62.9 us -> 63.1 us
    pallas_call x1, Pallas kernels: 35.7 us -> 36.5 us  [on_device(): pl.pallas_call(exchange_sums, out_shape=strips[:2] + [pltpu.VMEM((BLOCKS,...]
where the time goes in v9:
time: 63.8 us; the launch traced here: 63.1 us
  Pallas kernels  62.4 us (98%)
  between operations  0.7 us (1%)
    pallas_call x1, Pallas kernels, on_device(): pl.pallas_call(exchange_sums, out_shape=strips[:2] + [pltpu.VMEM((BLOCKS,...  36.5 us
    pallas_call x1, Pallas kernels, on_device(): pl.pallas_call(exchange_object, out_shape=[extended, pltpu.VMEM((2, PANEL...  18.9 us
    pallas_call x1, Pallas kernels, on_device(): pl.pallas_call(process_slots, out_shape=[summed, extended], in_specs=[SME...  4.3 us
    pallas_call x1, Pallas kernels, on_device(): pl.pallas_call(write_results, out_shape=[jax.ShapeDtypeStruct(object_fiel...  2.68 us

profile of v9, /device:TPU:1, one launch (start us, length us, event | category | flops | bytes accessed | tf_op | source)
XLA Modules:
  0.0 63.1 jit_solution(10470307793673035798)
XLA Ops:
  0.6 0.0 copy-start.1
  0.6 0.0 copy-start.2
  0.7 18.9 %exchange_object.1 = (f32[2,8,1024,128]{3,2,1,0:T(8,128)S(1)}, f32[2,6,768,128]{3,2,1,0:T(8,128)S(1)}, bf16[12,256,256]{2,1,0:T(8,128)(2,1)S(1)}, bf16[2,512,512...) custom-call(s32[8,16]{1,0:T(8,128)} %counts.1, ...), custom_call_target="tpu_custom_call" | custom-call | tf_op jit(solution)/shard_map/exchange_object/pallas_call | solution.py:535
  19.6 0.0 copy-done.1
  19.6 0.0 copy-done.2
  19.6 0.0 copy-start
  19.6 4.3 %process_slots.1 = (f32[5,2,256,128]{3,2,1,0:T(8,128)S(1)}, f32[2,8,1024,128]{3,2,1,0:T(8,128)S(1)}) custom-call(s32[8,16]{1,0:T(8,128)S(1)} %copy-done.1, s32[2,12]{1,0:T(2,128)S(1)} %bitcast.3, f32[2,8,1024,128]{3,2,1,0:T(8,128)S(1)} %get-tuple-element.17.wide, ...), custom_call_target="tpu_custom_call", output_to_operand_aliasing={{1}: (7, {}), {0}: (8, {})} | custom-call | tf_op jit(solution)/shard_map/process_slots/pallas_call | solution.py:568
  23.9 0.0 copy-done
  23.9 36.5 %exchange_sums.1 = (bf16[2,2,6,128,128]{4,3,2,1,0:T(8,128)(2,1)S(1)}, bf16[2,2,768,128]{3,2,1,0:T(8,128)(2,1)S(1)}, bf16[32,4,16,128]{3,2,1,0:T(8,128)(2,1)S(1)}...) custom-call(f32[2,8,1024,128]{3,2,1,0:T(8,128)S(1)} %get-tuple-element.24.canvas, ...), custom_call_target="tpu_custom_call" | custom-call | tf_op jit(solution)/shard_map/exchange_sums/pallas_call | solution.py:579
  60.4 2.7 %write_results.1 = (f32[2,768,768]{2,1,0:T(8,128)}, f32[2,2,256,256]{3,2,1,0:T(8,128)}) custom-call(f32[2,6,768,128]{3,2,1,0:T(8,128)S(1)} %get-tuple-element.27.ahead, bf16[2,2,6,128,128]{4,3,2,1,0:T(8,128)(2,1)S(1)} %get-tuple-element.28.got_v, bf16[2,2,768,128]{3,2,1,0:T(8,128)(2,1)S(1)} %get-tuple-element.29.got_h, ...), custom_call_target="tpu_custom_call" | custom-call | tf_op jit(solution)/shard_map/write_results/pallas_call | solution.py:601
Async XLA Ops:
  0.6 18.9 %copy-start.1 = (s32[8,16]{1,0:T(8,128)S(1)}, s32[8,16]{1,0:T(8,128)}, u32[]{:S(2)}) copy-start(s32[8,16]{1,0:T(8,128)} %counts.1) | copy-start | bytes 1540
  0.6 18.9 %copy-start.2 = (s32[1,1,2,12]{3,2,1,0:T(2,128)S(1)}, s32[1,1,2,12]{3,2,1,0:T(2,128)}, u32[]{:S(2)}) copy-start(s32[1,1,2,12]{3,2,1,0:T(2,128)} %param.9) | copy-start | bytes 292
  19.6 4.3 %copy-start = (f32[2,2,256,256]{3,2,1,0:T(8,128)S(1)}, f32[2,2,256,256]{3,2,1,0:T(8,128)}, u32[]{:S(2)}) copy-start(f32[2,2,256,256]{3,2,1,0:T(8,128)} %probe.5) | copy-start | bytes 3145732

commit v10 on v9

--- a/solution.py
+++ b/solution.py
@@ -97,8 +97,6 @@
         pltpu.make_async_copy(obj.at[:, :, k * LANES : (k + 1) * LANES], held.at[:, k], load.at[k])
         for k in range(PANELS)
     ]
-    for k in order:
-        loads[k].start()
     fetches = [
         pltpu.make_async_copy(waves, held_waves, load.at[PANELS]),
         pltpu.make_async_copy(probe, held_probe, load.at[PANELS + 1]),
@@ -106,8 +104,8 @@
         pltpu.make_async_copy(all_counts, counts, load.at[PANELS + 3]),
         pltpu.make_async_copy(all_centers, centers, load.at[PANELS + 4]),
     ]
-    for fetch in fetches:
-        fetch.start()
+    for copy in [loads[k] for k in order[:2]] + fetches[:2] + [loads[k] for k in order[2:]] + fetches[2:]:
+        copy.start()
     tiles = around(row, col)
     barrier = greet(tiles[:4])
     ends = (slice(0, HALF), slice(TILE - HALF, TILE), slice(HALF, TILE - HALF))
@@ -155,6 +153,17 @@
             pl.semaphore_wait(barrier, 4)
             for copy in sides:
                 copy.start()
+            for fetch in fetches[:2]:
+                fetch.wait()
+            real, imag = slice(0, SIZE), slice(SIZE, 2 * SIZE)
+            cosine, sine = held_waves[0].astype(BF16), held_waves[1].astype(BF16)
+            minus = (-held_waves[1]).astype(BF16)
+            for t in range(2):
+                tables[t, real, real] = cosine
+                tables[t, imag, imag] = cosine
+                tables[t, real, imag] = sine if t else minus
+                tables[t, imag, real] = minus if t else sine
+            low[...] = held_probe[...].astype(BF16).astype(F32)
     for copy in upright:
         copy.start()
     have = inside(row, col)
@@ -162,17 +171,8 @@
     def keep(i, value):
         return jnp.where(have[i], value.astype(F32), 0.0)
 
-    for fetch in fetches:
+    for fetch in fetches[2:]:
         fetch.wait()
-    real, imag = slice(0, SIZE), slice(SIZE, 2 * SIZE)
-    cosine, sine = held_waves[0].astype(BF16), held_waves[1].astype(BF16)
-    minus = (-held_waves[1]).astype(BF16)
-    for t in range(2):
-        tables[t, real, real] = cosine
-        tables[t, imag, imag] = cosine
-        tables[t, real, imag] = sine if t else minus
-        tables[t, imag, real] = minus if t else sine
-    low[...] = held_probe[...].astype(BF16).astype(F32)
     slots, _ = choose_slots(counts, centers)
 
     def run(i):

time: 63.8 us -> 64 us (level); the launches traced: 63.1 us -> 63.9 us
  Pallas kernels: 62.4 us -> 63.2 us
    pallas_call x1, Pallas kernels: 36.5 us -> 37.2 us  [on_device(): pl.pallas_call(exchange_sums, out_shape=strips[:2] + [pltpu.VMEM((BLOCKS,...]
where the time goes in v10:
time: 64 us; the launch traced here: 63.9 us
  Pallas kernels  63.2 us (99%)
  between operations  0.7 us (1%)
    pallas_call x1, Pallas kernels, on_device(): pl.pallas_call(exchange_sums, out_shape=strips[:2] + [pltpu.VMEM((BLOCKS,...  37.2 us
    pallas_call x1, Pallas kernels, on_device(): pl.pallas_call(exchange_object, out_shape=[extended, pltpu.VMEM((2, PANEL...  19 us
    pallas_call x1, Pallas kernels, on_device(): pl.pallas_call(process_slots, out_shape=[summed, extended], in_specs=[SME...  4.34 us
    pallas_call x1, Pallas kernels, on_device(): pl.pallas_call(write_results, out_shape=[jax.ShapeDtypeStruct(object_fiel...  2.68 us

profile of v10, /device:TPU:1, one launch (start us, length us, event | category | flops | bytes accessed | tf_op | source)
XLA Modules:
  0.0 63.9 jit_solution(10154928239488755852)
XLA Ops:
  0.6 0.0 copy-start.1
  0.6 0.0 copy-start.2
  0.7 19.0 %exchange_object.1 = (f32[2,8,1024,128]{3,2,1,0:T(8,128)S(1)}, f32[2,6,768,128]{3,2,1,0:T(8,128)S(1)}, bf16[12,256,256]{2,1,0:T(8,128)(2,1)S(1)}, bf16[2,512,512...) custom-call(s32[8,16]{1,0:T(8,128)} %counts.1, ...), custom_call_target="tpu_custom_call" | custom-call | tf_op jit(solution)/shard_map/exchange_object/pallas_call | solution.py:535
  19.7 0.0 copy-done.1
  19.7 0.0 copy-done.2
  19.7 0.0 copy-start
  19.7 4.3 %process_slots.1 = (f32[5,2,256,128]{3,2,1,0:T(8,128)S(1)}, f32[2,8,1024,128]{3,2,1,0:T(8,128)S(1)}) custom-call(s32[8,16]{1,0:T(8,128)S(1)} %copy-done.1, s32[2,12]{1,0:T(2,128)S(1)} %bitcast.3, f32[2,8,1024,128]{3,2,1,0:T(8,128)S(1)} %get-tuple-element.17.wide, ...), custom_call_target="tpu_custom_call", output_to_operand_aliasing={{1}: (7, {}), {0}: (8, {})} | custom-call | tf_op jit(solution)/shard_map/process_slots/pallas_call | solution.py:568
  24.0 0.0 copy-done
  24.0 37.2 %exchange_sums.1 = (bf16[2,2,6,128,128]{4,3,2,1,0:T(8,128)(2,1)S(1)}, bf16[2,2,768,128]{3,2,1,0:T(8,128)(2,1)S(1)}, bf16[32,4,16,128]{3,2,1,0:T(8,128)(2,1)S(1)}...) custom-call(f32[2,8,1024,128]{3,2,1,0:T(8,128)S(1)} %get-tuple-element.24.canvas, ...), custom_call_target="tpu_custom_call" | custom-call | tf_op jit(solution)/shard_map/exchange_sums/pallas_call | solution.py:579
  61.3 2.7 %write_results.1 = (f32[2,768,768]{2,1,0:T(8,128)}, f32[2,2,256,256]{3,2,1,0:T(8,128)}) custom-call(f32[2,6,768,128]{3,2,1,0:T(8,128)S(1)} %get-tuple-element.27.ahead, bf16[2,2,6,128,128]{4,3,2,1,0:T(8,128)(2,1)S(1)} %get-tuple-element.28.got_v, bf16[2,2,768,128]{3,2,1,0:T(8,128)(2,1)S(1)} %get-tuple-element.29.got_h, ...), custom_call_target="tpu_custom_call" | custom-call | tf_op jit(solution)/shard_map/write_results/pallas_call | solution.py:601
Async XLA Ops:
  0.6 19.0 %copy-start.1 = (s32[8,16]{1,0:T(8,128)S(1)}, s32[8,16]{1,0:T(8,128)}, u32[]{:S(2)}) copy-start(s32[8,16]{1,0:T(8,128)} %counts.1) | copy-start | bytes 1540
  0.6 19.0 %copy-start.2 = (s32[1,1,2,12]{3,2,1,0:T(2,128)S(1)}, s32[1,1,2,12]{3,2,1,0:T(2,128)}, u32[]{:S(2)}) copy-start(s32[1,1,2,12]{3,2,1,0:T(2,128)} %param.9) | copy-start | bytes 292
  19.7 4.4 %copy-start = (f32[2,2,256,256]{3,2,1,0:T(8,128)S(1)}, f32[2,2,256,256]{3,2,1,0:T(8,128)}, u32[]{:S(2)}) copy-start(f32[2,2,256,256]{3,2,1,0:T(8,128)} %probe.5) | copy-start | bytes 3145732
